TPU v7x, 512 devices: a whole 4x8x8 slice. The times are simulated.
512 devices in a mesh: dp: 4 (over x), context: 16 (over z, core), tensor: 8 (over y).
Axes of the slice: x: 4, y: 8, z: 8, core: 2. Of those that a mesh axis runs over, the one named last changes fastest.
Arguments:
- xs: bfloat16 [8192, 8192], P(('dp', 'context'), 'tensor'), parts along dimension 0, may hold values from -6 to 6
- bcs: bfloat16 [8192, 2, 2048], P(('dp', 'context'), None, 'tensor'), parts along dimension 0, may hold values from -6 to 6
- zs: bfloat16 [8192, 8192], P(('dp', 'context'), 'tensor'), parts along dimension 0, may hold values from -6 to 6
- dt_raw: bfloat16 [8192, 128], P(('dp', 'context'), 'tensor'), parts along dimension 0, may hold values from -3 to 3
- tail_x: bfloat16 [12, 8192], P('dp', 'tensor'), parts along dimension 0, may hold values from -6 to 6
- tail_bc: bfloat16 [12, 2, 2048], P('dp', None, 'tensor'), parts along dimension 0, may hold values from -6 to 6
- conv_x: bfloat16 [4, 8192], P(None, 'tensor'), may hold values from -3 to 3
- conv_bc: bfloat16 [4, 2, 2048], P(None, None, 'tensor'), may hold values from -3 to 3
- dt_bias: float32 [128], P('tensor'), may hold values from -3 to -1
- a_log: float32 [128], P('tensor'), may hold values from -10 to -0.6
- d_skip: float32 [128], P('tensor'), may hold values from 0.5 to 2
- init_state: float32 [512, 64, 256], P(('dp', 'tensor')), parts along dimension 0, may hold values from -6 to 6
- norm_gain: float32 [8192], P('tensor'), may hold values from 0.5 to 1.5
- out_weight: bfloat16 [8192, 8192], P('tensor', 'context'), may hold values from -0.0625 to 0.0625
Outputs:
- mixed: bfloat16 [8192, 8192], P(('dp', 'context', 'tensor')), parts along dimension 0
There are 4 independent parts, one for each index of `dp`. A program takes and returns all parts, laid end to end along the dimension named above; an argument that names none is the same for every part. Nothing has to cross between parts.
All inputs are finite; a program needn't handle non-finite values.
Results may differ from a plain program's by a relative error of at most 0.02.
Values may be sent and summed in bfloat16 or wider, within the bound.
No kernel may reach another device: no remote copies, remote signals or barrier semaphores. Data moves between devices by JAX's collectives and lax.ppermute only.
A program may use at most 64 MiB of HBM per device.

v0:
```python
import math

import jax
import jax.numpy as jnp
from jax import lax
from jax.sharding import PartitionSpec as P

H = 128
P_SIZE = 64
N = 256
G = 8


def passed_along(value, axis, steps):
    count = lax.axis_size(axis)
    leading, last = (max(0, -steps), min(count, count - steps))
    return lax.ppermute(value, axis, [(source, source + steps) for source in range(leading, last)])


def rounded(values):
    return lax.optimization_barrier(values.astype(jnp.bfloat16))


def causal_conv(prior, rows, kernel):
    full_rows = jnp.concatenate([prior.astype(jnp.float32), rows.astype(jnp.float32)], axis=0)
    length = rows.shape[0]
    running = kernel[0].astype(jnp.float32) * full_rows[0:length]
    for offset in range(1, kernel.shape[0]):
        running = running + kernel[offset].astype(jnp.float32) * full_rows[offset : offset + length]
    return rounded(jax.nn.silu(running))


def stretch_scan(inputs, deltas, rates, b_rows, c_rows, initial):
    length = inputs.shape[0]
    per_block = math.gcd(128, length)
    n_blocks = length // per_block

    def in_blocks(values):
        return values.reshape((n_blocks, per_block) + values.shape[1:])

    lower_mask = jnp.tril(jnp.ones((per_block, per_block), dtype=bool))[:, :, None, None]
    precise = lax.Precision.HIGHEST

    def advance(state, pieces):
        x_block, d_block, b_block, c_block = pieces
        cumulative = jnp.cumsum(d_block * rates, axis=0)
        spread_log = cumulative[:, None] - cumulative[None, :]
        decays = jnp.where(lower_mask, jnp.exp(jnp.where(lower_mask, spread_log, 0.0)), 0.0)
        scores = jnp.einsum(
            "ign,jgn->ijg",
            c_block.astype(jnp.bfloat16),
            b_block.astype(jnp.bfloat16),
            preferred_element_type=jnp.float32,
        )
        weights = decays * scores[..., None] * d_block[None]
        inside = jnp.einsum("ijgh,jghc->ighc", weights, x_block, precision=precise)
        carried = (
            jnp.einsum("ign,ghcn->ighc", c_block, state, precision=precise)
            * jnp.exp(cumulative)[..., None]
        )
        trailing = jnp.exp(cumulative[-1][None] - cumulative) * d_block
        increment = jnp.einsum(
            "jghc,jgn->ghcn", trailing[..., None] * x_block, b_block, precision=precise
        )
        return (jnp.exp(cumulative[-1])[..., None, None] * state + increment, inside + carried)

    final_state, outputs = lax.scan(
        advance,
        initial,
        (in_blocks(inputs), in_blocks(deltas), in_blocks(b_rows), in_blocks(c_rows)),
    )
    return (outputs.reshape(inputs.shape), final_state)


def gated_norm(scan_out, gate, gain):
    gated = scan_out.astype(jnp.float32) * jax.nn.silu(gate.astype(jnp.float32))
    row_count, width = gated.shape
    grouped = gated.reshape(row_count, width // (H * P_SIZE // G), H * P_SIZE // G)
    factor = lax.rsqrt(jnp.mean(grouped * grouped, axis=-1, keepdims=True) + 1e-05)
    return ((grouped * factor).reshape(row_count, width) * gain[None, :]).astype(jnp.bfloat16)


def body(
    xs,
    bcs,
    zs,
    dt_raw,
    tail_x,
    tail_bc,
    conv_x,
    conv_bc,
    dt_bias,
    a_log,
    d_skip,
    init_state,
    norm_gain,
    out_weight,
):
    rim_rows = conv_x.shape[0] - 1
    prior_x, prior_bc = passed_along((xs[-rim_rows:], bcs[-rim_rows:]), "context", 1)
    position = lax.axis_index("context")
    parties = lax.axis_size("context")
    at_start = position == 0
    prior_x = jnp.where(at_start, tail_x, prior_x)
    prior_bc = jnp.where(at_start, tail_bc, prior_bc)
    x_conv = causal_conv(prior_x, xs, conv_x)
    bc_conv = causal_conv(prior_bc, bcs, conv_bc)
    local_rows, x_cols = xs.shape
    heads_x = lax.all_to_all(x_conv, "context", split_axis=1, concat_axis=0, tiled=True)
    whole_bc, whole_dt = (
        lax.all_gather(bc_conv, "context", axis=0, tiled=True),
        lax.all_gather(dt_raw, "context", axis=0, tiled=True),
    )
    columns = x_cols // parties
    per_head = max(columns // P_SIZE, 1)
    channels = columns // per_head
    first_channel = position * columns
    head_start = first_channel // P_SIZE
    channel_start = first_channel % P_SIZE
    total_rows = heads_x.shape[0]
    bc_groups = whole_bc.astype(jnp.float32).reshape(total_rows, 2, -1, N)
    dt_mine = lax.dynamic_slice_in_dim(whole_dt, head_start, per_head, 1).astype(jnp.float32)
    bias_mine = lax.dynamic_slice_in_dim(dt_bias, head_start, per_head, 0)
    deltas = jax.nn.softplus(dt_mine + bias_mine[None, :]).reshape(total_rows, 1, per_head)
    rates = (-jnp.exp(lax.dynamic_slice_in_dim(a_log, head_start, per_head, 0))).reshape(
        1, per_head
    )
    skips = lax.dynamic_slice_in_dim(d_skip, head_start, per_head, 0).reshape(1, per_head)
    initial = lax.dynamic_slice(
        init_state, (head_start, channel_start, 0), (per_head, channels, N)
    ).reshape(1, per_head, channels, N)
    inputs = heads_x.astype(jnp.float32).reshape(total_rows, 1, per_head, channels)
    outputs, final_state = stretch_scan(
        inputs, deltas, rates, bc_groups[:, 0], bc_groups[:, 1], initial
    )
    mixed_heads = (
        (outputs + skips[None, :, :, None] * inputs)
        .astype(jnp.bfloat16)
        .reshape(total_rows, columns)
    )
    scan_out = lax.all_to_all(mixed_heads, "context", split_axis=0, concat_axis=1, tiled=True)
    normed = gated_norm(scan_out, zs, norm_gain)
    partial_value = jnp.dot(
        lax.all_gather(normed, "context", axis=0, tiled=True),
        out_weight,
        preferred_element_type=jnp.float32,
    )
    shuffled = lax.all_to_all(
        partial_value.astype(jnp.bfloat16), "context", split_axis=0, concat_axis=1, tiled=True
    )
    result_rows = lax.psum_scatter(
        shuffled.astype(jnp.float32).astype(jnp.bfloat16), "tensor", scatter_dimension=0, tiled=True
    )
    return result_rows


def solution(mesh):
    return jax.shard_map(
        body,
        mesh=mesh,
        in_specs=(
            P(("dp", "context"), "tensor"),
            P(("dp", "context"), None, "tensor"),
            P(("dp", "context"), "tensor"),
            P(("dp", "context"), "tensor"),
            P("dp", "tensor"),
            P("dp", None, "tensor"),
            P(None, "tensor"),
            P(None, None, "tensor"),
            P("tensor"),
            P("tensor"),
            P("tensor"),
            P(("dp", "tensor"), None, None),
            P("tensor"),
            P("tensor", "context"),
        ),
        out_specs=P(("dp", "context", "tensor"), None),
        check_vma=False,
    )
```

profile of v0, /device:TPU:4, one launch (start us, length us, event | category | flops | bytes accessed | tf_op | source)
XLA Modules:
  0.0 348.9 jit_solution(7903724849186492922)
XLA Ops:
  7.4 1.7 collective-permute-start.1
  11.6 1.1 fusion.48
  13.5 3.9 %collective-permute-start = (bf16[3,1024]{1,0:T(4,128)(2,1)S(1)}, bf16[3,1024]{1,0:T(4,128)(2,1)S(1)}, u32[]{:S(2)}, u32[]{:S(2)}) collective-permute-start(bf16[3,1024]{1,0:T(4,128)(2,1)S(1)} %slice.59), channel_id=1, source_target_pairs={{0,8},{8,16},{16,24},{24,32},{32,40},{40,48},{48,56},{56,64},{64,7... | collective-permute-start | bytes 18440 | tf_op jit(solution)/shard_map/ppermute | solution.py:17
  21.1 12.0 %all-to-all-start = ((bf16[128,16,64]{0,2,1:T(8,128)(2,1)}), bf16[128,16,64]{0,2,1:T(8,128)(2,1)S(1)}, u32[]{:S(2)}, u32[]{:S(2)}) async-start(bf16[128,16,64]{0,2,1:T(8,128)(2,1)} %bitcast.7), calls=%async_computation | async-start | bytes 524288 | tf_op jit(solution)/shard_map/all_to_all | solution.py:109
  35.6 20.5 %all_gather.9 = bf16[2048,16]{0,1:T(8,128)(2,1)S(1)} all-gather(bf16[128,16]{0,1:T(8,128)(2,1)S(1)} %copy-done.4), channel_id=1, replica_groups=mesh['dp'=4,'context'=16,'tensor'=8] {'context'}, dimensions={0}, use_global_device_ids=true | all-gather | bytes 69632 | tf_op jit(solution)/shard_map/all_gather | solution.py:112
  58.4 6.8 %all-gather.3.cloned.1.call-done = bf16[2048,2,256]{2,1,0:T(2,128)(2,1)} async-done(((bf16[128,2,256]{2,1,0:T(2,128)(2,1)}), bf16[2048,2,256]{2,1,0:T(2,128)(2,1)}) %all-gather.3.cloned.1.call-update) | async-done | bytes 2097168 | tf_op jit(solution)/shard_map/all_gather | solution.py:111
  65.2 3.2 bitcast_convert_fusion
  68.5 4.1 %fusion.52 = (f32[2048,1,1,256]{3,1,0,2:T(1,128)S(1)}, f32[2048,1,1,256]{3,1,0,2:T(1,128)}) fusion(f32[2048,2,1,256]{3,1,0,2:T(2,128)S(1)} %bitcast_convert_fusion), kind=kLoop, calls=%fused_computation.92 | loop fusion | bytes 8388608 | tf_op jit(solution)/shard_map/slice | solution.py:134
  72.6 105.2 %while.14 = (s32[]{:T(128)}, f32[1,1,64,256]{3,2,1,0:T(8,128)S(1)}, f32[16,128,1,1,64]{1,4,3,2,0:T(8,128)}, f32[16,128,1,1]{1,3,2,0:T(1,128)S(1)}, f32[1]{0:T(12...) while((s32[]{:T(128)}, f32[1,1,64,256]{3,2,1,0:T(8,128)S(1)}, ...), condition=%wide.region_2.3_spmd.clone.clone, body=%wide.region_0.2_spmd.clone.clone.sunk | while | flops 71475456 | bytes 1680533 | solution.py:67
  73.3 1.0 reduce.4
  74.9 1.1 constant_dynamic-slice_fusion.6
  79.9 1.0 reduce.4
  81.5 1.1 constant_dynamic-slice_fusion.6
  86.5 1.0 reduce.4
  88.1 1.1 constant_dynamic-slice_fusion.6
  93.1 1.0 reduce.4
  94.7 1.1 constant_dynamic-slice_fusion.6
  99.6 1.0 reduce.4
  101.2 1.1 constant_dynamic-slice_fusion.6
  106.2 1.0 reduce.4
  107.8 1.1 constant_dynamic-slice_fusion.6
  112.8 1.0 reduce.4
  114.4 1.1 constant_dynamic-slice_fusion.6
  119.4 1.0 reduce.4
  121.0 1.1 constant_dynamic-slice_fusion.6
  125.9 1.0 reduce.4
  127.5 1.1 constant_dynamic-slice_fusion.6
  132.5 1.0 reduce.4
  134.1 1.1 constant_dynamic-slice_fusion.6
  139.1 1.0 reduce.4
  140.7 1.1 constant_dynamic-slice_fusion.6
  145.7 1.0 reduce.4
  147.3 1.1 constant_dynamic-slice_fusion.6
  152.2 1.0 reduce.4
  153.8 1.1 constant_dynamic-slice_fusion.6
  158.8 1.0 reduce.4
  160.4 1.1 constant_dynamic-slice_fusion.6
  165.4 1.0 reduce.4
  167.0 1.1 constant_dynamic-slice_fusion.6
  172.0 1.0 reduce.4
  173.6 1.1 constant_dynamic-slice_fusion.6
  177.8 1.8 fusion.38
  179.6 15.6 %all_to_all.42 = bf16[16,128,64]{1,2,0:T(8,128)(2,1)S(1)} all-to-all(bf16[16,128,64]{1,2,0:T(8,128)(2,1)S(1)} %fusion.38), channel_id=1, replica_groups=mesh['dp'=4,'context'=16,'tensor'=8] {'context'}, dimensions={0} | all-to-all | bytes 524288 | tf_op jit(solution)/shard_map/all_to_all | solution.py:141
  196.7 42.9 %all-gather.5.cloned.1.call-done = bf16[2048,1024]{1,0:T(8,128)(2,1)} async-done(((bf16[128,1024]{1,0:T(8,128)(2,1)}), bf16[2048,1024]{1,0:T(8,128)(2,1)}) %all-gather.5.cloned.1.call-update) | async-done | bytes 4194320 | tf_op jit(solution)/shard_map/all_gather | solution.py:144
  239.6 4.5 %convolution_convert_fusion = bf16[2048,512]{1,0:T(8,128)(2,1)S(1)} fusion(bf16[2048,1024]{1,0:T(8,128)(2,1)} %all-gather.5.cloned.1.call-done, bf16[1024,512]{1,0:T(8,128)(2,1)S(1)} %copy-done), kind=kOutput, calls=%fused_computation.35 | convolution fusion | flops 2148532224 | bytes 7340032 | tf_op jit(solution)/shard_map/dot_general | solution.py:143
  244.1 53.8 %all_to_all.43 = bf16[16,128,512]{2,1,0:T(8,128)(2,1)S(1)} all-to-all(bf16[16,128,512]{2,1,0:T(8,128)(2,1)S(1)} %bitcast.172), channel_id=1, replica_groups=mesh['dp'=4,'context'=16,'tensor'=8] {'context'}, dimensions={0} | all-to-all | bytes 4194304 | tf_op jit(solution)/shard_map/all_to_all | solution.py:148
  297.9 1.6 copy.35
  299.5 42.9 %reduce-scatter.2.cloned.1.call-done = bf16[16,8192]{1,0:T(8,128)(2,1)} async-done(((bf16[128,8192]{1,0:T(8,128)(2,1)}), bf16[16,8192]{1,0:T(8,128)(2,1)}) %reduce-scatter.2.cloned.1.call-update) | async-done | bytes 262160 | tf_op jit(solution)/shard_map/reduce_scatter | solution.py:151
  (223 shorter events, 74.0 us)
Async XLA Ops:
  6.5 233.0 %copy-start = (bf16[1024,512]{1,0:T(8,128)(2,1)S(1)}, bf16[1024,512]{1,0:T(8,128)(2,1)}, u32[]{:S(2)}) copy-start(bf16[1024,512]{1,0:T(8,128)(2,1)} %param.29) | copy-start | bytes 3145732
  6.5 26.7 %copy-start.5 = (f32[16]{0:T(128)S(1)}, f32[16]{0:T(128)}, u32[]{:S(2)}) copy-start(f32[16]{0:T(128)} %param.24) | copy-start | bytes 196
  6.5 27.3 %copy-start.6 = (f32[16]{0:T(128)S(1)}, f32[16]{0:T(128)}, u32[]{:S(2)}) copy-start(f32[16]{0:T(128)} %param.25) | copy-start | bytes 196
  6.5 28.5 %copy-start.7 = (f32[16]{0:T(128)S(1)}, f32[16]{0:T(128)}, u32[]{:S(2)}) copy-start(f32[16]{0:T(128)} %param.26) | copy-start | bytes 196
  6.5 29.1 %copy-start.4 = (bf16[128,16]{0,1:T(8,128)(2,1)S(1)}, bf16[128,16]{0,1:T(8,128)(2,1)}, u32[]{:S(2)}) copy-start(bf16[128,16]{0,1:T(8,128)(2,1)} %param.19) | copy-start | bytes 12292
  6.5 58.7 %all-gather.3.cloned.1.call-start = ((), (), s32[]{:S(2)}) async-start(), calls=%async_computation.4 | async-start | bytes 2228224 | tf_op jit(solution)/shard_map/all_gather | solution.py:111
  7.4 3.5 collective-permute-start.1
  13.5 5.8 %collective-permute-start = (bf16[3,1024]{1,0:T(4,128)(2,1)S(1)}, bf16[3,1024]{1,0:T(4,128)(2,1)S(1)}, u32[]{:S(2)}, u32[]{:S(2)}) collective-permute-start(bf16[3,1024]{1,0:T(4,128)(2,1)S(1)} %slice.59), channel_id=1, source_target_pairs={{0,8},{8,16},{16,24},{24,32},{32,40},{40,48},{48,56},{56,64},{64,7... | collective-permute-start | bytes 18440 | tf_op jit(solution)/shard_map/ppermute | solution.py:17
  21.1 36.4 %all-to-all-start = ((bf16[128,16,64]{0,2,1:T(8,128)(2,1)}), bf16[128,16,64]{0,2,1:T(8,128)(2,1)S(1)}, u32[]{:S(2)}, u32[]{:S(2)}) async-start(bf16[128,16,64]{0,2,1:T(8,128)(2,1)} %bitcast.7), calls=%async_computation | async-start | bytes 524288 | tf_op jit(solution)/shard_map/all_to_all | solution.py:109
  33.2 206.4 %all-gather.5.cloned.1.call-start = ((), (), s32[]{:S(2)}) async-start(), calls=%async_computation.5 | async-start | bytes 4456448 | tf_op jit(solution)/shard_map/all_gather | solution.py:144
  57.5 7.7 %copy-start.1 = (bf16[128,16,64]{0,2,1:T(8,128)(2,1)}, bf16[128,16,64]{0,2,1:T(8,128)(2,1)S(1)}, u32[]{:S(2)}) copy-start(bf16[128,16,64]{0,2,1:T(8,128)(2,1)S(1)} %all-to-all-done) | copy-start | bytes 786436
  177.8 17.7 %copy-start.2 = (bf16[128,1024]{1,0:T(8,128)(2,1)S(1)}, bf16[128,1024]{1,0:T(8,128)(2,1)}, u32[]{:S(2)}) copy-start(bf16[128,1024]{1,0:T(8,128)(2,1)} %param.18) | copy-start | bytes 786436
  177.8 18.0 %copy-start.3 = (f32[1024]{0:T(1024)S(1)}, f32[1024]{0:T(1024)}, u32[]{:S(2)}) copy-start(f32[1024]{0:T(1024)} %param.28) | copy-start | bytes 12292
  196.6 145.7 %reduce-scatter.2.cloned.1.call-start = ((), (), s32[]{:S(2)}) async-start(), calls=%async_computation.6 | async-start | bytes 2359296 | tf_op jit(solution)/shard_map/reduce_scatter | solution.py:151
Sparse Core Ops, SparseCore 0:
  12.8 52.3 all-gather.2
  196.8 42.7 all-gather.4
  299.6 42.7 reduce-scatter.1
where the time goes:
time: 351 us; the launch traced here: 349 us
  waiting for transfers between devices  92.6 us (26%)
  blocking collectives  89.8 us (26%)
  local copies, waits for them, and re-layouts  52.1 us (15%)
  other arithmetic  42.1 us (12%)
  matrix products  30 us (9%)
  starting transfers between devices  17.8 us (5%)
  between operations  13.9 us (4%)
  loops' own time  10.6 us (3%)
    all_to_all x1, blocking collectives, body(): lax.all_to_all(partial_value.astype(jnp.bfloat16), 'context', split_axis=...  53.8 us
    all_gather x1, waiting for transfers between devices, body(): lax.all_gather(normed, 'context', axis=0, tiled=True)  42.9 us
    reduce_scatter x1, waiting for transfers between devices, body(): lax.psum_scatter(shuffled.astype(jnp.float32).astype(jnp.bfloat16), 'tens...  42.9 us
    dynamic_slice x48, local copies, waits for them, and re-layouts, stretch_scan(): lax.scan(advance, initial, (in_blocks(inputs), in_blocks(deltas), in_bloc...  31.2 us
    all_gather x1, blocking collectives, body(): lax.all_gather(dt_raw, 'context', axis=0, tiled=True)  20.5 us
    another operation x32, other arithmetic, advance(): cumulative = jnp.cumsum(d_block * rates, axis=0)  18.6 us
    all_to_all x1, blocking collectives, body(): lax.all_to_all(mixed_heads, 'context', split_axis=0, concat_axis=1, tiled...  15.6 us
    dot_general x16, matrix products, advance(): jnp.einsum('ign,ghcn->ighc', c_block, state, precision=precise)  14 us
  transfers between devices with their start and end apart: 6, of which 3 were waited for; matrix products, arithmetic and copies ran while one was open for 3% of the time, Pallas kernels for 0%

commit v1 on v0

v1 whole, which is shorter than its diff:
```python
import jax
import jax.numpy as jnp
from jax import lax
from jax.experimental import pallas as pl
from jax.experimental.pallas import tpu as pltpu
from jax.sharding import PartitionSpec as P

ROWS = 128
CHIP = 256
HALF = 512
HEADS = 8
P_SIZE = 64
N = 256
CHIPS = 8
PAIR = [(i, i ^ 1) for i in range(16)]
SAME_CORE = [[2 * i + k for i in range(CHIPS)] for k in range(2)]
CHIP_PAIRS = [[4 * q + i for i in range(4)] for q in range(4)]
STRIDED = [[4 * i + 2 * b + k for i in range(4)] for b in range(2) for k in range(2)]
UP = [(i, (i + 4) % 16) for i in range(16)]
DOWN = [(i, (i - 4) % 16) for i in range(16)]
TO_CORE_0 = [(2 * i + 1, 2 * i + 2) for i in range(CHIPS - 1)]
TO_CORE_1 = [(2 * i + 1, 2 * i + 3) for i in range(CHIPS - 1)]
F32 = jnp.float32
BF16 = jnp.bfloat16
EXACT = lax.Precision.HIGHEST
LIMIT = 40 * 1024 * 1024


def call(kernel, out_shape, scratch=(), flops=0, moved=0, **kwargs):
    return pl.pallas_call(
        kernel,
        out_shape=out_shape,
        scratch_shapes=list(scratch),
        compiler_params=pltpu.CompilerParams(vmem_limit_bytes=LIMIT),
        cost_estimate=pl.CostEstimate(flops=flops, bytes_accessed=moved, transcendentals=0),
        **kwargs,
    )


SMEM = pl.BlockSpec(memory_space=pltpu.SMEM)
VMEM = pl.BlockSpec(memory_space=pltpu.VMEM)


def shaped(shape, dtype):
    return jax.ShapeDtypeStruct(shape, dtype)


def silu(v):
    return v / (1.0 + jnp.exp(-v))


def half_of(ref, core):
    return ref[:, pl.ds(pl.multiple_of(core * HALF, HALF), HALF)]


def spread():
    head = lax.broadcasted_iota(jnp.int32, (128, HALF), 0)
    lane = lax.broadcasted_iota(jnp.int32, (128, HALF), 1)
    return (lane // P_SIZE == head).astype(F32)


def pack_kernel(where, xs, zs, bc, dt_other, send, halo_0, halo_1):
    core = where[0]
    send[:, 0:512] = half_of(xs, 1 - core)
    send[:, 512:1024] = half_of(zs, 1 - core)
    send[:, 1024:1536] = bc[...]
    send[:, 1536:1664] = dt_other[...]
    halo_0[:, 0:512] = xs[112:128, 0:512]
    halo_0[:, 512:1024] = bc[112:128, :]
    halo_1[:, 0:512] = xs[112:128, 512:1024]
    halo_1[:, 512:1024] = bc[112:128, :]


def conv_kernel(
    where, xs, bc, dt_own, got, halo_0, halo_1, tail, taps, heads,
    x_out, bc_out, cum_out, delta_out, send, rows, steps,
):
    core, chip = where[0], where[1]
    mine = pl.multiple_of(core * ROWS, ROWS)
    other = pl.multiple_of((1 - core) * ROWS, ROWS)
    rows[pl.ds(16 + mine, ROWS), 0:512] = half_of(xs, core).astype(F32)
    rows[pl.ds(16 + mine, ROWS), 512:1024] = bc[...].astype(F32)
    rows[pl.ds(16 + other, ROWS), 0:512] = got[:, 0:512].astype(F32)
    rows[pl.ds(16 + other, ROWS), 512:1024] = got[:, 1024:1536].astype(F32)
    halo = halo_0[...].astype(F32) + halo_1[...].astype(F32)
    rows[0:16, :] = jnp.where(chip == 0, tail[...], halo)
    for lane in range(0, 1024, 128):
        cut = slice(lane, lane + 128)
        total = taps[0:1, cut] * rows[13 : 13 + CHIP, cut]
        for k in range(1, 4):
            total = total + taps[k : k + 1, cut] * rows[13 + k : 13 + k + CHIP, cut]
        value = silu(total).astype(BF16)
        if lane < 512:
            x_out[:, cut] = value
        else:
            bc_out[:, lane - 512 : lane - 384] = value
    steps[pl.ds(mine, ROWS), :] = dt_own[...].astype(F32)
    steps[pl.ds(other, ROWS), :] = got[:, 1536:1664].astype(F32)
    raw = steps[...] + heads[0:1, 0:128]
    delta = jnp.maximum(raw, 0.0) + jnp.log(1.0 + jnp.exp(-jnp.abs(raw)))
    logs = delta * -jnp.exp(heads[1:2, 0:128])
    row = lax.broadcasted_iota(jnp.int32, (CHIP, CHIP), 0)
    column = lax.broadcasted_iota(jnp.int32, (CHIP, CHIP), 1)
    cum = jnp.dot((row >= column).astype(F32), logs, precision=EXACT, preferred_element_type=F32)
    cum_out[...] = cum
    delta_out[...] = delta
    last = cum[CHIP - 1 : CHIP, :]
    trailing = jnp.dot(jnp.exp(last - cum) * delta, spread(), precision=EXACT, preferred_element_type=F32)
    weighted = (x_out[...].astype(F32) * trailing).astype(BF16)
    added = lax.dot_general(
        weighted, bc_out[:, 0:N], (((0,), (0,)), ((), ())), preferred_element_type=F32
    )
    high = last.astype(BF16).astype(F32)
    middle = (last - high).astype(BF16).astype(F32)
    low = last - high - middle
    line = lax.broadcasted_iota(jnp.int32, (16, N), 0)
    for h in range(HEADS):
        send[h, 0:P_SIZE, :] = added[h * P_SIZE : (h + 1) * P_SIZE].astype(BF16)
        terms = jnp.where(
            line == 0,
            jnp.broadcast_to(high[:, h : h + 1], (16, N)),
            jnp.where(
                line == 1,
                jnp.broadcast_to(middle[:, h : h + 1], (16, N)),
                jnp.where(line == 2, jnp.broadcast_to(low[:, h : h + 1], (16, N)), 0.0),
            ),
        )
        send[h, P_SIZE : P_SIZE + 16, :] = terms.astype(BF16)


def inside_kernel(x, bc, cum, delta, heads, out):
    scores = lax.dot_general(
        bc[:, N : 2 * N], bc[:, 0:N], (((1,), (1,)), ((), ())), preferred_element_type=F32
    )
    row = lax.broadcasted_iota(jnp.int32, (CHIP, CHIP), 0)
    column = lax.broadcasted_iota(jnp.int32, (CHIP, CHIP), 1)
    scores = jnp.where(row >= column, scores, 0.0)
    cum_t = jnp.transpose(cum[...])
    delta_t = jnp.transpose(delta[...])
    lane = lax.broadcasted_iota(jnp.int32, (CHIP, 128), 1)
    for pair in range(HEADS // 2):
        cut = slice(pair * 128, pair * 128 + 128)
        values = x[:, cut]
        both = []
        for h in (2 * pair, 2 * pair + 1):
            decay = jnp.exp(jnp.minimum(cum[:, h : h + 1] - cum_t[h : h + 1, :], 0.0))
            weights = (decay * scores * delta_t[h : h + 1, :]).astype(BF16)
            both.append(jnp.dot(weights, values, preferred_element_type=F32))
        out[:, cut] = jnp.where(lane < P_SIZE, both[0], both[1]) + heads[2:3, cut] * values.astype(F32)


def prefix_kernel(got, first, out):
    state = first[...]
    for chip in range(CHIPS):
        out[chip] = state.astype(BF16)
        if chip < CHIPS - 1:
            terms = got[chip, P_SIZE : P_SIZE + 16, :].astype(F32)
            decay = jnp.exp(terms[0:1] + terms[1:2] + terms[2:3])
            state = decay * state + got[chip, 0:P_SIZE, :].astype(F32)


def gate_kernel(where, state, bc, cum, inside, zs, got, keep, send, total):
    core = where[0]
    mine = pl.multiple_of(core * ROWS, ROWS)
    other = pl.multiple_of((1 - core) * ROWS, ROWS)
    carried = lax.dot_general(
        bc[:, N : 2 * N], state[...], (((1,), (1,)), ((), ())), preferred_element_type=F32
    )
    decay = jnp.dot(jnp.exp(cum[...]), spread(), precision=EXACT, preferred_element_type=F32)
    total[...] = inside[...] + carried * decay
    keep[...] = total[pl.ds(mine, ROWS), :] * silu(half_of(zs, core).astype(F32))
    send[...] = (total[pl.ds(other, ROWS), :] * silu(got[:, 512:1024].astype(F32))).astype(BF16)


def norm_kernel(where, keep, got, gain, out):
    core = where[0]
    own, came = keep[...], got[...].astype(F32)
    squares = jnp.sum(own * own + came * came, axis=1, keepdims=True)
    factor = lax.rsqrt(squares * (1.0 / 1024.0) + 1e-05)
    at_own = pl.ds(pl.multiple_of(core * HALF, HALF), HALF)
    at_came = pl.ds(pl.multiple_of((1 - core) * HALF, HALF), HALF)
    out[:, at_own] = (own * factor * gain[:, at_own]).astype(BF16)
    out[:, at_came] = (came * factor * gain[:, at_came]).astype(BF16)


def product_kernel(where, own, below, above, far_low, far_high, weight, out):
    place = where[1] // 2

    def put(rows, block, first, count):
        value = jnp.dot(rows, weight[0], preferred_element_type=F32).astype(BF16)
        out[first : first + count, pl.ds(block, 1), :, :] = value.reshape(count, 1, 16, 512)

    put(own[...], place, 0, 8)
    put(below[...], (place + 3) % 4, 0, 8)
    put(above[...], (place + 1) % 4, 0, 8)
    put(far_low[...], (place + 2) % 4, 0, 4)
    put(far_high[...], (place + 2) % 4, 4, 4)


def body(
    xs, bcs, zs, dt_raw, tail_x, tail_bc, conv_x, conv_bc,
    dt_bias, a_log, d_skip, init_state, norm_gain, out_weight,
):
    position = lax.axis_index("context")
    core, chip = position % 2, position // 2
    where = jnp.stack([core, chip]).astype(jnp.int32)

    weights = lax.all_gather(
        out_weight, "context", axis=0, tiled=True, axis_index_groups=CHIP_PAIRS
    ).reshape(4, 1024, 512)

    bc = bcs.reshape(ROWS, 512)

    def steps_of(side):
        return jnp.pad(lax.dynamic_slice_in_dim(dt_raw, side * HEADS, HEADS, 1), ((0, 0), (0, 120)))

    send, halo_0, halo_1 = call(
        pack_kernel,
        (shaped((ROWS, 1664), BF16), shaped((16, 1024), BF16), shaped((16, 1024), BF16)),
        in_specs=[SMEM, VMEM, VMEM, VMEM, VMEM],
        moved=1 << 20,
    )(where, xs, zs, bc, steps_of(1 - core))
    got = lax.ppermute(send, "context", PAIR)
    halo_0 = lax.ppermute(halo_0, "context", TO_CORE_0)
    halo_1 = lax.ppermute(halo_1, "context", TO_CORE_1)

    def own_channels(value):
        return lax.dynamic_slice_in_dim(value, core * HALF, HALF, 1).astype(F32)

    def own_heads(value):
        return lax.dynamic_slice_in_dim(value, core * HEADS, HEADS, 0)

    tail = jnp.pad(
        jnp.concatenate([own_channels(tail_x), tail_bc.reshape(3, 512).astype(F32)], axis=1), ((13, 0), (0, 0))
    )
    taps = jnp.concatenate([own_channels(conv_x), conv_bc.reshape(4, 512).astype(F32)], axis=1)
    heads = jnp.stack(
        [
            jnp.pad(own_heads(dt_bias), (0, HALF - HEADS)),
            jnp.pad(own_heads(a_log), (0, HALF - HEADS)),
            jnp.repeat(own_heads(d_skip), P_SIZE),
        ]
    )
    x_conv, bc_conv, cum, delta, added = call(
        conv_kernel,
        (
            shaped((CHIP, HALF), BF16),
            shaped((CHIP, 512), BF16),
            shaped((CHIP, 128), F32),
            shaped((CHIP, 128), F32),
            shaped((HEADS, P_SIZE + 16, N), BF16),
        ),
        scratch=[pltpu.VMEM((CHIP + 16, 1024), F32), pltpu.VMEM((CHIP, 128), F32)],
        in_specs=[SMEM] + [VMEM] * 9,
        flops=200_000_000,
        moved=2 << 20,
    )(where, xs, bc, steps_of(core), got, halo_0, halo_1, tail, taps, heads)
    increments = lax.all_to_all(added, "context", 0, 0, tiled=True, axis_index_groups=SAME_CORE)
    inside = call(
        inside_kernel,
        shaped((CHIP, HALF), F32),
        in_specs=[VMEM] * 5,
        flops=400_000_000,
        moved=2 << 20,
    )(x_conv, bc_conv, cum, delta, heads)
    first = lax.dynamic_index_in_dim(init_state, core * HEADS + chip, 0, keepdims=False)
    states = call(
        prefix_kernel,
        shaped((CHIPS, P_SIZE, N), BF16),
        in_specs=[VMEM] * 2,
        moved=1 << 20,
    )(increments, first)
    states = lax.all_to_all(states, "context", 0, 0, tiled=True, axis_index_groups=SAME_CORE)
    keep, give = call(
        gate_kernel,
        (shaped((ROWS, HALF), F32), shaped((ROWS, HALF), BF16)),
        scratch=[pltpu.VMEM((CHIP, HALF), F32)],
        in_specs=[SMEM] + [VMEM] * 6,
        flops=100_000_000,
        moved=2 << 20,
    )(where, states.reshape(HEADS * P_SIZE, N), bc_conv, cum, inside, zs, got)
    came = lax.ppermute(give, "context", PAIR)
    normed = call(
        norm_kernel,
        shaped((ROWS, 1024), BF16),
        in_specs=[SMEM] + [VMEM] * 3,
        moved=1 << 20,
    )(where, keep, came, norm_gain.reshape(1, 1024))

    below = lax.ppermute(normed, "context", UP)
    above = lax.ppermute(normed, "context", DOWN)
    far_low = lax.ppermute(below[:64], "context", UP)
    far_high = lax.ppermute(above[64:], "context", DOWN)
    whole = lambda rows: pl.BlockSpec((rows, 1024), lambda j: (0, 0))
    partial_sums = call(
        product_kernel,
        shaped((8, 4, 16, 2048), BF16),
        grid=(4,),
        in_specs=[
            SMEM, whole(128), whole(128), whole(128), whole(64), whole(64),
            pl.BlockSpec((1, 1024, 512), lambda j: (j, 0, 0)),
        ],
        out_specs=pl.BlockSpec((8, 4, 16, 512), lambda j: (0, 0, 0, j)),
        flops=2_200_000_000,
        moved=7 << 20,
    )(where, normed, below, above, far_low, far_high, weights)
    summed = lax.psum_scatter(
        partial_sums.reshape(512, 2048), "tensor", scatter_dimension=0, tiled=True
    )
    return lax.all_to_all(
        summed.reshape(4, 16, 2048), "context", 0, 0, tiled=True, axis_index_groups=STRIDED
    ).transpose(1, 0, 2).reshape(16, 8192)


def solution(mesh):
    return jax.shard_map(
        body,
        mesh=mesh,
        in_specs=(
            P(("dp", "context"), "tensor"),
            P(("dp", "context"), None, "tensor"),
            P(("dp", "context"), "tensor"),
            P(("dp", "context"), "tensor"),
            P("dp", "tensor"),
            P("dp", None, "tensor"),
            P(None, "tensor"),
            P(None, None, "tensor"),
            P("tensor"),
            P("tensor"),
            P("tensor"),
            P(("dp", "tensor"), None, None),
            P("tensor"),
            P("tensor", "context"),
        ),
        out_specs=P(("dp", "context", "tensor"), None),
        check_vma=False,
    )
```

time: 351 us -> 190 us (0.54)
  the two profiles are of different devices: /device:TPU:4 before, /device:TPU:24 now
where the time goes in v1:
time: 190 us; the launch traced here: 189 us
  waiting for transfers between devices  94.2 us (50%)
  starting transfers between devices  37.7 us (20%)
  blocking collectives  17.4 us (9%)
  between operations  13.7 us (7%)
  Pallas kernels  13.1 us (7%)
  local copies, waits for them, and re-layouts  12.8 us (7%)
    reduce_scatter x1, waiting for transfers between devices, body(): lax.psum_scatter(partial_sums.reshape(512, 2048), 'tensor', scatter_dimen...  44 us
    all_to_all x1, blocking collectives, body(): lax.all_to_all(summed.reshape(4, 16, 2048), 'context', 0, 0, tiled=True,...  17.4 us
    all_to_all x1, waiting for transfers between devices, body(): lax.all_to_all(added, 'context', 0, 0, tiled=True, axis_index_groups=SAME...  17.2 us
    all_to_all x1, waiting for transfers between devices, body(): lax.all_to_all(states, 'context', 0, 0, tiled=True, axis_index_groups=SAM...  14.1 us
    ppermute x1, waiting for transfers between devices, body(): above = lax.ppermute(normed, 'context', DOWN)  10 us
    ppermute x1, starting transfers between devices, body(): got = lax.ppermute(send, 'context', PAIR)  8.97 us
    all_to_all x1, starting transfers between devices, body(): lax.all_to_all(added, 'context', 0, 0, tiled=True, axis_index_groups=SAME...  8.52 us
    unnamed x19, local copies, waits for them, and re-layouts  7.62 us
  transfers between devices with their start and end apart: 12, of which 7 were waited for; matrix products, arithmetic and copies ran while one was open for 4% of the time, Pallas kernels for 4%

profile of v1, /device:TPU:24, one launch (start us, length us, event | category | flops | bytes accessed | tf_op | source)
XLA Modules:
  0.0 189.0 jit_solution(1579188108565124965)
XLA Ops:
  6.5 0.7 all-gather.2.cloned.1.call-update
  7.3 0.7 constant_dynamic-slice_fusion.2
  8.0 0.1 copy.24
  8.1 0.9 copy.27
  9.1 0.1 pad_add_fusion.where
  9.2 0.9 copy-done.1
  10.1 0.9 copy-done.3
  11.1 0.6 shard_map.136
  11.6 0.7 collective-permute-start.1
  12.3 0.7 collective-permute-start.2
  13.0 9.0 %collective-permute-start = (bf16[128,1664]{1,0:T(8,128)(2,1)S(1)}, bf16[128,1664]{1,0:T(8,128)(2,1)S(1)}, u32[]{:S(2)}, u32[]{:S(2)}) collective-permute-start(bf16[128,1664]{1,0:T(8,128)(2,1)S(1)} %get-tuple-element.15), channel_id=1, source_target_pairs={{0,8},{8,0},{16,24},{24,16},{32,40},{40,32},{48,56},{56,48},{64,72... | collective-permute-start | bytes 1277960 | tf_op jit(solution)/shard_map/ppermute | solution.py:223
  22.0 0.7 dynamic_slice.29
  22.7 0.7 dynamic_slice.30
  23.4 0.7 dynamic_slice.31
  24.2 0.1 broadcast_in_dim.3
  24.2 0.1 stack_reshape.3
  24.3 0.7 copy.26
  25.0 0.7 copy.28
  25.7 0.7 constant_dynamic-slice_fusion.1
  26.4 0.7 constant_dynamic-slice_fusion
  27.1 0.1 copy.23
  27.3 0.0 copy-start.2
  27.3 1.0 copy-done.2
  28.3 3.7 %shard_map.137 = (bf16[256,512]{1,0:T(8,128)(2,1)S(1)}, bf16[256,512]{1,0:T(8,128)(2,1)S(1)}, f32[256,128]{1,0:T(8,128)S(1)}, f32[256,128]{1,0:T(8,128)S(1)}, bf16[8,80,256]{2,1,0:T(8,128)(2,1)}) custom-call(s32[2]{0:T(128)S(1)} %pad_add_fusion.where, bf16[128,1024]{1,0:T(8,128)(2,1)S(1)} %copy-done.2, bf16[128,512]{1,0:T(8,128)(2,1)S(1)} %bitcast.21, ...), custom_call_target="tpu_custom_call" | custom-call | flops 200000000 | bytes 2097152 | tf_op jit(solution)/shard_map/pallas_call | solution.py:244
  32.0 8.5 %all-to-all-start = ((bf16[8,80,256]{2,1,0:T(8,128)(2,1)}), bf16[8,80,256]{2,1,0:T(8,128)(2,1)S(1)}, u32[]{:S(2)}, u32[]{:S(2)}) async-start(bf16[8,80,256]{2,1,0:T(8,128)(2,1)} %get-tuple-element.18), calls=%async_computation | async-start | bytes 655360 | tf_op jit(solution)/shard_map/all_to_all | solution.py:258
  40.5 17.2 %all-to-all-done.got = bf16[8,80,256]{2,1,0:T(8,128)(2,1)S(1)} async-done(((bf16[8,80,256]{2,1,0:T(8,128)(2,1)}), bf16[8,80,256]{2,1,0:T(8,128)(2,1)S(1)}, u32[]{:S(2)}, u32[]{:S(2)}) %all-to-all-start) | async-done | bytes 327712 | tf_op jit(solution)/shard_map/all_to_all | solution.py:258
  57.8 0.8 shard_map.138
  58.5 3.4 %all-to-all-start.1 = ((bf16[8,64,256]{2,1,0:T(8,128)(2,1)}), bf16[8,64,256]{2,1,0:T(8,128)(2,1)S(1)}, u32[]{:S(2)}, u32[]{:S(2)}) async-start(bf16[8,64,256]{2,1,0:T(8,128)(2,1)} %shard_map.138), calls=%async_computation.1 | async-start | bytes 524288 | tf_op jit(solution)/shard_map/all_to_all | solution.py:273
  62.0 0.0 reduce-scatter.2.cloned.1.call-start
  62.0 0.8 shard_map.139.inside
  62.8 14.1 %all-to-all-done.1 = bf16[8,64,256]{2,1,0:T(8,128)(2,1)S(1)} async-done(((bf16[8,64,256]{2,1,0:T(8,128)(2,1)}), bf16[8,64,256]{2,1,0:T(8,128)(2,1)S(1)}, u32[]{:S(2)}, u32[]{:S(2)}) %all-to-all-start.1) | async-done | bytes 262176 | tf_op jit(solution)/shard_map/all_to_all | solution.py:273
  77.0 1.4 shard_map.140
  78.3 1.9 %collective-permute-start.3 = (bf16[128,512]{1,0:T(8,128)(2,1)S(1)}, bf16[128,512]{1,0:T(8,128)(2,1)S(1)}, u32[]{:S(2)}, u32[]{:S(2)}) collective-permute-start(bf16[128,512]{1,0:T(8,128)(2,1)S(1)} %get-tuple-element.24), channel_id=1, source_target_pairs={{0,8},{8,0},{16,24},{24,16},{32,40},{40,32},{48,56},{56,48},{64,72... | collective-permute-start | bytes 393224 | tf_op jit(solution)/shard_map/ppermute | solution.py:282
  80.2 1.3 collective-permute-done.3.got
  81.6 0.7 shard_map.141.own
  82.3 2.2 %collective-permute-start.5 = (bf16[128,1024]{1,0:T(8,128)(2,1)S(1)}, bf16[128,1024]{1,0:T(8,128)(2,1)S(1)}, u32[]{:S(2)}, u32[]{:S(2)}) collective-permute-start(bf16[128,1024]{1,0:T(8,128)(2,1)S(1)} %shard_map.141.own), channel_id=1, source_target_pairs={{0,96},{8,104},{16,112},{24,120},{32,0},{40,8},{48,16},{56,24},{64... | collective-permute-start | bytes 786440 | tf_op jit(solution)/shard_map/ppermute | solution.py:291
  84.4 4.6 %collective-permute-start.4 = (bf16[128,1024]{1,0:T(8,128)(2,1)S(1)}, bf16[128,1024]{1,0:T(8,128)(2,1)S(1)}, u32[]{:S(2)}, u32[]{:S(2)}) collective-permute-start(bf16[128,1024]{1,0:T(8,128)(2,1)S(1)} %shard_map.141.own), channel_id=1, source_target_pairs={{0,32},{8,40},{16,48},{24,56},{32,64},{40,72},{48,80},{56,88},{64,... | collective-permute-start | bytes 786440 | tf_op jit(solution)/shard_map/ppermute | solution.py:290
  89.0 10.0 %collective-permute-done.5.above = bf16[128,1024]{1,0:T(8,128)(2,1)S(1)} collective-permute-done((bf16[128,1024]{1,0:T(8,128)(2,1)S(1)}, bf16[128,1024]{1,0:T(8,128)(2,1)S(1)}, u32[]{:S(2)}, u32[]{:S(2)}) %collective-permute-start.5) | collective-permute-done | bytes 262176 | tf_op jit(solution)/shard_map/ppermute | solution.py:291
  99.0 3.5 %collective-permute-start.7 = (bf16[64,1024]{1,0:T(8,128)(2,1)S(1)}, bf16[64,1024]{1,0:T(8,128)(2,1)S(1)}, u32[]{:S(2)}, u32[]{:S(2)}) collective-permute-start(bf16[64,1024]{1,0:T(8,128)(2,1)S(1)} %slice.9), channel_id=1, source_target_pairs={{0,96},{8,104},{16,112},{24,120},{32,0},{40,8},{48,16},{56,24},{64... | collective-permute-start | bytes 393224 | tf_op jit(solution)/shard_map/ppermute | solution.py:293
  102.6 3.3 %collective-permute-start.6 = (bf16[64,1024]{1,0:T(8,128)(2,1)S(1)}, bf16[64,1024]{1,0:T(8,128)(2,1)S(1)}, u32[]{:S(2)}, u32[]{:S(2)}) collective-permute-start(bf16[64,1024]{1,0:T(8,128)(2,1)S(1)} %slice.8), channel_id=1, source_target_pairs={{0,32},{8,40},{16,48},{24,56},{32,64},{40,72},{48,80},{56,88},{64,... | collective-permute-start | bytes 393224 | tf_op jit(solution)/shard_map/ppermute | solution.py:292
  105.8 1.3 collective-permute-done.7.far_high
  107.1 5.6 %collective-permute-done.6.far_low = bf16[64,1024]{1,0:T(8,128)(2,1)S(1)} collective-permute-done((bf16[64,1024]{1,0:T(8,128)(2,1)S(1)}, bf16[64,1024]{1,0:T(8,128)(2,1)S(1)}, u32[]{:S(2)}, u32[]{:S(2)}) %collective-permute-start.6) | collective-permute-done | bytes 131104 | tf_op jit(solution)/shard_map/ppermute | solution.py:292
  112.7 2.2 %copy-done.6 = bf16[4096,512]{1,0:T(8,128)(2,1)S(1)} copy-done((bf16[4096,512]{1,0:T(8,128)(2,1)S(1)}, bf16[4096,512]{1,0:T(8,128)(2,1)}, u32[]{:S(2)}) %copy-start.6) | copy-done | bytes 4194328
  114.9 5.2 %shard_map.142 = bf16[8,4,16,2048]{3,2,1,0:T(8,128)(2,1)} custom-call(s32[2]{0:T(128)S(1)} %pad_add_fusion.where, bf16[128,1024]{1,0:T(8,128)(2,1)S(1)} %shard_map.141.own, bf16[128,1024]{1,0:T(8,128)(2,1)S(1)} %collective-permute-done.4.below, bf16[128,1024]{1,0:T(8,128)(2,1)S(1)} %collective-permute-done.5.above, ...), custom_call_target="tpu_custom_call" | custom-call | flops 2200000000 | bytes 7340032 | tf_op jit(solution)/shard_map/pallas_call | solution.py:295
  120.1 0.0 reduce-scatter.2.cloned.1.call-update
  120.1 44.0 %reduce-scatter.2.cloned.1.call-done = bf16[64,2048]{1,0:T(8,128)(2,1)} async-done(((bf16[512,2048]{1,0:T(8,128)(2,1)}), bf16[64,2048]{1,0:T(8,128)(2,1)}) %reduce-scatter.2.cloned.1.call-update) | async-done | bytes 262160 | tf_op jit(solution)/shard_map/reduce_scatter | solution.py:307
  164.1 17.4 %all_to_all.15 = bf16[4,16,2048]{2,1,0:T(8,128)(2,1)S(1)} all-to-all(bf16[4,16,2048]{2,1,0:T(8,128)(2,1)} %bitcast.26), channel_id=1, replica_groups={{0,32,64,96},{8,40,72,104},{16,48,80,112},{24,56,88,120},{1,33,65,97},{..., dimensions={0} | all-to-all | bytes 524288 | tf_op jit(solution)/shard_map/all_to_all | solution.py:310
  181.4 0.7 copy.25
  (25 shorter events, 0.1 us)
Async XLA Ops:
  6.5 34.0 %copy-start = (f32[16,64,256]{2,1,0:T(8,128)S(1)}, f32[16,64,256]{2,1,0:T(8,128)}, u32[]{:S(2)}) copy-start(f32[16,64,256]{2,1,0:T(8,128)} %param.25) | copy-start | bytes 3145732
  6.5 70.4 %copy-start.4 = (bf16[128,1024]{1,0:T(8,128)(2,1)S(1)}, bf16[128,1024]{1,0:T(8,128)(2,1)}, u32[]{:S(2)}) copy-start(bf16[128,1024]{1,0:T(8,128)(2,1)} %zs.3) | copy-start | bytes 786436
  6.5 75.0 %copy-start.5 = (f32[1024]{0:T(1024)S(1)}, f32[1024]{0:T(1024)}, u32[]{:S(2)}) copy-start(f32[1024]{0:T(1024)} %param.26) | copy-start | bytes 12292
  6.5 106.1 %all-gather.2.cloned.1.call-start = ((), (), s32[]{:S(2)}) async-start(), calls=%async_computation.4 | async-start | bytes 5242880 | tf_op jit(solution)/shard_map/all_gather | solution.py:208
  9.2 1.0 copy-start.1
  10.1 0.9 copy-start.3
  11.6 15.6 %collective-permute-start.1 = (bf16[16,1024]{1,0:T(8,128)(2,1)S(1)}, bf16[16,1024]{1,0:T(8,128)(2,1)S(1)}, u32[]{:S(2)}, u32[]{:S(2)}) collective-permute-start(bf16[16,1024]{1,0:T(8,128)(2,1)S(1)} %get-tuple-element.16), channel_id=1, source_target_pairs={{8,16},{24,32},{40,48},{56,64},{72,80},{88,96},{104,112},{9,17},{2... | collective-permute-start | bytes 98312 | tf_op jit(solution)/shard_map/ppermute | solution.py:224
  12.3 15.0 %collective-permute-start.2 = (bf16[16,1024]{1,0:T(8,128)(2,1)S(1)}, bf16[16,1024]{1,0:T(8,128)(2,1)S(1)}, u32[]{:S(2)}, u32[]{:S(2)}) collective-permute-start(bf16[16,1024]{1,0:T(8,128)(2,1)S(1)} %get-tuple-element.17), channel_id=1, source_target_pairs={{8,24},{24,40},{40,56},{56,72},{72,88},{88,104},{104,120},{9,25},{... | collective-permute-start | bytes 98312 | tf_op jit(solution)/shard_map/ppermute | solution.py:225
  13.0 14.3 %collective-permute-start = (bf16[128,1664]{1,0:T(8,128)(2,1)S(1)}, bf16[128,1664]{1,0:T(8,128)(2,1)S(1)}, u32[]{:S(2)}, u32[]{:S(2)}) collective-permute-start(bf16[128,1664]{1,0:T(8,128)(2,1)S(1)} %get-tuple-element.15), channel_id=1, source_target_pairs={{0,8},{8,0},{16,24},{24,16},{32,40},{40,32},{48,56},{56,48},{64,72... | collective-permute-start | bytes 1277960 | tf_op jit(solution)/shard_map/ppermute | solution.py:223
  27.3 1.0 copy-start.2
  32.0 25.8 %all-to-all-start = ((bf16[8,80,256]{2,1,0:T(8,128)(2,1)}), bf16[8,80,256]{2,1,0:T(8,128)(2,1)S(1)}, u32[]{:S(2)}, u32[]{:S(2)}) async-start(bf16[8,80,256]{2,1,0:T(8,128)(2,1)} %get-tuple-element.18), calls=%async_computation | async-start | bytes 655360 | tf_op jit(solution)/shard_map/all_to_all | solution.py:258
  58.5 18.4 %all-to-all-start.1 = ((bf16[8,64,256]{2,1,0:T(8,128)(2,1)}), bf16[8,64,256]{2,1,0:T(8,128)(2,1)S(1)}, u32[]{:S(2)}, u32[]{:S(2)}) async-start(bf16[8,64,256]{2,1,0:T(8,128)(2,1)} %shard_map.138), calls=%async_computation.1 | async-start | bytes 524288 | tf_op jit(solution)/shard_map/all_to_all | solution.py:273
  62.0 102.1 %reduce-scatter.2.cloned.1.call-start = ((), (), s32[]{:S(2)}) async-start(), calls=%async_computation.5 | async-start | bytes 2359296 | tf_op jit(solution)/shard_map/reduce_scatter | solution.py:307
  78.3 3.2 %collective-permute-start.3 = (bf16[128,512]{1,0:T(8,128)(2,1)S(1)}, bf16[128,512]{1,0:T(8,128)(2,1)S(1)}, u32[]{:S(2)}, u32[]{:S(2)}) collective-permute-start(bf16[128,512]{1,0:T(8,128)(2,1)S(1)} %get-tuple-element.24), channel_id=1, source_target_pairs={{0,8},{8,0},{16,24},{24,16},{32,40},{40,32},{48,56},{56,48},{64,72... | collective-permute-start | bytes 393224 | tf_op jit(solution)/shard_map/ppermute | solution.py:282
  82.3 16.8 %collective-permute-start.5 = (bf16[128,1024]{1,0:T(8,128)(2,1)S(1)}, bf16[128,1024]{1,0:T(8,128)(2,1)S(1)}, u32[]{:S(2)}, u32[]{:S(2)}) collective-permute-start(bf16[128,1024]{1,0:T(8,128)(2,1)S(1)} %shard_map.141.own), channel_id=1, source_target_pairs={{0,96},{8,104},{16,112},{24,120},{32,0},{40,8},{48,16},{56,24},{64... | collective-permute-start | bytes 786440 | tf_op jit(solution)/shard_map/ppermute | solution.py:291
  84.4 18.1 %collective-permute-start.4 = (bf16[128,1024]{1,0:T(8,128)(2,1)S(1)}, bf16[128,1024]{1,0:T(8,128)(2,1)S(1)}, u32[]{:S(2)}, u32[]{:S(2)}) collective-permute-start(bf16[128,1024]{1,0:T(8,128)(2,1)S(1)} %shard_map.141.own), channel_id=1, source_target_pairs={{0,32},{8,40},{16,48},{24,56},{32,64},{40,72},{48,80},{56,88},{64,... | collective-permute-start | bytes 786440 | tf_op jit(solution)/shard_map/ppermute | solution.py:290
  99.0 8.1 %collective-permute-start.7 = (bf16[64,1024]{1,0:T(8,128)(2,1)S(1)}, bf16[64,1024]{1,0:T(8,128)(2,1)S(1)}, u32[]{:S(2)}, u32[]{:S(2)}) collective-permute-start(bf16[64,1024]{1,0:T(8,128)(2,1)S(1)} %slice.9), channel_id=1, source_target_pairs={{0,96},{8,104},{16,112},{24,120},{32,0},{40,8},{48,16},{56,24},{64... | collective-permute-start | bytes 393224 | tf_op jit(solution)/shard_map/ppermute | solution.py:293
  102.6 10.1 %collective-permute-start.6 = (bf16[64,1024]{1,0:T(8,128)(2,1)S(1)}, bf16[64,1024]{1,0:T(8,128)(2,1)S(1)}, u32[]{:S(2)}, u32[]{:S(2)}) collective-permute-start(bf16[64,1024]{1,0:T(8,128)(2,1)S(1)} %slice.8), channel_id=1, source_target_pairs={{0,32},{8,40},{16,48},{24,56},{32,64},{40,72},{48,80},{56,88},{64,... | collective-permute-start | bytes 393224 | tf_op jit(solution)/shard_map/ppermute | solution.py:292
  112.7 2.2 %copy-start.6 = (bf16[4096,512]{1,0:T(8,128)(2,1)S(1)}, bf16[4096,512]{1,0:T(8,128)(2,1)}, u32[]{:S(2)}) copy-start(bf16[4096,512]{1,0:T(8,128)(2,1)} %all-gather.2.cloned.1.call-done) | copy-start | bytes 12582916
Sparse Core Ops, SparseCore 0:
  9.5 68.5 all-gather.1
  120.2 43.8 reduce-scatter.1

commit v2 on v1

v2 whole, which is shorter than its diff:
```python
import functools

import jax
import jax.numpy as jnp
from jax import lax
from jax.experimental import pallas as pl
from jax.experimental.pallas import tpu as pltpu
from jax.sharding import PartitionSpec as P

ROWS = 128
CHIP = 256
HALF = 512
HEADS = 8
P_SIZE = 64
N = 256
CHIPS = 8
PAIR = [(i, i ^ 1) for i in range(16)]
SAME_CORE = [[2 * i + k for i in range(CHIPS)] for k in range(2)]
UP = [(i, (i + 2) % 16) for i in range(16)]
DOWN = [(i, (i - 2) % 16) for i in range(16)]
CROSS = [(8 * i + t, 8 * (i ^ 1) + (t ^ 1)) for i in range(16) for t in range(8)]
BESIDE = [(t, t ^ 1) for t in range(8)]
PARITY = [[0, 2, 4, 6], [1, 3, 5, 7]]
CORES = [[2 * i, 2 * i + 1] for i in range(CHIPS)]
BOTH = [[0, 1], [2, 3], [4, 5], [6, 7]]
NEAR = (0, 1, 7, 2, 6)
FAR = (3, 5, 4)
TO_CORE_0 = [(2 * i + 1, 2 * i + 2) for i in range(CHIPS - 1)]
TO_CORE_1 = [(2 * i + 1, 2 * i + 3) for i in range(CHIPS - 1)]
F32 = jnp.float32
BF16 = jnp.bfloat16
EXACT = lax.Precision.HIGHEST
LIMIT = 24 * 1024 * 1024
WIDE = 63 * 1024 * 1024


def call(kernel, out_shape, scratch=(), flops=0, moved=0, limit=LIMIT, **kwargs):
    return pl.pallas_call(
        kernel,
        out_shape=out_shape,
        scratch_shapes=list(scratch),
        compiler_params=pltpu.CompilerParams(vmem_limit_bytes=limit),
        cost_estimate=pl.CostEstimate(flops=flops, bytes_accessed=moved, transcendentals=0),
        **kwargs,
    )


SMEM = pl.BlockSpec(memory_space=pltpu.SMEM)
VMEM = pl.BlockSpec(memory_space=pltpu.VMEM)
HBM = pl.BlockSpec(memory_space=pltpu.HBM)


def shaped(shape, dtype):
    return jax.ShapeDtypeStruct(shape, dtype)


def silu(v):
    return v / (1.0 + jnp.exp(-v))


def half_of(ref, core):
    return ref[:, pl.ds(pl.multiple_of(core * HALF, HALF), HALF)]


def spread():
    head = lax.broadcasted_iota(jnp.int32, (128, HALF), 0)
    lane = lax.broadcasted_iota(jnp.int32, (128, HALF), 1)
    return (lane // P_SIZE == head).astype(F32)


def place():
    position = lax.axis_index("context")
    return lax.rem(position, 2), lax.div(position, 2)


def copies(pairs, sems):
    return [pltpu.make_async_copy(source, target, sems.at[i]) for i, (source, target) in enumerate(pairs)]


def fetch(pairs, sems):
    moving = copies(pairs, sems)
    for copy in moving:
        copy.start()
    for copy in moving:
        copy.wait()


def lanes(core):
    return pl.ds(pl.multiple_of(core * HALF, HALF), HALF)


def tokens(core):
    return pl.ds(pl.multiple_of(core * ROWS, ROWS), ROWS)


TAPS, BIAS, RATE = 16, 20, 21


def pack_kernel(
    xs, zs, bcs, dt, tail_x, tail_bc, taps_x, taps_bc, bias, rate,
    send, halo_0, halo_1, mine, fixed, b_c, steps, tail_2, tail_3, taps_2, taps_3, bias_1, rate_1, heads, sems,
):
    core, _ = place()
    heads[...] = jnp.zeros((2, 128), F32)
    fetch(
        [
            (bcs, b_c),
            (dt, steps),
            (tail_x, tail_2),
            (tail_bc, tail_3),
            (taps_x, taps_2),
            (taps_bc, taps_3),
            (bias, bias_1),
            (rate, rate_1),
            (xs.at[:, lanes(1 - core)], send.at[:, 0:512]),
            (zs.at[:, lanes(1 - core)], send.at[:, 1152:1664]),
            (xs.at[:, lanes(core)], mine),
            (xs.at[112:128, 0:512], halo_0.at[:, 0:512]),
            (xs.at[112:128, 512:1024], halo_1.at[:, 0:512]),
        ],
        sems,
    )
    send[:, 512:768] = b_c[:, 0, :]
    send[:, 768:1024] = b_c[:, 1, :]
    by_head = jnp.concatenate([steps[...].astype(F32), jnp.zeros((112, ROWS), F32)], axis=0)
    send[:, 1024:1152] = jnp.transpose(by_head).astype(BF16)
    halo_0[:, 512:1024] = send[112:128, 512:1024]
    halo_1[:, 512:1024] = send[112:128, 512:1024]
    fixed[...] = jnp.zeros((32, 1024), F32)
    fixed[13:16, 0:512] = half_of(tail_2, core).astype(F32)
    fixed[13:16, 512:768] = tail_3[:, 0, :].astype(F32)
    fixed[13:16, 768:1024] = tail_3[:, 1, :].astype(F32)
    fixed[TAPS : TAPS + 4, 0:512] = half_of(taps_2, core).astype(F32)
    fixed[TAPS : TAPS + 4, 512:768] = taps_3[:, 0, :].astype(F32)
    fixed[TAPS : TAPS + 4, 768:1024] = taps_3[:, 1, :].astype(F32)
    heads[0:1, 0:16] = bias_1[...]
    heads[1:2, 0:16] = rate_1[...]
    own = jnp.where(core == 0, heads[...], pltpu.roll(heads[...], 120, 1))
    fixed[BIAS : BIAS + 1, 0:128] = own[0:1]
    fixed[RATE : RATE + 1, 0:128] = -jnp.exp(own[1:2])


def conv_kernel(
    xs_in, sent_in, got_in, halo_0_in, halo_1_in, fixed_in,
    added_out, x_out, bc_out, cum_out, delta_out, rows, steps, x_conv, bc_conv, cums, deltas,
    xs, sent, got, halo_0, halo_1, fixed, sems,
):
    core, chip = place()
    mine, other = tokens(core), tokens(1 - core)
    fetch(
        [
            (xs_in, xs),
            (sent_in.at[:, 512:1152], sent),
            (got_in.at[:, 0:1152], got),
            (halo_0_in, halo_0),
            (halo_1_in, halo_1),
            (fixed_in, fixed),
        ],
        sems.at[4:10],
    )
    first = pl.multiple_of(core * ROWS + 16, 16)
    second = pl.multiple_of((1 - core) * ROWS + 16, 16)
    rows[pl.ds(first, ROWS), 0:512] = xs[...].astype(F32)
    rows[pl.ds(first, ROWS), 512:1024] = sent[:, 0:512].astype(F32)
    rows[pl.ds(second, ROWS), :] = got[:, 0:1024].astype(F32)
    halo = halo_0[...].astype(F32) + halo_1[...].astype(F32)
    rows[0:16, :] = jnp.where(chip == 0, fixed[0:16, :], halo)
    for lane in range(0, 1024, 128):
        cut = slice(lane, lane + 128)
        total = fixed[TAPS : TAPS + 1, cut] * rows[13 : 13 + CHIP, cut]
        for k in range(1, 4):
            total = total + fixed[TAPS + k : TAPS + k + 1, cut] * rows[13 + k : 13 + k + CHIP, cut]
        value = silu(total).astype(BF16)
        if lane < 512:
            x_conv[:, cut] = value
        else:
            bc_conv[:, lane - 512 : lane - 384] = value
    steps[mine, :] = sent[:, 512:640].astype(F32)
    steps[other, :] = got[:, 1024:1152].astype(F32)
    raw = jnp.where(core == 0, steps[...], pltpu.roll(steps[...], 120, 1)) + fixed[BIAS : BIAS + 1, 0:128]
    delta = jnp.maximum(raw, 0.0) + jnp.log(1.0 + jnp.exp(-jnp.abs(raw)))
    logs = delta * fixed[RATE : RATE + 1, 0:128]
    row = lax.broadcasted_iota(jnp.int32, (CHIP, CHIP), 0)
    column = lax.broadcasted_iota(jnp.int32, (CHIP, CHIP), 1)
    cum = jnp.dot((row >= column).astype(F32), logs, precision=EXACT, preferred_element_type=F32)
    cums[...] = cum
    deltas[...] = delta
    kept = copies(
        [(x_conv, x_out), (bc_conv, bc_out), (cums, cum_out), (deltas, delta_out)],
        sems.at[0:4],
    )
    for copy in kept:
        copy.start()
    last = cum[CHIP - 1 : CHIP, :]
    trailing = jnp.dot(jnp.exp(last - cum) * delta, spread(), precision=EXACT, preferred_element_type=F32)
    weighted = (x_conv[...].astype(F32) * trailing).astype(BF16)
    added = lax.dot_general(
        weighted, bc_conv[:, 0:N], (((0,), (0,)), ((), ())), preferred_element_type=F32
    )
    high = last.astype(BF16).astype(F32)
    middle = (last - high).astype(BF16).astype(F32)
    low = last - high - middle
    line = lax.broadcasted_iota(jnp.int32, (16, N), 0)
    for h in range(HEADS):
        added_out[h, 0:P_SIZE, :] = added[h * P_SIZE : (h + 1) * P_SIZE].astype(BF16)
        terms = jnp.where(
            line == 0,
            jnp.broadcast_to(high[:, h : h + 1], (16, N)),
            jnp.where(
                line == 1,
                jnp.broadcast_to(middle[:, h : h + 1], (16, N)),
                jnp.where(line == 2, jnp.broadcast_to(low[:, h : h + 1], (16, N)), 0.0),
            ),
        )
        added_out[h, P_SIZE : P_SIZE + 16, :] = terms.astype(BF16)
    for copy in kept:
        copy.wait()


def inside_kernel(x_in, bc_in, cum_in, delta_in, skip, out, x, bc, cum, delta, total, sems):
    core, _ = place()
    fetch([(x_in, x), (bc_in, bc), (cum_in, cum), (delta_in, delta)], sems)
    scores = lax.dot_general(
        bc[:, N : 2 * N], bc[:, 0:N], (((1,), (1,)), ((), ())), preferred_element_type=F32
    )
    row = lax.broadcasted_iota(jnp.int32, (CHIP, CHIP), 0)
    column = lax.broadcasted_iota(jnp.int32, (CHIP, CHIP), 1)
    scores = jnp.where(row >= column, scores, 0.0)
    cum_t = jnp.transpose(cum[...])
    delta_t = jnp.transpose(delta[...])
    lane = lax.broadcasted_iota(jnp.int32, (CHIP, 128), 1)
    for pair in range(HEADS // 2):
        cut = slice(pair * 128, pair * 128 + 128)
        values = x[:, cut]
        both = []
        for h in (2 * pair, 2 * pair + 1):
            decay = jnp.exp(jnp.minimum(cum[:, h : h + 1] - cum_t[h : h + 1, :], 0.0))
            weights = (decay * scores * delta_t[h : h + 1, :]).astype(BF16)
            through = skip[core * HEADS + h] * values.astype(F32)
            both.append(jnp.dot(weights, values, preferred_element_type=F32) + through)
        total[:, cut] = jnp.where(lane < P_SIZE, both[0], both[1])
    fetch([(total, out)], sems)


def prefix_kernel(got, first, out):
    state = first[...]
    for chip in range(CHIPS):
        out[chip] = state.astype(BF16)
        if chip < CHIPS - 1:
            terms = got[chip, P_SIZE : P_SIZE + 16, :].astype(F32)
            decay = jnp.exp(terms[0:1] + terms[1:2] + terms[2:3])
            state = decay * state + got[chip, 0:P_SIZE, :].astype(F32)


def carry_kernel(
    state_in, bc_in, cum_in, inside_in, zs, got, gain_in,
    keep, to_core, to_next, to_cross, state, c, cum, inside, gate, gain, pieces, sems,
):
    core, _ = place()
    fetch(
        [
            (bc_in.at[:, N : 2 * N], c),
            (cum_in, cum),
            (inside_in, inside),
            (zs.at[:, lanes(core)], gate.at[tokens(core), :]),
            (got.at[:, 1152:1664], gate.at[tokens(1 - core), :]),
            (state_in, state),
            (gain_in, gain),
        ],
        sems,
    )
    carried = lax.dot_general(
        c[...], state[...], (((1,), (1,)), ((), ())), preferred_element_type=F32
    )
    decay = jnp.dot(jnp.exp(cum[...]), spread(), precision=EXACT, preferred_element_type=F32)
    gated = (inside[...] + carried * decay) * silu(gate[...].astype(F32))
    pieces[...] = gated.astype(BF16).reshape(2, 4, 2, 16, HALF)

    def piece(side, parity):
        return pieces[pl.ds(side, 1), :, pl.ds(parity, 1)].reshape(64, HALF)

    odd = lax.rem(lax.axis_index("tensor"), 2)
    whole = gain[:, lanes(core)]
    high = whole.astype(BF16).astype(F32)
    middle = (whole - high).astype(BF16).astype(F32)
    low = whole - high - middle
    line = lax.broadcasted_iota(jnp.int32, (16, HALF), 0)
    terms = jnp.where(line == 0, high, jnp.where(line == 1, middle, jnp.where(line == 2, low, 0.0)))
    for out, side, parity in (
        (keep, core, odd), (to_core, 1 - core, odd), (to_next, core, 1 - odd), (to_cross, 1 - core, 1 - odd),
    ):
        out[0:64, :] = piece(side, parity)
        out[64:80, :] = terms.astype(BF16)


def norm_kernel(keep, core_got, next_got, cross_got, out):
    core, _ = place()
    odd = lax.rem(lax.axis_index("tensor"), 2)
    for mine, came, position in ((keep, core_got, odd), (next_got, cross_got, 1 - odd)):
        values = [ref[0:64, :].astype(F32) for ref in (mine, came)]
        squares = jnp.sum(values[0] * values[0] + values[1] * values[1], axis=1, keepdims=True)
        factor = lax.rsqrt(squares * (1.0 / 1024.0) + 1e-05)
        for ref, value, side in ((mine, values[0], core), (came, values[1], 1 - core)):
            terms = ref[64:80, :].astype(F32)
            gain = terms[0:1] + terms[1:2] + terms[2:3]
            at = pl.ds(pl.multiple_of(position * 1024 + side * HALF, HALF), HALF)
            out[:, at] = (value * factor * gain).astype(BF16)


def product_kernel(*refs):
    *blocks, weights_in, out, rows, weights, result, sems = refs
    count = len(blocks)
    weight_copies = copies([(weights_in.at[i], weights.at[i]) for i in range(4)], sems)
    row_copies = copies([(block, rows.at[r * 64 : (r + 1) * 64]) for r, block in enumerate(blocks)], sems.at[4:])
    for copy in weight_copies[:1] + row_copies + weight_copies[1:]:
        copy.start()
    for copy in row_copies:
        copy.wait()
    moving = []
    for side in range(2):
        weight_copies[2 * side].wait()
        value = jnp.dot(rows[:, 0:1024], weights[2 * side], preferred_element_type=F32)
        weight_copies[2 * side + 1].wait()
        value = value + jnp.dot(rows[:, 1024:2048], weights[2 * side + 1], preferred_element_type=F32)
        value = value.astype(BF16)
        for r in range(count):
            result[side, :, r] = value[r * 64 : (r + 1) * 64].reshape(4, 16, HALF)
        copy = pltpu.make_async_copy(
            result.at[side], out.at[:, :, :, side * HALF : (side + 1) * HALF], sems.at[4 + count + side]
        )
        copy.start()
        moving.append(copy)
    for copy in moving:
        copy.wait()


def product(blocks, weights):
    count = len(blocks)
    return call(
        product_kernel,
        shaped((4, count, 16, 1024), BF16),
        scratch=[
            pltpu.VMEM((count * 64, 2048), BF16),
            pltpu.VMEM((4, 1024, HALF), BF16),
            pltpu.VMEM((2, 4, count, 16, HALF), BF16),
            pltpu.SemaphoreType.DMA((6 + count,)),
        ],
        in_specs=[HBM] * (count + 1),
        out_specs=HBM,
        limit=WIDE,
    )(*blocks, weights)


def summed_over(terms, unit):
    total = terms[0, unit].astype(F32)
    for source in range(1, 4):
        total = total + terms[source, unit].astype(F32)
    return total.astype(BF16)


def collect_kernel(near, far, out, summed, sems):
    _, chip = place()
    moving = copies([(near, summed)], sems)
    moving[0].start()
    for r, before in enumerate(FAR):
        out[lax.rem(chip + (CHIPS - before), CHIPS)] = summed_over(far, r)
    moving[0].wait()
    for r, before in enumerate(NEAR):
        out[lax.rem(chip + (CHIPS - before), CHIPS)] = summed[r]


def body(
    xs, bcs, zs, dt_raw, tail_x, tail_bc, conv_x, conv_bc,
    dt_bias, a_log, d_skip, init_state, norm_gain, out_weight,
):
    core, chip = place()
    weights = lax.all_gather(out_weight, "tensor", axis=0, tiled=True, axis_index_groups=BOTH)
    sent, halo_0, halo_1, mine, fixed = call(
        pack_kernel,
        (
            shaped((ROWS, 1664), BF16),
            shaped((16, 1024), BF16),
            shaped((16, 1024), BF16),
            shaped((ROWS, HALF), BF16),
            shaped((32, 1024), F32),
        ),
        scratch=[
            pltpu.VMEM((ROWS, 2, N), BF16),
            pltpu.VMEM((16, ROWS), BF16),
            pltpu.VMEM((3, 1024), BF16),
            pltpu.VMEM((3, 2, N), BF16),
            pltpu.VMEM((4, 1024), BF16),
            pltpu.VMEM((4, 2, N), BF16),
            pltpu.VMEM((1, 16), F32),
            pltpu.VMEM((1, 16), F32),
            pltpu.VMEM((2, 128), F32),
            pltpu.SemaphoreType.DMA((13,)),
        ],
        in_specs=[HBM] * 10,
        out_specs=[VMEM] * 5,
        moved=1 << 20,
        limit=WIDE,
    )(
        xs, zs, bcs, dt_raw.T, tail_x, tail_bc, conv_x, conv_bc,
        dt_bias.reshape(1, 16), a_log.reshape(1, 16),
    )
    got = lax.ppermute(sent, "context", PAIR)
    halo_0 = lax.ppermute(halo_0, "context", TO_CORE_0)
    halo_1 = lax.ppermute(halo_1, "context", TO_CORE_1)
    added, x_conv, bc_conv, cum, delta = call(
        conv_kernel,
        (
            shaped((HEADS, P_SIZE + 16, N), BF16),
            shaped((CHIP, HALF), BF16),
            shaped((CHIP, 512), BF16),
            shaped((CHIP, 128), F32),
            shaped((CHIP, 128), F32),
        ),
        scratch=[
            pltpu.VMEM((CHIP + 16, 1024), F32),
            pltpu.VMEM((CHIP, 128), F32),
            pltpu.VMEM((CHIP, HALF), BF16),
            pltpu.VMEM((CHIP, 512), BF16),
            pltpu.VMEM((CHIP, 128), F32),
            pltpu.VMEM((CHIP, 128), F32),
            pltpu.VMEM((ROWS, HALF), BF16),
            pltpu.VMEM((ROWS, 640), BF16),
            pltpu.VMEM((ROWS, 1152), BF16),
            pltpu.VMEM((16, 1024), BF16),
            pltpu.VMEM((16, 1024), BF16),
            pltpu.VMEM((32, 1024), F32),
            pltpu.SemaphoreType.DMA((10,)),
        ],
        in_specs=[HBM] * 6,
        out_specs=[VMEM] + [HBM] * 4,
        limit=WIDE,
        flops=200_000_000,
        moved=2 << 20,
    )(mine, sent, got, halo_0, halo_1, fixed)
    increments = lax.all_to_all(added, "context", 0, 0, tiled=True, axis_index_groups=SAME_CORE)
    inside = call(
        inside_kernel,
        shaped((CHIP, HALF), F32),
        scratch=[
            pltpu.VMEM((CHIP, HALF), BF16),
            pltpu.VMEM((CHIP, 512), BF16),
            pltpu.VMEM((CHIP, 128), F32),
            pltpu.VMEM((CHIP, 128), F32),
            pltpu.VMEM((CHIP, HALF), F32),
            pltpu.SemaphoreType.DMA((4,)),
        ],
        in_specs=[HBM] * 4 + [SMEM],
        out_specs=HBM,
        flops=400_000_000,
        moved=2 << 20,
    )(x_conv, bc_conv, cum, delta, d_skip)
    increments, inside = lax.optimization_barrier((increments, inside))
    first = lax.dynamic_index_in_dim(init_state, core * HEADS + chip, 0, keepdims=False)
    states = call(
        prefix_kernel,
        shaped((CHIPS, P_SIZE, N), BF16),
        in_specs=[VMEM] * 2,
        moved=1 << 20,
    )(increments, first)
    states = lax.all_to_all(states, "context", 0, 0, tiled=True, axis_index_groups=SAME_CORE)
    states, weights = lax.optimization_barrier((states, weights))
    weights = lax.all_gather(weights, "context", axis=0, tiled=True, axis_index_groups=CORES)
    weights = weights.reshape(4, 1024, HALF)
    gain = norm_gain.reshape(1, 1024)
    keep, to_core, to_next, to_cross = call(
        carry_kernel,
        (shaped((80, HALF), BF16),) * 4,
        scratch=[
            pltpu.VMEM((HEADS * P_SIZE, N), BF16),
            pltpu.VMEM((CHIP, N), BF16),
            pltpu.VMEM((CHIP, 128), F32),
            pltpu.VMEM((CHIP, HALF), F32),
            pltpu.VMEM((CHIP, HALF), BF16),
            pltpu.VMEM((1, 1024), F32),
            pltpu.VMEM((2, 4, 2, 16, HALF), BF16),
            pltpu.SemaphoreType.DMA((7,)),
        ],
        in_specs=[HBM] * 7,
        out_specs=[VMEM] * 4,
        limit=WIDE,
        flops=100_000_000,
        moved=2 << 20,
    )(states.reshape(HEADS * P_SIZE, N), bc_conv, cum, inside, zs, got, gain)
    core_got = lax.ppermute(to_core, "context", PAIR)
    next_got = lax.ppermute(to_next, "tensor", BESIDE)
    cross_got = lax.ppermute(to_cross, ("context", "tensor"), CROSS)
    normed = call(
        norm_kernel,
        shaped((64, 2048), BF16),
        in_specs=[VMEM] * 4,
        out_specs=VMEM,
        moved=1 << 20,
    )(keep, core_got, next_got, cross_got)

    up, down = [normed], [normed]
    for step in range(4):
        up.append(lax.ppermute(up[-1], "context", UP))
        if step < 3:
            down.append(lax.ppermute(down[-1], "context", DOWN))
    blocks = {**{r: up[r] for r in range(5)}, **{CHIPS - r: down[r] for r in range(1, 4)}}
    near = product([blocks[r] for r in NEAR], weights)
    far = product([blocks[r] for r in FAR], weights)
    near = lax.psum_scatter(
        near.reshape(4 * 16 * len(NEAR), 1024), "tensor",
        scatter_dimension=0, tiled=True, axis_index_groups=PARITY,
    )
    far = lax.all_to_all(
        far.reshape(4, 16 * len(FAR), 1024), "tensor", 0, 0, tiled=True, axis_index_groups=PARITY
    )
    ready = call(
        collect_kernel,
        shaped((CHIPS, 16, 1024), BF16),
        scratch=[pltpu.VMEM((len(NEAR), 16, 1024), BF16), pltpu.SemaphoreType.DMA((1,))],
        in_specs=[HBM, VMEM],
        moved=2 << 20,
    )(near.reshape(len(NEAR), 16, 1024), far.reshape(4, len(FAR), 16, 1024))
    return lax.all_to_all(
        ready, "context", 0, 0, tiled=True, axis_index_groups=SAME_CORE
    ).transpose(1, 0, 2).reshape(16, 8192)


def solution(mesh):
    return jax.shard_map(
        body,
        mesh=mesh,
        in_specs=(
            P(("dp", "context"), "tensor"),
            P(("dp", "context"), None, "tensor"),
            P(("dp", "context"), "tensor"),
            P(("dp", "context"), "tensor"),
            P("dp", "tensor"),
            P("dp", None, "tensor"),
            P(None, "tensor"),
            P(None, None, "tensor"),
            P("tensor"),
            P("tensor"),
            P("tensor"),
            P(("dp", "tensor"), None, None),
            P("tensor"),
            P("tensor", "context"),
        ),
        out_specs=P(("dp", "context", "tensor"), None),
        check_vma=False,
    )
```

time: 190 us -> 173 us (0.911)
  the two profiles are of different devices: /device:TPU:24 before, /device:TPU:2 now
where the time goes in v2:
time: 173 us; the launch traced here: 172 us
  starting transfers between devices  47.6 us (28%)
  blocking collectives  46.4 us (27%)
  waiting for transfers between devices  33.5 us (19%)
  Pallas kernels  21.4 us (12%)
  between operations  13.4 us (8%)
  local copies, waits for them, and re-layouts  10 us (6%)
    all_to_all x1, blocking collectives, body(): lax.all_to_all(far.reshape(4, 16 * len(FAR), 1024), 'tensor', 0, 0, tiled...  17.7 us
    ppermute x4, waiting for transfers between devices, body(): up.append(lax.ppermute(up[-1], 'context', UP))  15.1 us
    all_to_all x1, starting transfers between devices, body(): lax.all_to_all(added, 'context', 0, 0, tiled=True, axis_index_groups=SAME...  15 us
    all_to_all x1, blocking collectives, body(): lax.all_to_all(states, 'context', 0, 0, tiled=True, axis_index_groups=SAM...  14.9 us
    all_to_all x1, blocking collectives, body(): lax.all_to_all(ready, 'context', 0, 0, tiled=True, axis_index_groups=SAME...  13.8 us
    ppermute x3, starting transfers between devices, body(): down.append(lax.ppermute(down[-1], 'context', DOWN))  10.5 us
    ppermute x4, starting transfers between devices, body(): up.append(lax.ppermute(up[-1], 'context', UP))  10.2 us
    pallas_call x2, Pallas kernels, product(): call(product_kernel, shaped((4, count, 16, 1024), BF16), scratch=[pltpu.V...  8.47 us
  transfers between devices with their start and end apart: 17, of which 9 were waited for; matrix products, arithmetic and copies ran while one was open for 0% of the time, Pallas kernels for 10%

profile of v2, /device:TPU:2, one launch (start us, length us, event | category | flops | bytes accessed | tf_op | source)
XLA Modules:
  0.0 172.2 jit_solution(2844362865319781039)
XLA Ops:
  6.5 0.7 all-gather.3.cloned.1.call-update
  7.3 2.5 %shard_map.136 = (bf16[128,1664]{1,0:T(8,128)(2,1)}, bf16[16,1024]{1,0:T(8,128)(2,1)}, bf16[16,1024]{1,0:T(8,128)(2,1)}, bf16[128,512]{1,0:T(8,128)(2,1)}, f32[32,1024]{1,0:T(8,128)}) custom-call(bf16[128,1024]{1,0:T(8,128)(2,1)} %xs.1, bf16[128,1024]{1,0:T(8,128)(2,1)} %zs.3, bf16[128,2,256]{2,1,0:T(2,128)(2,1)} %bcs.1, bf16[16,128]{1,0:T(8,128)(2,1)} %bitcast.23, ...), custom_call_target="tpu_custom_call" | custom-call | bytes 1048576 | tf_op jit(solution)/shard_map/pallas_call | solution.py:378
  9.8 1.9 %collective-permute-start = (bf16[128,1664]{1,0:T(8,128)(2,1)}, bf16[128,1664]{1,0:T(8,128)(2,1)S(1)}, u32[]{:S(2)}, u32[]{:S(2)}) collective-permute-start(bf16[128,1664]{1,0:T(8,128)(2,1)} %get-tuple-element.24.sent_in), channel_id=1, source_target_pairs={{0,8},{8,0},{16,24},{24,16},{32,40},{40,32},{48,56},{56,48},{64,72... | collective-permute-start | bytes 1277960 | tf_op jit(solution)/shard_map/ppermute | solution.py:407
  11.7 0.7 collective-permute-start.1
  12.4 0.7 collective-permute-start.2
  13.1 0.6 collective-permute-done.got_in.got
  13.7 0.7 copy-done.9
  14.4 5.3 %shard_map.137 = (bf16[8,80,256]{2,1,0:T(8,128)(2,1)}, bf16[256,512]{1,0:T(8,128)(2,1)}, bf16[256,512]{1,0:T(8,128)(2,1)}, f32[256,128]{1,0:T(8,128)}, f32[256,128]{1,0:T(8,128)}) custom-call(bf16[128,512]{1,0:T(8,128)(2,1)} %get-tuple-element.23.xs_in, bf16[128,1664]{1,0:T(8,128)(2,1)} %get-tuple-element.24.sent_in, bf16[128,1664]{1,0:T(8,128)(2,1)} %copy-done.9, ...), custom_call_target="tpu_custom_call" | custom-call | flops 200000000 | bytes 2097152 | tf_op jit(solution)/shard_map/pallas_call | solution.py:410
  19.7 15.0 %all-to-all-start = ((bf16[8,80,256]{2,1,0:T(8,128)(2,1)}), bf16[8,80,256]{2,1,0:T(8,128)(2,1)S(1)}, u32[]{:S(2)}, u32[]{:S(2)}) async-start(bf16[8,80,256]{2,1,0:T(8,128)(2,1)} %get-tuple-element.28), calls=%async_computation | async-start | bytes 655360 | tf_op jit(solution)/shard_map/all_to_all | solution.py:440
  34.8 0.8 dynamic-slice_bitcast_fusion.first
  35.6 0.9 copy-done.2
  36.6 0.9 copy-done.4
  37.5 0.9 copy-done.6
  38.4 0.9 copy-done.7
  39.3 0.7 copy-done.8
  40.0 1.8 %shard_map.138.inside_in = f32[256,512]{1,0:T(8,128)S(1)} custom-call(bf16[256,512]{1,0:T(8,128)(2,1)S(1)} %copy-done.6, bf16[256,512]{1,0:T(8,128)(2,1)S(1)} %copy-done.2, f32[256,128]{1,0:T(8,128)S(1)} %copy-done.4, f32[256,128]{1,0:T(8,128)S(1)} %copy-done.7, f32[16]{0:T(128)S(1)} %copy-done.8), custom_call_target="tpu_custom_call" | custom-call | flops 400000000 | bytes 2097152 | tf_op jit(solution)/shard_map/pallas_call | solution.py:441
  41.8 0.8 copy-done.1
  42.6 4.6 %all-to-all-done.got = bf16[8,80,256]{2,1,0:T(8,128)(2,1)S(1)} async-done(((bf16[8,80,256]{2,1,0:T(8,128)(2,1)}), bf16[8,80,256]{2,1,0:T(8,128)(2,1)S(1)}, u32[]{:S(2)}, u32[]{:S(2)}) %all-to-all-start) | async-done | bytes 327712 | tf_op jit(solution)/shard_map/all_to_all | solution.py:440
  47.2 0.1 shard_map.139
  47.3 14.9 %all_to_all.20 = bf16[8,64,256]{2,1,0:T(8,128)(2,1)} all-to-all(bf16[8,64,256]{2,1,0:T(8,128)(2,1)S(1)} %shard_map.139), channel_id=1, replica_groups={{0,16,32,48,64,80,96,112},{8,24,40,56,72,88,104,120},{1,17,33,49,65,81,..., dimensions={0} | all-to-all | bytes 524288 | tf_op jit(solution)/shard_map/all_to_all | solution.py:465
  62.3 2.8 %shard_map.140 = (bf16[80,512]{1,0:T(8,128)(2,1)}, bf16[80,512]{1,0:T(8,128)(2,1)}, bf16[80,512]{1,0:T(8,128)(2,1)}, bf16[80,512]{1,0:T(8,128)(2,1)}) custom-call(bf16[512,256]{1,0:T(8,128)(2,1)} %bitcast.21, bf16[256,512]{1,0:T(8,128)(2,1)} %get-tuple-element.30.bc_in, f32[256,128]{1,0:T(8,128)} %get-tuple-element.31.cum_in, f32[256,512]{1,0:T(8,128)} %copy-done.1, ...), custom_call_target="tpu_custom_call" | custom-call | flops 100000000 | bytes 2097152 | tf_op jit(solution)/shard_map/pallas_call | solution.py:470
  65.1 3.2 %collective-permute-start.3 = (bf16[80,512]{1,0:T(8,128)(2,1)}, bf16[80,512]{1,0:T(8,128)(2,1)S(1)}, u32[]{:S(2)}, u32[]{:S(2)}) collective-permute-start(bf16[80,512]{1,0:T(8,128)(2,1)} %get-tuple-element.37), channel_id=1, source_target_pairs={{0,8},{8,0},{16,24},{24,16},{32,40},{40,32},{48,56},{56,48},{64,72... | collective-permute-start | bytes 245768 | tf_op jit(solution)/shard_map/ppermute | solution.py:489
  68.3 3.5 %collective-permute-start.4 = (bf16[80,512]{1,0:T(8,128)(2,1)}, bf16[80,512]{1,0:T(8,128)(2,1)S(1)}, u32[]{:S(2)}, u32[]{:S(2)}) collective-permute-start(bf16[80,512]{1,0:T(8,128)(2,1)} %get-tuple-element.38), channel_id=1, source_target_pairs={{0,1},{1,0},{2,3},{3,2},{4,5},{5,4},{6,7},{7,6},{8,9},{9,8},{10,11... | collective-permute-start | bytes 245768 | tf_op jit(solution)/shard_map/ppermute | solution.py:490
  71.8 1.9 %collective-permute-start.5 = (bf16[80,512]{1,0:T(8,128)(2,1)}, bf16[80,512]{1,0:T(8,128)(2,1)S(1)}, u32[]{:S(2)}, u32[]{:S(2)}) collective-permute-start(bf16[80,512]{1,0:T(8,128)(2,1)} %get-tuple-element.39), channel_id=1, source_target_pairs={{0,9},{1,8},{2,11},{3,10},{4,13},{5,12},{6,15},{7,14},{8,1},{9,0},... | collective-permute-start | bytes 245768 | tf_op jit(solution)/shard_map/ppermute | solution.py:491
  73.7 1.1 collective-permute-done.4.next_got
  74.8 3.7 %collective-permute-done.5.cross_got = bf16[80,512]{1,0:T(8,128)(2,1)S(1)} collective-permute-done((bf16[80,512]{1,0:T(8,128)(2,1)}, bf16[80,512]{1,0:T(8,128)(2,1)S(1)}, u32[]{:S(2)}, u32[]{:S(2)}) %collective-permute-start.5) | collective-permute-done | bytes 81952 | tf_op jit(solution)/shard_map/ppermute | solution.py:491
  78.6 0.9 copy-done.5
  79.5 0.1 shard_map.141.refs_0_
  79.6 1.9 %collective-permute-start.7 = (bf16[64,2048]{1,0:T(8,128)(2,1)S(1)}, bf16[64,2048]{1,0:T(8,128)(2,1)S(1)}, u32[]{:S(2)}, u32[]{:S(2)}) collective-permute-start(bf16[64,2048]{1,0:T(8,128)(2,1)S(1)} %shard_map.141.refs_0_), channel_id=1, source_target_pairs={{0,112},{8,120},{16,0},{24,8},{32,16},{40,24},{48,32},{56,40},{64,... | collective-permute-start | bytes 786440 | tf_op jit(solution)/shard_map/ppermute | solution.py:504
  81.6 3.9 %collective-permute-start.6 = (bf16[64,2048]{1,0:T(8,128)(2,1)S(1)}, bf16[64,2048]{1,0:T(8,128)(2,1)S(1)}, u32[]{:S(2)}, u32[]{:S(2)}) collective-permute-start(bf16[64,2048]{1,0:T(8,128)(2,1)S(1)} %shard_map.141.refs_0_), channel_id=1, source_target_pairs={{0,16},{8,24},{16,32},{24,40},{32,48},{40,56},{48,64},{56,72},{64,... | collective-permute-start | bytes 786440 | tf_op jit(solution)/shard_map/ppermute | solution.py:502
  85.5 4.3 %collective-permute-done.7.refs_2_ = bf16[64,2048]{1,0:T(8,128)(2,1)S(1)} collective-permute-done((bf16[64,2048]{1,0:T(8,128)(2,1)S(1)}, bf16[64,2048]{1,0:T(8,128)(2,1)S(1)}, u32[]{:S(2)}, u32[]{:S(2)}) %collective-permute-start.7) | collective-permute-done | bytes 262176 | tf_op jit(solution)/shard_map/ppermute | solution.py:504
  89.8 3.4 %collective-permute-start.9 = (bf16[64,2048]{1,0:T(8,128)(2,1)S(1)}, bf16[64,2048]{1,0:T(8,128)(2,1)S(1)}, u32[]{:S(2)}, u32[]{:S(2)}) collective-permute-start(bf16[64,2048]{1,0:T(8,128)(2,1)S(1)} %collective-permute-done.7.refs_2_), channel_id=1, source_target_pairs={{0,112},{8,120},{16,0},{24,8},{32,16},{40,24},{48,32},{56,40},{64,... | collective-permute-start | bytes 786440 | tf_op jit(solution)/shard_map/ppermute | solution.py:504
  93.2 2.4 %collective-permute-start.8 = (bf16[64,2048]{1,0:T(8,128)(2,1)S(1)}, bf16[64,2048]{1,0:T(8,128)(2,1)}, u32[]{:S(2)}, u32[]{:S(2)}) collective-permute-start(bf16[64,2048]{1,0:T(8,128)(2,1)S(1)} %collective-permute-done.6.refs_1_), channel_id=1, source_target_pairs={{0,16},{8,24},{16,32},{24,40},{32,48},{40,56},{48,64},{56,72},{64,... | collective-permute-start | bytes 786440 | tf_op jit(solution)/shard_map/ppermute | solution.py:502
  95.6 3.4 %collective-permute-done.9.refs_4_ = bf16[64,2048]{1,0:T(8,128)(2,1)S(1)} collective-permute-done((bf16[64,2048]{1,0:T(8,128)(2,1)S(1)}, bf16[64,2048]{1,0:T(8,128)(2,1)S(1)}, u32[]{:S(2)}, u32[]{:S(2)}) %collective-permute-start.9) | collective-permute-done | bytes 262176 | tf_op jit(solution)/shard_map/ppermute | solution.py:504
  99.0 4.8 %collective-permute-done.8.refs_3_ = bf16[64,2048]{1,0:T(8,128)(2,1)} collective-permute-done((bf16[64,2048]{1,0:T(8,128)(2,1)S(1)}, bf16[64,2048]{1,0:T(8,128)(2,1)}, u32[]{:S(2)}, u32[]{:S(2)}) %collective-permute-start.8) | collective-permute-done | bytes 262176 | tf_op jit(solution)/shard_map/ppermute | solution.py:502
  103.8 4.6 %shard_map.142 = bf16[4,5,16,1024]{3,2,1,0:T(8,128)(2,1)} custom-call(bf16[64,2048]{1,0:T(8,128)(2,1)} %copy-done, bf16[64,2048]{1,0:T(8,128)(2,1)} %copy-done.12, bf16[64,2048]{1,0:T(8,128)(2,1)} %copy-done.11, bf16[64,2048]{1,0:T(8,128)(2,1)} %collective-permute-done.8.refs_3_, bf16[64,2048]{1,0:T(8,128)(2,1)} %copy-done.10, bf16[4,1024,512]{2,1,0:T(8,128)(2,1)} %bitcast.17), custom_call_target="tpu_custom_call" | custom-call | tf_op jit(solution)/shard_map/pallas_call | solution.py:339
  108.5 1.9 %collective-permute-start.10 = (bf16[64,2048]{1,0:T(8,128)(2,1)}, bf16[64,2048]{1,0:T(8,128)(2,1)S(1)}, u32[]{:S(2)}, u32[]{:S(2)}) collective-permute-start(bf16[64,2048]{1,0:T(8,128)(2,1)} %collective-permute-done.8.refs_3_), channel_id=1, source_target_pairs={{0,16},{8,24},{16,32},{24,40},{32,48},{40,56},{48,64},{56,72},{64,... | collective-permute-start | bytes 786440 | tf_op jit(solution)/shard_map/ppermute | solution.py:502
  110.4 5.1 %collective-permute-start.11 = (bf16[64,2048]{1,0:T(8,128)(2,1)}, bf16[64,2048]{1,0:T(8,128)(2,1)S(1)}, u32[]{:S(2)}, u32[]{:S(2)}) collective-permute-start(bf16[64,2048]{1,0:T(8,128)(2,1)} %copy-done.10), channel_id=1, source_target_pairs={{0,112},{8,120},{16,0},{24,8},{32,16},{40,24},{48,32},{56,40},{64,... | collective-permute-start | bytes 786440 | tf_op jit(solution)/shard_map/ppermute | solution.py:504
  115.6 2.8 %collective-permute-done.10.refs_0_ = bf16[64,2048]{1,0:T(8,128)(2,1)S(1)} collective-permute-done((bf16[64,2048]{1,0:T(8,128)(2,1)}, bf16[64,2048]{1,0:T(8,128)(2,1)S(1)}, u32[]{:S(2)}, u32[]{:S(2)}) %collective-permute-start.10) | collective-permute-done | bytes 262176 | tf_op jit(solution)/shard_map/ppermute | solution.py:502
  118.3 1.9 %collective-permute-start.12 = (bf16[64,2048]{1,0:T(8,128)(2,1)S(1)}, bf16[64,2048]{1,0:T(8,128)(2,1)S(1)}, u32[]{:S(2)}, u32[]{:S(2)}) collective-permute-start(bf16[64,2048]{1,0:T(8,128)(2,1)S(1)} %collective-permute-done.10.refs_0_), channel_id=1, source_target_pairs={{0,16},{8,24},{16,32},{24,40},{32,48},{40,56},{48,64},{56,72},{64,... | collective-permute-start | bytes 786440 | tf_op jit(solution)/shard_map/ppermute | solution.py:502
  120.3 7.5 %collective-permute-done.12.refs_2_ = bf16[64,2048]{1,0:T(8,128)(2,1)S(1)} collective-permute-done((bf16[64,2048]{1,0:T(8,128)(2,1)S(1)}, bf16[64,2048]{1,0:T(8,128)(2,1)S(1)}, u32[]{:S(2)}, u32[]{:S(2)}) %collective-permute-start.12) | collective-permute-done | bytes 262176 | tf_op jit(solution)/shard_map/ppermute | solution.py:502
  127.8 0.7 copy-done.15
  128.5 3.9 %shard_map.143 = bf16[4,3,16,1024]{3,2,1,0:T(8,128)(2,1)} custom-call(bf16[64,2048]{1,0:T(8,128)(2,1)} %copy-done.13, bf16[64,2048]{1,0:T(8,128)(2,1)} %copy-done.14, bf16[64,2048]{1,0:T(8,128)(2,1)} %copy-done.15, bf16[4,1024,512]{2,1,0:T(8,128)(2,1)} %bitcast.18), custom_call_target="tpu_custom_call" | custom-call | tf_op jit(solution)/shard_map/pallas_call | solution.py:339
  132.3 17.7 %all_to_all.21 = bf16[4,48,1024]{2,1,0:T(8,128)(2,1)S(1)} all-to-all(bf16[4,48,1024]{2,1,0:T(8,128)(2,1)} %bitcast.20), channel_id=1, replica_groups={{0,2,4,6},{1,3,5,7},{8,10,12,14},{9,11,13,15},{16,18,20,22},{17,19,21,2..., dimensions={0} | all-to-all | bytes 786432 | tf_op jit(solution)/shard_map/all_to_all | solution.py:512
  150.0 0.9 copy-done.3
  150.9 0.3 shard_map.144
  151.2 13.8 %all_to_all.22 = bf16[8,16,1024]{2,1,0:T(8,128)(2,1)S(1)} all-to-all(bf16[8,16,1024]{2,1,0:T(8,128)(2,1)S(1)} %shard_map.144), channel_id=1, replica_groups={{0,16,32,48,64,80,96,112},{8,24,40,56,72,88,104,120},{1,17,33,49,65,81,..., dimensions={0} | all-to-all | bytes 524288 | tf_op jit(solution)/shard_map/all_to_all | solution.py:522
  165.0 0.7 copy.16
  (39 shorter events, 0.2 us)
Async XLA Ops:
  6.5 55.7 %all-gather.3.cloned.1.call-start = ((), (), s32[]{:S(2)}) async-start(), calls=%async_computation.5 | async-start | bytes 3145728 | tf_op jit(solution)/shard_map/all_gather | solution.py:377
  9.8 3.9 %collective-permute-start = (bf16[128,1664]{1,0:T(8,128)(2,1)}, bf16[128,1664]{1,0:T(8,128)(2,1)S(1)}, u32[]{:S(2)}, u32[]{:S(2)}) collective-permute-start(bf16[128,1664]{1,0:T(8,128)(2,1)} %get-tuple-element.24.sent_in), channel_id=1, source_target_pairs={{0,8},{8,0},{16,24},{24,16},{32,40},{40,32},{48,56},{56,48},{64,72... | collective-permute-start | bytes 1277960 | tf_op jit(solution)/shard_map/ppermute | solution.py:407
  11.7 1.3 collective-permute-start.1
  12.4 0.7 collective-permute-start.2
  13.1 0.6 copy-start.16
  13.1 0.6 copy-start.17
  13.7 0.7 copy-start.9
  19.7 27.5 %all-to-all-start = ((bf16[8,80,256]{2,1,0:T(8,128)(2,1)}), bf16[8,80,256]{2,1,0:T(8,128)(2,1)S(1)}, u32[]{:S(2)}, u32[]{:S(2)}) async-start(bf16[8,80,256]{2,1,0:T(8,128)(2,1)} %get-tuple-element.28), calls=%async_computation | async-start | bytes 655360 | tf_op jit(solution)/shard_map/all_to_all | solution.py:440
  34.7 69.1 %all-gather.5.cloned.1.call-start = ((), (), s32[]{:S(2)}) async-start(), calls=%async_computation.6 | async-start | bytes 6291456 | tf_op jit(solution)/shard_map/all_gather | solution.py:467
  35.6 0.9 copy-start.2
  36.6 0.9 copy-start.4
  37.5 0.9 copy-start.6
  38.4 0.9 copy-start.7
  39.3 0.7 copy-start.8
  41.8 0.8 copy-start.1
  62.2 87.8 %reduce-scatter.2.cloned.1.call-start = ((), (), s32[]{:S(2)}) async-start(), calls=%async_computation.7 | async-start | bytes 819200 | tf_op jit(solution)/shard_map/reduce_scatter | solution.py:508
  65.1 8.6 %collective-permute-start.3 = (bf16[80,512]{1,0:T(8,128)(2,1)}, bf16[80,512]{1,0:T(8,128)(2,1)S(1)}, u32[]{:S(2)}, u32[]{:S(2)}) collective-permute-start(bf16[80,512]{1,0:T(8,128)(2,1)} %get-tuple-element.37), channel_id=1, source_target_pairs={{0,8},{8,0},{16,24},{24,16},{32,40},{40,32},{48,56},{56,48},{64,72... | collective-permute-start | bytes 245768 | tf_op jit(solution)/shard_map/ppermute | solution.py:489
  68.3 6.5 %collective-permute-start.4 = (bf16[80,512]{1,0:T(8,128)(2,1)}, bf16[80,512]{1,0:T(8,128)(2,1)S(1)}, u32[]{:S(2)}, u32[]{:S(2)}) collective-permute-start(bf16[80,512]{1,0:T(8,128)(2,1)} %get-tuple-element.38), channel_id=1, source_target_pairs={{0,1},{1,0},{2,3},{3,2},{4,5},{5,4},{6,7},{7,6},{8,9},{9,8},{10,11... | collective-permute-start | bytes 245768 | tf_op jit(solution)/shard_map/ppermute | solution.py:490
  71.8 6.8 %collective-permute-start.5 = (bf16[80,512]{1,0:T(8,128)(2,1)}, bf16[80,512]{1,0:T(8,128)(2,1)S(1)}, u32[]{:S(2)}, u32[]{:S(2)}) collective-permute-start(bf16[80,512]{1,0:T(8,128)(2,1)} %get-tuple-element.39), channel_id=1, source_target_pairs={{0,9},{1,8},{2,11},{3,10},{4,13},{5,12},{6,15},{7,14},{8,1},{9,0},... | collective-permute-start | bytes 245768 | tf_op jit(solution)/shard_map/ppermute | solution.py:491
  78.6 0.9 copy-start.5
  79.6 24.2 %copy-start = (bf16[64,2048]{1,0:T(8,128)(2,1)}, bf16[64,2048]{1,0:T(8,128)(2,1)S(1)}, u32[]{:S(2)}) copy-start(bf16[64,2048]{1,0:T(8,128)(2,1)S(1)} %shard_map.141.refs_0_) | copy-start | bytes 786436
  79.6 10.1 %collective-permute-start.7 = (bf16[64,2048]{1,0:T(8,128)(2,1)S(1)}, bf16[64,2048]{1,0:T(8,128)(2,1)S(1)}, u32[]{:S(2)}, u32[]{:S(2)}) collective-permute-start(bf16[64,2048]{1,0:T(8,128)(2,1)S(1)} %shard_map.141.refs_0_), channel_id=1, source_target_pairs={{0,112},{8,120},{16,0},{24,8},{32,16},{40,24},{48,32},{56,40},{64,... | collective-permute-start | bytes 786440 | tf_op jit(solution)/shard_map/ppermute | solution.py:504
  81.6 11.6 %collective-permute-start.6 = (bf16[64,2048]{1,0:T(8,128)(2,1)S(1)}, bf16[64,2048]{1,0:T(8,128)(2,1)S(1)}, u32[]{:S(2)}, u32[]{:S(2)}) collective-permute-start(bf16[64,2048]{1,0:T(8,128)(2,1)S(1)} %shard_map.141.refs_0_), channel_id=1, source_target_pairs={{0,16},{8,24},{16,32},{24,40},{32,48},{40,56},{48,64},{56,72},{64,... | collective-permute-start | bytes 786440 | tf_op jit(solution)/shard_map/ppermute | solution.py:502
  89.8 14.1 %copy-start.11 = (bf16[64,2048]{1,0:T(8,128)(2,1)}, bf16[64,2048]{1,0:T(8,128)(2,1)S(1)}, u32[]{:S(2)}) copy-start(bf16[64,2048]{1,0:T(8,128)(2,1)S(1)} %collective-permute-done.7.refs_2_) | copy-start | bytes 786436
  89.8 9.3 %collective-permute-start.9 = (bf16[64,2048]{1,0:T(8,128)(2,1)S(1)}, bf16[64,2048]{1,0:T(8,128)(2,1)S(1)}, u32[]{:S(2)}, u32[]{:S(2)}) collective-permute-start(bf16[64,2048]{1,0:T(8,128)(2,1)S(1)} %collective-permute-done.7.refs_2_), channel_id=1, source_target_pairs={{0,112},{8,120},{16,0},{24,8},{32,16},{40,24},{48,32},{56,40},{64,... | collective-permute-start | bytes 786440 | tf_op jit(solution)/shard_map/ppermute | solution.py:504
  93.2 5.9 %copy-start.12 = (bf16[64,2048]{1,0:T(8,128)(2,1)}, bf16[64,2048]{1,0:T(8,128)(2,1)S(1)}, u32[]{:S(2)}) copy-start(bf16[64,2048]{1,0:T(8,128)(2,1)S(1)} %collective-permute-done.6.refs_1_) | copy-start | bytes 786436
  93.2 10.6 %collective-permute-start.8 = (bf16[64,2048]{1,0:T(8,128)(2,1)S(1)}, bf16[64,2048]{1,0:T(8,128)(2,1)}, u32[]{:S(2)}, u32[]{:S(2)}) collective-permute-start(bf16[64,2048]{1,0:T(8,128)(2,1)S(1)} %collective-permute-done.6.refs_1_), channel_id=1, source_target_pairs={{0,16},{8,24},{16,32},{24,40},{32,48},{40,56},{48,64},{56,72},{64,... | collective-permute-start | bytes 786440 | tf_op jit(solution)/shard_map/ppermute | solution.py:502
  99.0 4.8 %copy-start.10 = (bf16[64,2048]{1,0:T(8,128)(2,1)}, bf16[64,2048]{1,0:T(8,128)(2,1)S(1)}, u32[]{:S(2)}) copy-start(bf16[64,2048]{1,0:T(8,128)(2,1)S(1)} %collective-permute-done.9.refs_4_) | copy-start | bytes 786436
  108.5 9.8 %collective-permute-start.10 = (bf16[64,2048]{1,0:T(8,128)(2,1)}, bf16[64,2048]{1,0:T(8,128)(2,1)S(1)}, u32[]{:S(2)}, u32[]{:S(2)}) collective-permute-start(bf16[64,2048]{1,0:T(8,128)(2,1)} %collective-permute-done.8.refs_3_), channel_id=1, source_target_pairs={{0,16},{8,24},{16,32},{24,40},{32,48},{40,56},{48,64},{56,72},{64,... | collective-permute-start | bytes 786440 | tf_op jit(solution)/shard_map/ppermute | solution.py:502
  110.4 9.8 %collective-permute-start.11 = (bf16[64,2048]{1,0:T(8,128)(2,1)}, bf16[64,2048]{1,0:T(8,128)(2,1)S(1)}, u32[]{:S(2)}, u32[]{:S(2)}) collective-permute-start(bf16[64,2048]{1,0:T(8,128)(2,1)} %copy-done.10), channel_id=1, source_target_pairs={{0,112},{8,120},{16,0},{24,8},{32,16},{40,24},{48,32},{56,40},{64,... | collective-permute-start | bytes 786440 | tf_op jit(solution)/shard_map/ppermute | solution.py:504
  118.3 9.5 %copy-start.13 = (bf16[64,2048]{1,0:T(8,128)(2,1)}, bf16[64,2048]{1,0:T(8,128)(2,1)S(1)}, u32[]{:S(2)}) copy-start(bf16[64,2048]{1,0:T(8,128)(2,1)S(1)} %collective-permute-done.10.refs_0_) | copy-start | bytes 786436
  118.3 9.5 %collective-permute-start.12 = (bf16[64,2048]{1,0:T(8,128)(2,1)S(1)}, bf16[64,2048]{1,0:T(8,128)(2,1)S(1)}, u32[]{:S(2)}, u32[]{:S(2)}) collective-permute-start(bf16[64,2048]{1,0:T(8,128)(2,1)S(1)} %collective-permute-done.10.refs_0_), channel_id=1, source_target_pairs={{0,16},{8,24},{16,32},{24,40},{32,48},{40,56},{48,64},{56,72},{64,... | collective-permute-start | bytes 786440 | tf_op jit(solution)/shard_map/ppermute | solution.py:502
  120.2 7.5 %copy-start.14 = (bf16[64,2048]{1,0:T(8,128)(2,1)}, bf16[64,2048]{1,0:T(8,128)(2,1)S(1)}, u32[]{:S(2)}) copy-start(bf16[64,2048]{1,0:T(8,128)(2,1)S(1)} %collective-permute-done.11.refs_1_) | copy-start | bytes 786436
  127.8 0.7 copy-start.15
  150.0 0.9 copy-start.3
Sparse Core Ops, SparseCore 0:
  9.4 45.6 all-gather.2
  62.4 19.2 all-gather.4
  108.6 27.9 reduce-scatter.1

commit v3 on v2

--- a/solution.py
+++ b/solution.py
@@ -45,7 +45,6 @@
     )
 
 
-SMEM = pl.BlockSpec(memory_space=pltpu.SMEM)
 VMEM = pl.BlockSpec(memory_space=pltpu.VMEM)
 HBM = pl.BlockSpec(memory_space=pltpu.HBM)
 
@@ -217,9 +216,9 @@
         copy.wait()
 
 
-def inside_kernel(x_in, bc_in, cum_in, delta_in, skip, out, x, bc, cum, delta, total, sems):
+def inside_kernel(x_in, bc_in, cum_in, delta_in, skip_in, out, x, bc, cum, delta, skip, total, sems):
     core, _ = place()
-    fetch([(x_in, x), (bc_in, bc), (cum_in, cum), (delta_in, delta)], sems)
+    fetch([(x_in, x), (bc_in, bc), (cum_in, cum), (delta_in, delta), (skip_in, skip)], sems)
     scores = lax.dot_general(
         bc[:, N : 2 * N], bc[:, 0:N], (((1,), (1,)), ((), ())), preferred_element_type=F32
     )
@@ -236,7 +235,8 @@
         for h in (2 * pair, 2 * pair + 1):
             decay = jnp.exp(jnp.minimum(cum[:, h : h + 1] - cum_t[h : h + 1, :], 0.0))
             weights = (decay * scores * delta_t[h : h + 1, :]).astype(BF16)
-            through = skip[core * HEADS + h] * values.astype(F32)
+            scale = jnp.where(core == 0, skip[:, h : h + 1], skip[:, HEADS + h : HEADS + h + 1])
+            through = scale * values.astype(F32)
             both.append(jnp.dot(weights, values, preferred_element_type=F32) + through)
         total[:, cut] = jnp.where(lane < P_SIZE, both[0], both[1])
     fetch([(total, out)], sems)
@@ -307,26 +307,24 @@
             out[:, at] = (value * factor * gain).astype(BF16)
 
 
+def stage_kernel(source, out, sems):
+    fetch([(source.at[i], out.at[i]) for i in range(4)], sems)
+
+
 def product_kernel(*refs):
-    *blocks, weights_in, out, rows, weights, result, sems = refs
+    *blocks, weights, out, rows, result, sems = refs
     count = len(blocks)
-    weight_copies = copies([(weights_in.at[i], weights.at[i]) for i in range(4)], sems)
-    row_copies = copies([(block, rows.at[r * 64 : (r + 1) * 64]) for r, block in enumerate(blocks)], sems.at[4:])
-    for copy in weight_copies[:1] + row_copies + weight_copies[1:]:
-        copy.start()
-    for copy in row_copies:
-        copy.wait()
+    for r, block in enumerate(blocks):
+        rows[r * 64 : (r + 1) * 64, :] = block[...]
     moving = []
     for side in range(2):
-        weight_copies[2 * side].wait()
         value = jnp.dot(rows[:, 0:1024], weights[2 * side], preferred_element_type=F32)
-        weight_copies[2 * side + 1].wait()
         value = value + jnp.dot(rows[:, 1024:2048], weights[2 * side + 1], preferred_element_type=F32)
         value = value.astype(BF16)
         for r in range(count):
             result[side, :, r] = value[r * 64 : (r + 1) * 64].reshape(4, 16, HALF)
         copy = pltpu.make_async_copy(
-            result.at[side], out.at[:, :, :, side * HALF : (side + 1) * HALF], sems.at[4 + count + side]
+            result.at[side], out.at[:, :, :, side * HALF : (side + 1) * HALF], sems.at[side]
         )
         copy.start()
         moving.append(copy)
@@ -341,13 +339,13 @@
         shaped((4, count, 16, 1024), BF16),
         scratch=[
             pltpu.VMEM((count * 64, 2048), BF16),
-            pltpu.VMEM((4, 1024, HALF), BF16),
             pltpu.VMEM((2, 4, count, 16, HALF), BF16),
-            pltpu.SemaphoreType.DMA((6 + count,)),
-        ],
-        in_specs=[HBM] * (count + 1),
+            pltpu.SemaphoreType.DMA((2,)),
+        ],
+        in_specs=[VMEM] * (count + 1),
         out_specs=HBM,
-        limit=WIDE,
+        flops=count * 270_000_000,
+        moved=6 << 20,
     )(*blocks, weights)
 
 
@@ -446,14 +444,16 @@
             pltpu.VMEM((CHIP, 512), BF16),
             pltpu.VMEM((CHIP, 128), F32),
             pltpu.VMEM((CHIP, 128), F32),
+            pltpu.VMEM((1, 16), F32),
             pltpu.VMEM((CHIP, HALF), F32),
-            pltpu.SemaphoreType.DMA((4,)),
-        ],
-        in_specs=[HBM] * 4 + [SMEM],
+            pltpu.SemaphoreType.DMA((5,)),
+        ],
+        in_specs=[HBM] * 5,
         out_specs=HBM,
         flops=400_000_000,
         moved=2 << 20,
-    )(x_conv, bc_conv, cum, delta, d_skip)
+        limit=WIDE,
+    )(x_conv, bc_conv, cum, delta, d_skip.reshape(1, 16))
     increments, inside = lax.optimization_barrier((increments, inside))
     first = lax.dynamic_index_in_dim(init_state, core * HEADS + chip, 0, keepdims=False)
     states = call(
@@ -486,9 +486,9 @@
         flops=100_000_000,
         moved=2 << 20,
     )(states.reshape(HEADS * P_SIZE, N), bc_conv, cum, inside, zs, got, gain)
+    cross_got = lax.ppermute(to_cross, ("context", "tensor"), CROSS)
+    next_got = lax.ppermute(to_next, "tensor", BESIDE)
     core_got = lax.ppermute(to_core, "context", PAIR)
-    next_got = lax.ppermute(to_next, "tensor", BESIDE)
-    cross_got = lax.ppermute(to_cross, ("context", "tensor"), CROSS)
     normed = call(
         norm_kernel,
         shaped((64, 2048), BF16),
@@ -497,14 +497,28 @@
         moved=1 << 20,
     )(keep, core_got, next_got, cross_got)
 
+    def staged(weights):
+        return call(
+            stage_kernel,
+            shaped((4, 1024, HALF), BF16),
+            scratch=[pltpu.SemaphoreType.DMA((4,))],
+            in_specs=[HBM],
+            out_specs=VMEM,
+            moved=8 << 20,
+            limit=48 * 1024 * 1024,
+        )(weights)
+
     up, down = [normed], [normed]
     for step in range(4):
+        if step == 1:
+            up[1], weights = lax.optimization_barrier((up[1], weights))
         up.append(lax.ppermute(up[-1], "context", UP))
         if step < 3:
             down.append(lax.ppermute(down[-1], "context", DOWN))
     blocks = {**{r: up[r] for r in range(5)}, **{CHIPS - r: down[r] for r in range(1, 4)}}
-    near = product([blocks[r] for r in NEAR], weights)
-    far = product([blocks[r] for r in FAR], weights)
+    near = product([blocks[r] for r in NEAR], staged(weights))
+    blocks[3], weights = lax.optimization_barrier((blocks[3], weights))
+    far = product([blocks[r] for r in FAR], staged(weights))
     near = lax.psum_scatter(
         near.reshape(4 * 16 * len(NEAR), 1024), "tensor",
         scatter_dimension=0, tiled=True, axis_index_groups=PARITY,

time: 173 us -> 169 us (0.977)
  the two profiles are of different devices: /device:TPU:2 before, /device:TPU:16 now
where the time goes in v3:
time: 169 us; the launch traced here: 168 us
  blocking collectives  48.3 us (29%)
  starting transfers between devices  47.5 us (28%)
  waiting for transfers between devices  33.1 us (20%)
  Pallas kernels  21.8 us (13%)
  between operations  13.4 us (8%)
  local copies, waits for them, and re-layouts  4.14 us (2%)
    all_to_all x1, blocking collectives, body(): lax.all_to_all(ready, 'context', 0, 0, tiled=True, axis_index_groups=SAME...  18.1 us
    all_to_all x1, blocking collectives, body(): lax.all_to_all(far.reshape(4, 16 * len(FAR), 1024), 'tensor', 0, 0, tiled...  15.3 us
    all_to_all x1, starting transfers between devices, body(): lax.all_to_all(added, 'context', 0, 0, tiled=True, axis_index_groups=SAME...  15 us
    all_to_all x1, blocking collectives, body(): lax.all_to_all(states, 'context', 0, 0, tiled=True, axis_index_groups=SAM...  14.9 us
    ppermute x4, waiting for transfers between devices, body(): up.append(lax.ppermute(up[-1], 'context', UP))  12.6 us
    ppermute x3, starting transfers between devices, body(): down.append(lax.ppermute(down[-1], 'context', DOWN))  10.5 us
    ppermute x4, starting transfers between devices, body(): up.append(lax.ppermute(up[-1], 'context', UP))  10.2 us
    all_to_all x1, waiting for transfers between devices, body(): lax.all_to_all(added, 'context', 0, 0, tiled=True, axis_index_groups=SAME...  8.8 us
  transfers between devices with their start and end apart: 17, of which 9 were waited for; matrix products, arithmetic and copies ran while one was open for 1% of the time, Pallas kernels for 11%

profile of v3, /device:TPU:16, one launch (start us, length us, event | category | flops | bytes accessed | tf_op | source)
XLA Modules:
  0.0 168.2 jit_solution(3852755388053050584)
XLA Ops:
  6.5 0.7 all-gather.3.cloned.1.call-update
  7.3 2.5 %shard_map.136 = (bf16[128,1664]{1,0:T(8,128)(2,1)}, bf16[16,1024]{1,0:T(8,128)(2,1)}, bf16[16,1024]{1,0:T(8,128)(2,1)}, bf16[128,512]{1,0:T(8,128)(2,1)}, f32[32,1024]{1,0:T(8,128)}) custom-call(bf16[128,1024]{1,0:T(8,128)(2,1)} %xs.1, bf16[128,1024]{1,0:T(8,128)(2,1)} %zs.3, bf16[128,2,256]{2,1,0:T(2,128)(2,1)} %bcs.1, bf16[16,128]{1,0:T(8,128)(2,1)} %bitcast.23, ...), custom_call_target="tpu_custom_call" | custom-call | bytes 1048576 | tf_op jit(solution)/shard_map/pallas_call | solution.py:376
  9.8 1.9 %collective-permute-start = (bf16[128,1664]{1,0:T(8,128)(2,1)}, bf16[128,1664]{1,0:T(8,128)(2,1)S(1)}, u32[]{:S(2)}, u32[]{:S(2)}) collective-permute-start(bf16[128,1664]{1,0:T(8,128)(2,1)} %get-tuple-element.28.sent_in), channel_id=1, source_target_pairs={{0,8},{8,0},{16,24},{24,16},{32,40},{40,32},{48,56},{56,48},{64,72... | collective-permute-start | bytes 1277960 | tf_op jit(solution)/shard_map/ppermute | solution.py:405
  11.7 0.7 collective-permute-start.1
  12.4 0.7 collective-permute-start.2
  13.1 0.6 collective-permute-done.got_in.got
  13.6 0.0 copy-done.4
  13.7 0.7 copy-done.2
  14.4 5.2 %shard_map.137 = (bf16[8,80,256]{2,1,0:T(8,128)(2,1)}, bf16[256,512]{1,0:T(8,128)(2,1)}, bf16[256,512]{1,0:T(8,128)(2,1)}, f32[256,128]{1,0:T(8,128)}, f32[256,128]{1,0:T(8,128)}) custom-call(bf16[128,512]{1,0:T(8,128)(2,1)} %get-tuple-element.27.xs_in, bf16[128,1664]{1,0:T(8,128)(2,1)} %get-tuple-element.28.sent_in, bf16[128,1664]{1,0:T(8,128)(2,1)} %copy-done.2, ...), custom_call_target="tpu_custom_call" | custom-call | flops 200000000 | bytes 2097152 | tf_op jit(solution)/shard_map/pallas_call | solution.py:408
  19.6 15.0 %all-to-all-start = ((bf16[8,80,256]{2,1,0:T(8,128)(2,1)}), bf16[8,80,256]{2,1,0:T(8,128)(2,1)S(1)}, u32[]{:S(2)}, u32[]{:S(2)}) async-start(bf16[8,80,256]{2,1,0:T(8,128)(2,1)} %get-tuple-element.32), calls=%async_computation | async-start | bytes 655360 | tf_op jit(solution)/shard_map/all_to_all | solution.py:438
  34.6 0.0 all-gather.5.cloned.1.call-start
  34.7 0.8 dynamic-slice_bitcast_fusion.first
  35.6 2.8 %shard_map.138.inside_in = f32[256,512]{1,0:T(8,128)} custom-call(bf16[256,512]{1,0:T(8,128)(2,1)} %get-tuple-element.33.x_in, bf16[256,512]{1,0:T(8,128)(2,1)} %get-tuple-element.34.bc_in, f32[256,128]{1,0:T(8,128)} %get-tuple-element.35.cum_in, f32[256,128]{1,0:T(8,128)} %get-tuple-element.36.delta_in, f32[1,16]{1,0:T(1,128)} %bitcast.27), custom_call_target="tpu_custom_call" | custom-call | flops 400000000 | bytes 2097152 | tf_op jit(solution)/shard_map/pallas_call | solution.py:439
  38.4 8.8 %all-to-all-done.got = bf16[8,80,256]{2,1,0:T(8,128)(2,1)S(1)} async-done(((bf16[8,80,256]{2,1,0:T(8,128)(2,1)}), bf16[8,80,256]{2,1,0:T(8,128)(2,1)S(1)}, u32[]{:S(2)}, u32[]{:S(2)}) %all-to-all-start) | async-done | bytes 327712 | tf_op jit(solution)/shard_map/all_to_all | solution.py:438
  47.2 0.1 shard_map.139
  47.2 14.9 %all_to_all.20 = bf16[8,64,256]{2,1,0:T(8,128)(2,1)} all-to-all(bf16[8,64,256]{2,1,0:T(8,128)(2,1)S(1)} %shard_map.139), channel_id=1, replica_groups={{0,16,32,48,64,80,96,112},{8,24,40,56,72,88,104,120},{1,17,33,49,65,81,..., dimensions={0} | all-to-all | bytes 524288 | tf_op jit(solution)/shard_map/all_to_all | solution.py:465
  62.1 0.0 all-gather.5.cloned.1.call-update
  62.2 0.0 reduce-scatter.2.cloned.1.call-start
  62.2 2.8 %shard_map.140 = (bf16[80,512]{1,0:T(8,128)(2,1)}, bf16[80,512]{1,0:T(8,128)(2,1)}, bf16[80,512]{1,0:T(8,128)(2,1)}, bf16[80,512]{1,0:T(8,128)(2,1)}) custom-call(bf16[512,256]{1,0:T(8,128)(2,1)} %bitcast.21, bf16[256,512]{1,0:T(8,128)(2,1)} %get-tuple-element.34.bc_in, f32[256,128]{1,0:T(8,128)} %get-tuple-element.35.cum_in, ...), custom_call_target="tpu_custom_call" | custom-call | flops 100000000 | bytes 2097152 | tf_op jit(solution)/shard_map/pallas_call | solution.py:470
  65.1 3.2 %collective-permute-start.3 = (bf16[80,512]{1,0:T(8,128)(2,1)}, bf16[80,512]{1,0:T(8,128)(2,1)S(1)}, u32[]{:S(2)}, u32[]{:S(2)}) collective-permute-start(bf16[80,512]{1,0:T(8,128)(2,1)} %get-tuple-element.41), channel_id=1, source_target_pairs={{0,8},{8,0},{16,24},{24,16},{32,40},{40,32},{48,56},{56,48},{64,72... | collective-permute-start | bytes 245768 | tf_op jit(solution)/shard_map/ppermute | solution.py:491
  68.2 3.5 %collective-permute-start.4 = (bf16[80,512]{1,0:T(8,128)(2,1)}, bf16[80,512]{1,0:T(8,128)(2,1)S(1)}, u32[]{:S(2)}, u32[]{:S(2)}) collective-permute-start(bf16[80,512]{1,0:T(8,128)(2,1)} %get-tuple-element.42), channel_id=1, source_target_pairs={{0,1},{1,0},{2,3},{3,2},{4,5},{5,4},{6,7},{7,6},{8,9},{9,8},{10,11... | collective-permute-start | bytes 245768 | tf_op jit(solution)/shard_map/ppermute | solution.py:490
  71.7 1.9 %collective-permute-start.5 = (bf16[80,512]{1,0:T(8,128)(2,1)}, bf16[80,512]{1,0:T(8,128)(2,1)S(1)}, u32[]{:S(2)}, u32[]{:S(2)}) collective-permute-start(bf16[80,512]{1,0:T(8,128)(2,1)} %get-tuple-element.43), channel_id=1, source_target_pairs={{0,9},{1,8},{2,11},{3,10},{4,13},{5,12},{6,15},{7,14},{8,1},{9,0},... | collective-permute-start | bytes 245768 | tf_op jit(solution)/shard_map/ppermute | solution.py:489
  73.7 1.1 collective-permute-done.4.next_got
  74.8 3.7 %collective-permute-done.5.cross_got = bf16[80,512]{1,0:T(8,128)(2,1)S(1)} collective-permute-done((bf16[80,512]{1,0:T(8,128)(2,1)}, bf16[80,512]{1,0:T(8,128)(2,1)S(1)}, u32[]{:S(2)}, u32[]{:S(2)}) %collective-permute-start.5) | collective-permute-done | bytes 81952 | tf_op jit(solution)/shard_map/ppermute | solution.py:489
  78.5 0.9 copy-done.1
  79.4 0.1 shard_map.141.refs_0_
  79.5 1.9 %collective-permute-start.7 = (bf16[64,2048]{1,0:T(8,128)(2,1)S(1)}, bf16[64,2048]{1,0:T(8,128)(2,1)S(1)}, u32[]{:S(2)}, u32[]{:S(2)}) collective-permute-start(bf16[64,2048]{1,0:T(8,128)(2,1)S(1)} %shard_map.141.refs_0_), channel_id=1, source_target_pairs={{0,112},{8,120},{16,0},{24,8},{32,16},{40,24},{48,32},{56,40},{64,... | collective-permute-start | bytes 786440 | tf_op jit(solution)/shard_map/ppermute | solution.py:517
  81.4 3.9 %collective-permute-start.6 = (bf16[64,2048]{1,0:T(8,128)(2,1)S(1)}, bf16[64,2048]{1,0:T(8,128)(2,1)S(1)}, u32[]{:S(2)}, u32[]{:S(2)}) collective-permute-start(bf16[64,2048]{1,0:T(8,128)(2,1)S(1)} %shard_map.141.refs_0_), channel_id=1, source_target_pairs={{0,16},{8,24},{16,32},{24,40},{32,48},{40,56},{48,64},{56,72},{64,... | collective-permute-start | bytes 786440 | tf_op jit(solution)/shard_map/ppermute | solution.py:515
  85.4 4.3 %collective-permute-done.7.refs_2_ = bf16[64,2048]{1,0:T(8,128)(2,1)S(1)} collective-permute-done((bf16[64,2048]{1,0:T(8,128)(2,1)S(1)}, bf16[64,2048]{1,0:T(8,128)(2,1)S(1)}, u32[]{:S(2)}, u32[]{:S(2)}) %collective-permute-start.7) | collective-permute-done | bytes 262176 | tf_op jit(solution)/shard_map/ppermute | solution.py:517
  89.7 3.4 %collective-permute-start.9 = (bf16[64,2048]{1,0:T(8,128)(2,1)S(1)}, bf16[64,2048]{1,0:T(8,128)(2,1)S(1)}, u32[]{:S(2)}, u32[]{:S(2)}) collective-permute-start(bf16[64,2048]{1,0:T(8,128)(2,1)S(1)} %collective-permute-done.7.refs_2_), channel_id=1, source_target_pairs={{0,112},{8,120},{16,0},{24,8},{32,16},{40,24},{48,32},{56,40},{64,... | collective-permute-start | bytes 786440 | tf_op jit(solution)/shard_map/ppermute | solution.py:517
  93.1 0.0 all-gather.5.cloned.1.call-done
  93.1 2.4 %collective-permute-start.8 = (bf16[64,2048]{1,0:T(8,128)(2,1)S(1)}, bf16[64,2048]{1,0:T(8,128)(2,1)S(1)}, u32[]{:S(2)}, u32[]{:S(2)}) collective-permute-start(bf16[64,2048]{1,0:T(8,128)(2,1)S(1)} %collective-permute-done.6.refs_1_), channel_id=1, source_target_pairs={{0,16},{8,24},{16,32},{24,40},{32,48},{40,56},{48,64},{56,72},{64,... | collective-permute-start | bytes 786440 | tf_op jit(solution)/shard_map/ppermute | solution.py:515
  95.6 2.2 %shard_map.142.refs_5_ = bf16[4,1024,512]{2,1,0:T(8,128)(2,1)S(1)} custom-call(bf16[4,1024,512]{2,1,0:T(8,128)(2,1)} %bitcast.19), custom_call_target="tpu_custom_call" | custom-call | bytes 8388608 | tf_op jit(solution)/shard_map/pallas_call | solution.py:501
  97.8 1.2 collective-permute-done.9.refs_4_
  99.0 4.7 %collective-permute-done.8.refs_3_ = bf16[64,2048]{1,0:T(8,128)(2,1)S(1)} collective-permute-done((bf16[64,2048]{1,0:T(8,128)(2,1)S(1)}, bf16[64,2048]{1,0:T(8,128)(2,1)S(1)}, u32[]{:S(2)}, u32[]{:S(2)}) %collective-permute-start.8) | collective-permute-done | bytes 262176 | tf_op jit(solution)/shard_map/ppermute | solution.py:515
  103.7 2.3 %shard_map.143 = bf16[4,5,16,1024]{3,2,1,0:T(8,128)(2,1)} custom-call(bf16[64,2048]{1,0:T(8,128)(2,1)S(1)} %shard_map.141.refs_0_, bf16[64,2048]{1,0:T(8,128)(2,1)S(1)} %collective-permute-done.6.refs_1_, bf16[64,2048]{1,0:T(8,128)(2,1)S(1)} %collective-permute-done.7.refs_2_, bf16[64,2048]{1,0:T(8,128)(2,1)S(1)} %collective-permute-done.8.refs_3_, ...), custom_call_target="tpu_custom_call" | custom-call | flops 1350000000 | bytes 6291456 | tf_op jit(solution)/shard_map/pallas_call | solution.py:337
  106.0 1.9 %collective-permute-start.10 = (bf16[64,2048]{1,0:T(8,128)(2,1)S(1)}, bf16[64,2048]{1,0:T(8,128)(2,1)S(1)}, u32[]{:S(2)}, u32[]{:S(2)}) collective-permute-start(bf16[64,2048]{1,0:T(8,128)(2,1)S(1)} %collective-permute-done.8.refs_3_), channel_id=1, source_target_pairs={{0,16},{8,24},{16,32},{24,40},{32,48},{40,56},{48,64},{56,72},{64,... | collective-permute-start | bytes 786440 | tf_op jit(solution)/shard_map/ppermute | solution.py:515
  108.0 5.1 %collective-permute-start.11 = (bf16[64,2048]{1,0:T(8,128)(2,1)S(1)}, bf16[64,2048]{1,0:T(8,128)(2,1)S(1)}, u32[]{:S(2)}, u32[]{:S(2)}) collective-permute-start(bf16[64,2048]{1,0:T(8,128)(2,1)S(1)} %collective-permute-done.9.refs_4_), channel_id=1, source_target_pairs={{0,112},{8,120},{16,0},{24,8},{32,16},{40,24},{48,32},{56,40},{64,... | collective-permute-start | bytes 786440 | tf_op jit(solution)/shard_map/ppermute | solution.py:517
  113.1 2.6 %collective-permute-done.10.refs_0_ = bf16[64,2048]{1,0:T(8,128)(2,1)S(1)} collective-permute-done((bf16[64,2048]{1,0:T(8,128)(2,1)S(1)}, bf16[64,2048]{1,0:T(8,128)(2,1)S(1)}, u32[]{:S(2)}, u32[]{:S(2)}) %collective-permute-start.10) | collective-permute-done | bytes 262176 | tf_op jit(solution)/shard_map/ppermute | solution.py:515
  115.7 1.9 %collective-permute-start.12 = (bf16[64,2048]{1,0:T(8,128)(2,1)S(1)}, bf16[64,2048]{1,0:T(8,128)(2,1)S(1)}, u32[]{:S(2)}, u32[]{:S(2)}) collective-permute-start(bf16[64,2048]{1,0:T(8,128)(2,1)S(1)} %collective-permute-done.10.refs_0_), channel_id=1, source_target_pairs={{0,16},{8,24},{16,32},{24,40},{32,48},{40,56},{48,64},{56,72},{64,... | collective-permute-start | bytes 786440 | tf_op jit(solution)/shard_map/ppermute | solution.py:515
  117.6 2.2 %shard_map.144.refs_3_ = bf16[4,1024,512]{2,1,0:T(8,128)(2,1)S(1)} custom-call(bf16[4,1024,512]{2,1,0:T(8,128)(2,1)} %bitcast.20), custom_call_target="tpu_custom_call" | custom-call | bytes 8388608 | tf_op jit(solution)/shard_map/pallas_call | solution.py:501
  119.8 5.3 %collective-permute-done.12.refs_2_ = bf16[64,2048]{1,0:T(8,128)(2,1)S(1)} collective-permute-done((bf16[64,2048]{1,0:T(8,128)(2,1)S(1)}, bf16[64,2048]{1,0:T(8,128)(2,1)S(1)}, u32[]{:S(2)}, u32[]{:S(2)}) %collective-permute-start.12) | collective-permute-done | bytes 262176 | tf_op jit(solution)/shard_map/ppermute | solution.py:515
  125.1 1.2 shard_map.145
  126.4 15.3 %all_to_all.21 = bf16[4,48,1024]{2,1,0:T(8,128)(2,1)S(1)} all-to-all(bf16[4,48,1024]{2,1,0:T(8,128)(2,1)S(1)} %bitcast.17), channel_id=1, replica_groups={{0,2,4,6},{1,3,5,7},{8,10,12,14},{9,11,13,15},{16,18,20,22},{17,19,21,2..., dimensions={0} | all-to-all | bytes 786432 | tf_op jit(solution)/shard_map/all_to_all | solution.py:526
  141.7 0.9 copy-done
  142.6 0.3 shard_map.146
  142.8 18.1 %all_to_all.22 = bf16[8,16,1024]{2,1,0:T(8,128)(2,1)S(1)} all-to-all(bf16[8,16,1024]{2,1,0:T(8,128)(2,1)S(1)} %shard_map.146), channel_id=1, replica_groups={{0,16,32,48,64,80,96,112},{8,24,40,56,72,88,104,120},{1,17,33,49,65,81,..., dimensions={0} | all-to-all | bytes 524288 | tf_op jit(solution)/shard_map/all_to_all | solution.py:536
  160.9 0.7 copy.16
  (15 shorter events, 0.0 us)
Async XLA Ops:
  6.5 55.6 %all-gather.3.cloned.1.call-start = ((), (), s32[]{:S(2)}) async-start(), calls=%async_computation.5 | async-start | bytes 3145728 | tf_op jit(solution)/shard_map/all_gather | solution.py:375
  9.8 3.9 %collective-permute-start = (bf16[128,1664]{1,0:T(8,128)(2,1)}, bf16[128,1664]{1,0:T(8,128)(2,1)S(1)}, u32[]{:S(2)}, u32[]{:S(2)}) collective-permute-start(bf16[128,1664]{1,0:T(8,128)(2,1)} %get-tuple-element.28.sent_in), channel_id=1, source_target_pairs={{0,8},{8,0},{16,24},{24,16},{32,40},{40,32},{48,56},{56,48},{64,72... | collective-permute-start | bytes 1277960 | tf_op jit(solution)/shard_map/ppermute | solution.py:405
  11.7 1.3 collective-permute-start.1
  12.4 0.7 collective-permute-start.2
  13.0 0.6 copy-start.3
  13.1 0.6 copy-start.4
  13.6 0.8 copy-start.2
  19.6 27.5 %all-to-all-start = ((bf16[8,80,256]{2,1,0:T(8,128)(2,1)}), bf16[8,80,256]{2,1,0:T(8,128)(2,1)S(1)}, u32[]{:S(2)}, u32[]{:S(2)}) async-start(bf16[8,80,256]{2,1,0:T(8,128)(2,1)} %get-tuple-element.32), calls=%async_computation | async-start | bytes 655360 | tf_op jit(solution)/shard_map/all_to_all | solution.py:438
  34.6 58.5 %all-gather.5.cloned.1.call-start = ((), (), s32[]{:S(2)}) async-start(), calls=%async_computation.6 | async-start | bytes 6291456 | tf_op jit(solution)/shard_map/all_gather | solution.py:467
  62.2 79.5 %reduce-scatter.2.cloned.1.call-start = ((), (), s32[]{:S(2)}) async-start(), calls=%async_computation.7 | async-start | bytes 819200 | tf_op jit(solution)/shard_map/reduce_scatter | solution.py:522
  65.1 8.6 %collective-permute-start.3 = (bf16[80,512]{1,0:T(8,128)(2,1)}, bf16[80,512]{1,0:T(8,128)(2,1)S(1)}, u32[]{:S(2)}, u32[]{:S(2)}) collective-permute-start(bf16[80,512]{1,0:T(8,128)(2,1)} %get-tuple-element.41), channel_id=1, source_target_pairs={{0,8},{8,0},{16,24},{24,16},{32,40},{40,32},{48,56},{56,48},{64,72... | collective-permute-start | bytes 245768 | tf_op jit(solution)/shard_map/ppermute | solution.py:491
  68.2 6.5 %collective-permute-start.4 = (bf16[80,512]{1,0:T(8,128)(2,1)}, bf16[80,512]{1,0:T(8,128)(2,1)S(1)}, u32[]{:S(2)}, u32[]{:S(2)}) collective-permute-start(bf16[80,512]{1,0:T(8,128)(2,1)} %get-tuple-element.42), channel_id=1, source_target_pairs={{0,1},{1,0},{2,3},{3,2},{4,5},{5,4},{6,7},{7,6},{8,9},{9,8},{10,11... | collective-permute-start | bytes 245768 | tf_op jit(solution)/shard_map/ppermute | solution.py:490
  71.7 6.8 %collective-permute-start.5 = (bf16[80,512]{1,0:T(8,128)(2,1)}, bf16[80,512]{1,0:T(8,128)(2,1)S(1)}, u32[]{:S(2)}, u32[]{:S(2)}) collective-permute-start(bf16[80,512]{1,0:T(8,128)(2,1)} %get-tuple-element.43), channel_id=1, source_target_pairs={{0,9},{1,8},{2,11},{3,10},{4,13},{5,12},{6,15},{7,14},{8,1},{9,0},... | collective-permute-start | bytes 245768 | tf_op jit(solution)/shard_map/ppermute | solution.py:489
  78.5 0.9 copy-start.1
  79.5 10.2 %collective-permute-start.7 = (bf16[64,2048]{1,0:T(8,128)(2,1)S(1)}, bf16[64,2048]{1,0:T(8,128)(2,1)S(1)}, u32[]{:S(2)}, u32[]{:S(2)}) collective-permute-start(bf16[64,2048]{1,0:T(8,128)(2,1)S(1)} %shard_map.141.refs_0_), channel_id=1, source_target_pairs={{0,112},{8,120},{16,0},{24,8},{32,16},{40,24},{48,32},{56,40},{64,... | collective-permute-start | bytes 786440 | tf_op jit(solution)/shard_map/ppermute | solution.py:517
  81.4 11.6 %collective-permute-start.6 = (bf16[64,2048]{1,0:T(8,128)(2,1)S(1)}, bf16[64,2048]{1,0:T(8,128)(2,1)S(1)}, u32[]{:S(2)}, u32[]{:S(2)}) collective-permute-start(bf16[64,2048]{1,0:T(8,128)(2,1)S(1)} %shard_map.141.refs_0_), channel_id=1, source_target_pairs={{0,16},{8,24},{16,32},{24,40},{32,48},{40,56},{48,64},{56,72},{64,... | collective-permute-start | bytes 786440 | tf_op jit(solution)/shard_map/ppermute | solution.py:515
  89.7 9.3 %collective-permute-start.9 = (bf16[64,2048]{1,0:T(8,128)(2,1)S(1)}, bf16[64,2048]{1,0:T(8,128)(2,1)S(1)}, u32[]{:S(2)}, u32[]{:S(2)}) collective-permute-start(bf16[64,2048]{1,0:T(8,128)(2,1)S(1)} %collective-permute-done.7.refs_2_), channel_id=1, source_target_pairs={{0,112},{8,120},{16,0},{24,8},{32,16},{40,24},{48,32},{56,40},{64,... | collective-permute-start | bytes 786440 | tf_op jit(solution)/shard_map/ppermute | solution.py:517
  93.1 10.6 %collective-permute-start.8 = (bf16[64,2048]{1,0:T(8,128)(2,1)S(1)}, bf16[64,2048]{1,0:T(8,128)(2,1)S(1)}, u32[]{:S(2)}, u32[]{:S(2)}) collective-permute-start(bf16[64,2048]{1,0:T(8,128)(2,1)S(1)} %collective-permute-done.6.refs_1_), channel_id=1, source_target_pairs={{0,16},{8,24},{16,32},{24,40},{32,48},{40,56},{48,64},{56,72},{64,... | collective-permute-start | bytes 786440 | tf_op jit(solution)/shard_map/ppermute | solution.py:515
  106.0 9.7 %collective-permute-start.10 = (bf16[64,2048]{1,0:T(8,128)(2,1)S(1)}, bf16[64,2048]{1,0:T(8,128)(2,1)S(1)}, u32[]{:S(2)}, u32[]{:S(2)}) collective-permute-start(bf16[64,2048]{1,0:T(8,128)(2,1)S(1)} %collective-permute-done.8.refs_3_), channel_id=1, source_target_pairs={{0,16},{8,24},{16,32},{24,40},{32,48},{40,56},{48,64},{56,72},{64,... | collective-permute-start | bytes 786440 | tf_op jit(solution)/shard_map/ppermute | solution.py:515
  108.0 11.9 %collective-permute-start.11 = (bf16[64,2048]{1,0:T(8,128)(2,1)S(1)}, bf16[64,2048]{1,0:T(8,128)(2,1)S(1)}, u32[]{:S(2)}, u32[]{:S(2)}) collective-permute-start(bf16[64,2048]{1,0:T(8,128)(2,1)S(1)} %collective-permute-done.9.refs_4_), channel_id=1, source_target_pairs={{0,112},{8,120},{16,0},{24,8},{32,16},{40,24},{48,32},{56,40},{64,... | collective-permute-start | bytes 786440 | tf_op jit(solution)/shard_map/ppermute | solution.py:517
  115.7 9.5 %collective-permute-start.12 = (bf16[64,2048]{1,0:T(8,128)(2,1)S(1)}, bf16[64,2048]{1,0:T(8,128)(2,1)S(1)}, u32[]{:S(2)}, u32[]{:S(2)}) collective-permute-start(bf16[64,2048]{1,0:T(8,128)(2,1)S(1)} %collective-permute-done.10.refs_0_), channel_id=1, source_target_pairs={{0,16},{8,24},{16,32},{24,40},{32,48},{40,56},{48,64},{56,72},{64,... | collective-permute-start | bytes 786440 | tf_op jit(solution)/shard_map/ppermute | solution.py:515
  141.7 0.9 copy-start
Sparse Core Ops, SparseCore 0:
  9.4 45.4 all-gather.2
  62.3 19.1 all-gather.4
  106.1 27.9 reduce-scatter.1

commit v4 on v3

--- a/solution.py
+++ b/solution.py
@@ -216,9 +216,26 @@
         copy.wait()
 
 
-def inside_kernel(x_in, bc_in, cum_in, delta_in, skip_in, out, x, bc, cum, delta, skip, total, sems):
+def inside_kernel(
+    x_in, bc_in, cum_in, delta_in, skip_in, zs, got,
+    out, scale_out, x, bc, cum, delta, skip, gate, total, scales, sems,
+):
     core, _ = place()
-    fetch([(x_in, x), (bc_in, bc), (cum_in, cum), (delta_in, delta), (skip_in, skip)], sems)
+    fetch(
+        [
+            (x_in, x),
+            (bc_in, bc),
+            (cum_in, cum),
+            (delta_in, delta),
+            (skip_in, skip),
+            (zs.at[:, lanes(core)], gate.at[tokens(core), :]),
+            (got.at[:, 1152:1664], gate.at[tokens(1 - core), :]),
+        ],
+        sems,
+    )
+    decays = jnp.dot(jnp.exp(cum[...]), spread(), precision=EXACT, preferred_element_type=F32)
+    gates = silu(gate[...].astype(F32))
+    scales[...] = decays * gates
     scores = lax.dot_general(
         bc[:, N : 2 * N], bc[:, 0:N], (((1,), (1,)), ((), ())), preferred_element_type=F32
     )
@@ -235,11 +252,11 @@
         for h in (2 * pair, 2 * pair + 1):
             decay = jnp.exp(jnp.minimum(cum[:, h : h + 1] - cum_t[h : h + 1, :], 0.0))
             weights = (decay * scores * delta_t[h : h + 1, :]).astype(BF16)
-            scale = jnp.where(core == 0, skip[:, h : h + 1], skip[:, HEADS + h : HEADS + h + 1])
-            through = scale * values.astype(F32)
+            skips = jnp.where(core == 0, skip[:, h : h + 1], skip[:, HEADS + h : HEADS + h + 1])
+            through = skips * values.astype(F32)
             both.append(jnp.dot(weights, values, preferred_element_type=F32) + through)
-        total[:, cut] = jnp.where(lane < P_SIZE, both[0], both[1])
-    fetch([(total, out)], sems)
+        total[:, cut] = jnp.where(lane < P_SIZE, both[0], both[1]) * gates[:, cut]
+    fetch([(total, out), (scales, scale_out)], sems)
 
 
 def prefix_kernel(got, first, out):
@@ -253,18 +270,16 @@
 
 
 def carry_kernel(
-    state_in, bc_in, cum_in, inside_in, zs, got, gain_in,
-    keep, to_core, to_next, to_cross, state, c, cum, inside, gate, gain, pieces, sems,
+    state_in, bc_in, inside_in, scale_in, gain_in,
+    keep, to_core, to_next, to_cross, state, c, inside, scale, gain, pieces, sems,
 ):
     core, _ = place()
     fetch(
         [
             (bc_in.at[:, N : 2 * N], c),
-            (cum_in, cum),
+            (state_in, state),
             (inside_in, inside),
-            (zs.at[:, lanes(core)], gate.at[tokens(core), :]),
-            (got.at[:, 1152:1664], gate.at[tokens(1 - core), :]),
-            (state_in, state),
+            (scale_in, scale),
             (gain_in, gain),
         ],
         sems,
@@ -272,8 +287,7 @@
     carried = lax.dot_general(
         c[...], state[...], (((1,), (1,)), ((), ())), preferred_element_type=F32
     )
-    decay = jnp.dot(jnp.exp(cum[...]), spread(), precision=EXACT, preferred_element_type=F32)
-    gated = (inside[...] + carried * decay) * silu(gate[...].astype(F32))
+    gated = inside[...] + carried * scale[...]
     pieces[...] = gated.astype(BF16).reshape(2, 4, 2, 16, HALF)
 
     def piece(side, parity):
@@ -293,7 +307,7 @@
         out[64:80, :] = terms.astype(BF16)
 
 
-def norm_kernel(keep, core_got, next_got, cross_got, out):
+def norm_kernel(cross_got, next_got, core_got, keep, out):
     core, _ = place()
     odd = lax.rem(lax.axis_index("tensor"), 2)
     for mine, came, position in ((keep, core_got, odd), (next_got, cross_got, 1 - odd)):
@@ -436,24 +450,26 @@
         moved=2 << 20,
     )(mine, sent, got, halo_0, halo_1, fixed)
     increments = lax.all_to_all(added, "context", 0, 0, tiled=True, axis_index_groups=SAME_CORE)
-    inside = call(
+    inside, scale = call(
         inside_kernel,
-        shaped((CHIP, HALF), F32),
+        (shaped((CHIP, HALF), F32), shaped((CHIP, HALF), F32)),
         scratch=[
             pltpu.VMEM((CHIP, HALF), BF16),
             pltpu.VMEM((CHIP, 512), BF16),
             pltpu.VMEM((CHIP, 128), F32),
             pltpu.VMEM((CHIP, 128), F32),
             pltpu.VMEM((1, 16), F32),
+            pltpu.VMEM((CHIP, HALF), BF16),
             pltpu.VMEM((CHIP, HALF), F32),
-            pltpu.SemaphoreType.DMA((5,)),
-        ],
-        in_specs=[HBM] * 5,
-        out_specs=HBM,
+            pltpu.VMEM((CHIP, HALF), F32),
+            pltpu.SemaphoreType.DMA((7,)),
+        ],
+        in_specs=[HBM] * 7,
+        out_specs=[HBM] * 2,
         flops=400_000_000,
         moved=2 << 20,
         limit=WIDE,
-    )(x_conv, bc_conv, cum, delta, d_skip.reshape(1, 16))
+    )(x_conv, bc_conv, cum, delta, d_skip.reshape(1, 16), zs, got)
     increments, inside = lax.optimization_barrier((increments, inside))
     first = lax.dynamic_index_in_dim(init_state, core * HEADS + chip, 0, keepdims=False)
     states = call(
@@ -473,19 +489,18 @@
         scratch=[
             pltpu.VMEM((HEADS * P_SIZE, N), BF16),
             pltpu.VMEM((CHIP, N), BF16),
-            pltpu.VMEM((CHIP, 128), F32),
             pltpu.VMEM((CHIP, HALF), F32),
-            pltpu.VMEM((CHIP, HALF), BF16),
+            pltpu.VMEM((CHIP, HALF), F32),
             pltpu.VMEM((1, 1024), F32),
             pltpu.VMEM((2, 4, 2, 16, HALF), BF16),
-            pltpu.SemaphoreType.DMA((7,)),
-        ],
-        in_specs=[HBM] * 7,
+            pltpu.SemaphoreType.DMA((5,)),
+        ],
+        in_specs=[HBM] * 5,
         out_specs=[VMEM] * 4,
         limit=WIDE,
         flops=100_000_000,
         moved=2 << 20,
-    )(states.reshape(HEADS * P_SIZE, N), bc_conv, cum, inside, zs, got, gain)
+    )(states.reshape(HEADS * P_SIZE, N), bc_conv, inside, scale, gain)
     cross_got = lax.ppermute(to_cross, ("context", "tensor"), CROSS)
     next_got = lax.ppermute(to_next, "tensor", BESIDE)
     core_got = lax.ppermute(to_core, "context", PAIR)
@@ -495,7 +510,7 @@
         in_specs=[VMEM] * 4,
         out_specs=VMEM,
         moved=1 << 20,
-    )(keep, core_got, next_got, cross_got)
+    )(cross_got, next_got, core_got, keep)
 
     def staged(weights):
         return call(

time: 169 us -> 166 us (0.982)
  waiting for transfers between devices: 33.1 us -> 28.2 us
  blocking collectives: 48.3 us -> 50.1 us
    ppermute x1, waiting for transfers between devices: 3.7 us -> 0.01 us  [body(): cross_got = lax.ppermute(to_cross, ('context', 'tensor'), CROSS)]
    all_to_all x1, blocking collectives: 15.3 us -> 18 us  [body(): lax.all_to_all(far.reshape(4, 16 * len(FAR), 1024), 'tensor', 0, 0, tiled...]
    ppermute x1, starting transfers between devices: 1.92 us -> 4.37 us  [body(): cross_got = lax.ppermute(to_cross, ('context', 'tensor'), CROSS)]
  transfers between devices with their start and end apart: 17 -> 17, of which waited for: 9 -> 8; matrix products, arithmetic and copies ran while one was open for 1% -> 1% of each run, Pallas kernels for 11% -> 12%
where the time goes in v4:
time: 166 us; the launch traced here: 165 us
  blocking collectives  50.1 us (30%)
  starting transfers between devices  47.6 us (29%)
  waiting for transfers between devices  28.2 us (17%)
  Pallas kernels  22 us (13%)
  between operations  13.4 us (8%)
  local copies, waits for them, and re-layouts  4.17 us (3%)
    all_to_all x1, blocking collectives, body(): lax.all_to_all(far.reshape(4, 16 * len(FAR), 1024), 'tensor', 0, 0, tiled...  18 us
    all_to_all x1, blocking collectives, body(): lax.all_to_all(ready, 'context', 0, 0, tiled=True, axis_index_groups=SAME...  17.2 us
    all_to_all x1, starting transfers between devices, body(): lax.all_to_all(added, 'context', 0, 0, tiled=True, axis_index_groups=SAME...  15 us
    all_to_all x1, blocking collectives, body(): lax.all_to_all(states, 'context', 0, 0, tiled=True, axis_index_groups=SAM...  14.9 us
    ppermute x4, waiting for transfers between devices, body(): up.append(lax.ppermute(up[-1], 'context', UP))  12.3 us
    ppermute x3, starting transfers between devices, body(): down.append(lax.ppermute(down[-1], 'context', DOWN))  10.5 us
    ppermute x4, starting transfers between devices, body(): up.append(lax.ppermute(up[-1], 'context', UP))  10.2 us
    all_to_all x1, waiting for transfers between devices, body(): lax.all_to_all(added, 'context', 0, 0, tiled=True, axis_index_groups=SAME...  8.28 us
  transfers between devices with their start and end apart: 17, of which 8 were waited for; matrix products, arithmetic and copies ran while one was open for 1% of the time, Pallas kernels for 12%

profile of v4, /device:TPU:16, one launch (start us, length us, event | category | flops | bytes accessed | tf_op | source)
XLA Modules:
  0.0 165.4 jit_solution(2847417788906566460)
XLA Ops:
  6.5 0.7 all-gather.3.cloned.1.call-update
  7.3 2.5 %shard_map.136 = (bf16[128,1664]{1,0:T(8,128)(2,1)}, bf16[16,1024]{1,0:T(8,128)(2,1)}, bf16[16,1024]{1,0:T(8,128)(2,1)}, bf16[128,512]{1,0:T(8,128)(2,1)}, f32[32,1024]{1,0:T(8,128)}) custom-call(bf16[128,1024]{1,0:T(8,128)(2,1)} %xs.1, bf16[128,1024]{1,0:T(8,128)(2,1)} %zs.3, bf16[128,2,256]{2,1,0:T(2,128)(2,1)} %bcs.1, bf16[16,128]{1,0:T(8,128)(2,1)} %bitcast.23, ...), custom_call_target="tpu_custom_call" | custom-call | bytes 1048576 | tf_op jit(solution)/shard_map/pallas_call | solution.py:390
  9.8 1.9 %collective-permute-start = (bf16[128,1664]{1,0:T(8,128)(2,1)}, bf16[128,1664]{1,0:T(8,128)(2,1)S(1)}, u32[]{:S(2)}, u32[]{:S(2)}) collective-permute-start(bf16[128,1664]{1,0:T(8,128)(2,1)} %get-tuple-element.30.sent_in), channel_id=1, source_target_pairs={{0,8},{8,0},{16,24},{24,16},{32,40},{40,32},{48,56},{56,48},{64,72... | collective-permute-start | bytes 1277960 | tf_op jit(solution)/shard_map/ppermute | solution.py:419
  11.7 0.7 collective-permute-start.1
  12.4 0.7 collective-permute-start.2
  13.1 0.6 collective-permute-done.got_in.got
  13.6 0.0 copy-done.3
  13.7 0.7 copy-done.2
  14.4 5.2 %shard_map.137 = (bf16[8,80,256]{2,1,0:T(8,128)(2,1)}, bf16[256,512]{1,0:T(8,128)(2,1)}, bf16[256,512]{1,0:T(8,128)(2,1)}, f32[256,128]{1,0:T(8,128)}, f32[256,128]{1,0:T(8,128)}) custom-call(bf16[128,512]{1,0:T(8,128)(2,1)} %get-tuple-element.29.xs_in, bf16[128,1664]{1,0:T(8,128)(2,1)} %get-tuple-element.30.sent_in, bf16[128,1664]{1,0:T(8,128)(2,1)} %copy-done.2, ...), custom_call_target="tpu_custom_call" | custom-call | flops 200000000 | bytes 2097152 | tf_op jit(solution)/shard_map/pallas_call | solution.py:422
  19.7 15.0 %all-to-all-start = ((bf16[8,80,256]{2,1,0:T(8,128)(2,1)}), bf16[8,80,256]{2,1,0:T(8,128)(2,1)S(1)}, u32[]{:S(2)}, u32[]{:S(2)}) async-start(bf16[8,80,256]{2,1,0:T(8,128)(2,1)} %get-tuple-element.34), calls=%async_computation | async-start | bytes 655360 | tf_op jit(solution)/shard_map/all_to_all | solution.py:452
  34.7 0.0 all-gather.5.cloned.1.call-start
  34.7 0.8 dynamic-slice_bitcast_fusion.first
  35.6 3.3 %shard_map.138 = (f32[256,512]{1,0:T(8,128)}, f32[256,512]{1,0:T(8,128)}) custom-call(bf16[256,512]{1,0:T(8,128)(2,1)} %get-tuple-element.35.x_in, bf16[256,512]{1,0:T(8,128)(2,1)} %get-tuple-element.36.bc_in, f32[256,128]{1,0:T(8,128)} %get-tuple-element.37.cum_in, f32[256,128]{1,0:T(8,128)} %get-tuple-element.38.delta_in, f32[1,16]{1,0:T(1,128)} %bitcast.27, ...), custom_call_target="tpu_custom_call" | custom-call | flops 400000000 | bytes 2097152 | tf_op jit(solution)/shard_map/pallas_call | solution.py:453
  38.9 8.3 %all-to-all-done.got = bf16[8,80,256]{2,1,0:T(8,128)(2,1)S(1)} async-done(((bf16[8,80,256]{2,1,0:T(8,128)(2,1)}), bf16[8,80,256]{2,1,0:T(8,128)(2,1)S(1)}, u32[]{:S(2)}, u32[]{:S(2)}) %all-to-all-start) | async-done | bytes 327712 | tf_op jit(solution)/shard_map/all_to_all | solution.py:452
  47.2 0.1 shard_map.139
  47.3 14.9 %all_to_all.20 = bf16[8,64,256]{2,1,0:T(8,128)(2,1)} all-to-all(bf16[8,64,256]{2,1,0:T(8,128)(2,1)S(1)} %shard_map.139), channel_id=1, replica_groups={{0,16,32,48,64,80,96,112},{8,24,40,56,72,88,104,120},{1,17,33,49,65,81,..., dimensions={0} | all-to-all | bytes 524288 | tf_op jit(solution)/shard_map/all_to_all | solution.py:481
  62.2 0.0 all-gather.5.cloned.1.call-update
  62.2 0.0 reduce-scatter.2.cloned.1.call-start
  62.2 2.4 %shard_map.140 = (bf16[80,512]{1,0:T(8,128)(2,1)}, bf16[80,512]{1,0:T(8,128)(2,1)}, bf16[80,512]{1,0:T(8,128)(2,1)}, bf16[80,512]{1,0:T(8,128)(2,1)}) custom-call(bf16[512,256]{1,0:T(8,128)(2,1)} %bitcast.22, bf16[256,512]{1,0:T(8,128)(2,1)} %get-tuple-element.36.bc_in, f32[256,512]{1,0:T(8,128)} %get-tuple-element.42.inside_in, ...), custom_call_target="tpu_custom_call" | custom-call | flops 100000000 | bytes 2097152 | tf_op jit(solution)/shard_map/pallas_call | solution.py:486
  64.6 4.4 %collective-permute-start.3 = (bf16[80,512]{1,0:T(8,128)(2,1)}, bf16[80,512]{1,0:T(8,128)(2,1)S(1)}, u32[]{:S(2)}, u32[]{:S(2)}) collective-permute-start(bf16[80,512]{1,0:T(8,128)(2,1)} %get-tuple-element.44), channel_id=1, source_target_pairs={{0,9},{1,8},{2,11},{3,10},{4,13},{5,12},{6,15},{7,14},{8,1},{9,0},... | collective-permute-start | bytes 245768 | tf_op jit(solution)/shard_map/ppermute | solution.py:504
  69.0 2.4 %collective-permute-start.4 = (bf16[80,512]{1,0:T(8,128)(2,1)}, bf16[80,512]{1,0:T(8,128)(2,1)S(1)}, u32[]{:S(2)}, u32[]{:S(2)}) collective-permute-start(bf16[80,512]{1,0:T(8,128)(2,1)} %get-tuple-element.45), channel_id=1, source_target_pairs={{0,1},{1,0},{2,3},{3,2},{4,5},{5,4},{6,7},{7,6},{8,9},{9,8},{10,11... | collective-permute-start | bytes 245768 | tf_op jit(solution)/shard_map/ppermute | solution.py:505
  71.4 1.9 %collective-permute-start.5 = (bf16[80,512]{1,0:T(8,128)(2,1)}, bf16[80,512]{1,0:T(8,128)(2,1)S(1)}, u32[]{:S(2)}, u32[]{:S(2)}) collective-permute-start(bf16[80,512]{1,0:T(8,128)(2,1)} %get-tuple-element.46), channel_id=1, source_target_pairs={{0,8},{8,0},{16,24},{24,16},{32,40},{40,32},{48,56},{56,48},{64,72... | collective-permute-start | bytes 245768 | tf_op jit(solution)/shard_map/ppermute | solution.py:506
  73.3 2.2 %collective-permute-done.4.next_got = bf16[80,512]{1,0:T(8,128)(2,1)S(1)} collective-permute-done((bf16[80,512]{1,0:T(8,128)(2,1)}, bf16[80,512]{1,0:T(8,128)(2,1)S(1)}, u32[]{:S(2)}, u32[]{:S(2)}) %collective-permute-start.4) | collective-permute-done | bytes 81952 | tf_op jit(solution)/shard_map/ppermute | solution.py:505
  75.5 0.9 copy-done.1
  76.4 0.1 shard_map.141.refs_0_
  76.6 1.9 %collective-permute-start.7 = (bf16[64,2048]{1,0:T(8,128)(2,1)S(1)}, bf16[64,2048]{1,0:T(8,128)(2,1)S(1)}, u32[]{:S(2)}, u32[]{:S(2)}) collective-permute-start(bf16[64,2048]{1,0:T(8,128)(2,1)S(1)} %shard_map.141.refs_0_), channel_id=1, source_target_pairs={{0,112},{8,120},{16,0},{24,8},{32,16},{40,24},{48,32},{56,40},{64,... | collective-permute-start | bytes 786440 | tf_op jit(solution)/shard_map/ppermute | solution.py:532
  78.5 3.9 %collective-permute-start.6 = (bf16[64,2048]{1,0:T(8,128)(2,1)S(1)}, bf16[64,2048]{1,0:T(8,128)(2,1)S(1)}, u32[]{:S(2)}, u32[]{:S(2)}) collective-permute-start(bf16[64,2048]{1,0:T(8,128)(2,1)S(1)} %shard_map.141.refs_0_), channel_id=1, source_target_pairs={{0,16},{8,24},{16,32},{24,40},{32,48},{40,56},{48,64},{56,72},{64,... | collective-permute-start | bytes 786440 | tf_op jit(solution)/shard_map/ppermute | solution.py:530
  82.5 3.6 %collective-permute-done.7.refs_2_ = bf16[64,2048]{1,0:T(8,128)(2,1)S(1)} collective-permute-done((bf16[64,2048]{1,0:T(8,128)(2,1)S(1)}, bf16[64,2048]{1,0:T(8,128)(2,1)S(1)}, u32[]{:S(2)}, u32[]{:S(2)}) %collective-permute-start.7) | collective-permute-done | bytes 262176 | tf_op jit(solution)/shard_map/ppermute | solution.py:532
  86.1 3.4 %collective-permute-start.9 = (bf16[64,2048]{1,0:T(8,128)(2,1)S(1)}, bf16[64,2048]{1,0:T(8,128)(2,1)S(1)}, u32[]{:S(2)}, u32[]{:S(2)}) collective-permute-start(bf16[64,2048]{1,0:T(8,128)(2,1)S(1)} %collective-permute-done.7.refs_2_), channel_id=1, source_target_pairs={{0,112},{8,120},{16,0},{24,8},{32,16},{40,24},{48,32},{56,40},{64,... | collective-permute-start | bytes 786440 | tf_op jit(solution)/shard_map/ppermute | solution.py:532
  89.5 0.0 all-gather.5.cloned.1.call-done
  89.5 2.4 %collective-permute-start.8 = (bf16[64,2048]{1,0:T(8,128)(2,1)S(1)}, bf16[64,2048]{1,0:T(8,128)(2,1)S(1)}, u32[]{:S(2)}, u32[]{:S(2)}) collective-permute-start(bf16[64,2048]{1,0:T(8,128)(2,1)S(1)} %collective-permute-done.6.refs_1_), channel_id=1, source_target_pairs={{0,16},{8,24},{16,32},{24,40},{32,48},{40,56},{48,64},{56,72},{64,... | collective-permute-start | bytes 786440 | tf_op jit(solution)/shard_map/ppermute | solution.py:530
  91.9 2.2 %shard_map.142.refs_5_ = bf16[4,1024,512]{2,1,0:T(8,128)(2,1)S(1)} custom-call(bf16[4,1024,512]{2,1,0:T(8,128)(2,1)} %bitcast.19), custom_call_target="tpu_custom_call" | custom-call | bytes 8388608 | tf_op jit(solution)/shard_map/pallas_call | solution.py:516
  94.2 0.4 collective-permute-done.9.refs_4_
  94.6 4.7 %collective-permute-done.8.refs_3_ = bf16[64,2048]{1,0:T(8,128)(2,1)S(1)} collective-permute-done((bf16[64,2048]{1,0:T(8,128)(2,1)S(1)}, bf16[64,2048]{1,0:T(8,128)(2,1)S(1)}, u32[]{:S(2)}, u32[]{:S(2)}) %collective-permute-start.8) | collective-permute-done | bytes 262176 | tf_op jit(solution)/shard_map/ppermute | solution.py:530
  99.3 2.3 %shard_map.143 = bf16[4,5,16,1024]{3,2,1,0:T(8,128)(2,1)} custom-call(bf16[64,2048]{1,0:T(8,128)(2,1)S(1)} %shard_map.141.refs_0_, bf16[64,2048]{1,0:T(8,128)(2,1)S(1)} %collective-permute-done.6.refs_1_, bf16[64,2048]{1,0:T(8,128)(2,1)S(1)} %collective-permute-done.7.refs_2_, bf16[64,2048]{1,0:T(8,128)(2,1)S(1)} %collective-permute-done.8.refs_3_, ...), custom_call_target="tpu_custom_call" | custom-call | flops 1350000000 | bytes 6291456 | tf_op jit(solution)/shard_map/pallas_call | solution.py:351
  101.6 0.0 reduce-scatter.2.cloned.1.call-update
  101.6 1.9 %collective-permute-start.10 = (bf16[64,2048]{1,0:T(8,128)(2,1)S(1)}, bf16[64,2048]{1,0:T(8,128)(2,1)S(1)}, u32[]{:S(2)}, u32[]{:S(2)}) collective-permute-start(bf16[64,2048]{1,0:T(8,128)(2,1)S(1)} %collective-permute-done.8.refs_3_), channel_id=1, source_target_pairs={{0,16},{8,24},{16,32},{24,40},{32,48},{40,56},{48,64},{56,72},{64,... | collective-permute-start | bytes 786440 | tf_op jit(solution)/shard_map/ppermute | solution.py:530
  103.5 5.1 %collective-permute-start.11 = (bf16[64,2048]{1,0:T(8,128)(2,1)S(1)}, bf16[64,2048]{1,0:T(8,128)(2,1)S(1)}, u32[]{:S(2)}, u32[]{:S(2)}) collective-permute-start(bf16[64,2048]{1,0:T(8,128)(2,1)S(1)} %collective-permute-done.9.refs_4_), channel_id=1, source_target_pairs={{0,112},{8,120},{16,0},{24,8},{32,16},{40,24},{48,32},{56,40},{64,... | collective-permute-start | bytes 786440 | tf_op jit(solution)/shard_map/ppermute | solution.py:532
  108.6 2.4 %collective-permute-done.10.refs_0_ = bf16[64,2048]{1,0:T(8,128)(2,1)S(1)} collective-permute-done((bf16[64,2048]{1,0:T(8,128)(2,1)S(1)}, bf16[64,2048]{1,0:T(8,128)(2,1)S(1)}, u32[]{:S(2)}, u32[]{:S(2)}) %collective-permute-start.10) | collective-permute-done | bytes 262176 | tf_op jit(solution)/shard_map/ppermute | solution.py:530
  111.1 1.9 %collective-permute-start.12 = (bf16[64,2048]{1,0:T(8,128)(2,1)S(1)}, bf16[64,2048]{1,0:T(8,128)(2,1)S(1)}, u32[]{:S(2)}, u32[]{:S(2)}) collective-permute-start(bf16[64,2048]{1,0:T(8,128)(2,1)S(1)} %collective-permute-done.10.refs_0_), channel_id=1, source_target_pairs={{0,16},{8,24},{16,32},{24,40},{32,48},{40,56},{48,64},{56,72},{64,... | collective-permute-start | bytes 786440 | tf_op jit(solution)/shard_map/ppermute | solution.py:530
  113.0 2.3 %shard_map.144.refs_3_ = bf16[4,1024,512]{2,1,0:T(8,128)(2,1)S(1)} custom-call(bf16[4,1024,512]{2,1,0:T(8,128)(2,1)} %bitcast.20), custom_call_target="tpu_custom_call" | custom-call | bytes 8388608 | tf_op jit(solution)/shard_map/pallas_call | solution.py:516
  115.3 5.2 %collective-permute-done.12.refs_2_ = bf16[64,2048]{1,0:T(8,128)(2,1)S(1)} collective-permute-done((bf16[64,2048]{1,0:T(8,128)(2,1)S(1)}, bf16[64,2048]{1,0:T(8,128)(2,1)S(1)}, u32[]{:S(2)}, u32[]{:S(2)}) %collective-permute-start.12) | collective-permute-done | bytes 262176 | tf_op jit(solution)/shard_map/ppermute | solution.py:530
  120.5 1.2 shard_map.145
  121.8 18.0 %all_to_all.21 = bf16[4,48,1024]{2,1,0:T(8,128)(2,1)S(1)} all-to-all(bf16[4,48,1024]{2,1,0:T(8,128)(2,1)S(1)} %bitcast.17), channel_id=1, replica_groups={{0,2,4,6},{1,3,5,7},{8,10,12,14},{9,11,13,15},{16,18,20,22},{17,19,21,2..., dimensions={0} | all-to-all | bytes 786432 | tf_op jit(solution)/shard_map/all_to_all | solution.py:541
  139.7 0.9 copy-done
  140.6 0.3 shard_map.146
  140.9 17.2 %all_to_all.22 = bf16[8,16,1024]{2,1,0:T(8,128)(2,1)S(1)} all-to-all(bf16[8,16,1024]{2,1,0:T(8,128)(2,1)S(1)} %shard_map.146), channel_id=1, replica_groups={{0,16,32,48,64,80,96,112},{8,24,40,56,72,88,104,120},{1,17,33,49,65,81,..., dimensions={0} | all-to-all | bytes 524288 | tf_op jit(solution)/shard_map/all_to_all | solution.py:551
  158.1 0.7 copy.16
  (15 shorter events, 0.0 us)
Async XLA Ops:
  6.5 55.6 %all-gather.3.cloned.1.call-start = ((), (), s32[]{:S(2)}) async-start(), calls=%async_computation.5 | async-start | bytes 3145728 | tf_op jit(solution)/shard_map/all_gather | solution.py:389
  9.8 3.9 %collective-permute-start = (bf16[128,1664]{1,0:T(8,128)(2,1)}, bf16[128,1664]{1,0:T(8,128)(2,1)S(1)}, u32[]{:S(2)}, u32[]{:S(2)}) collective-permute-start(bf16[128,1664]{1,0:T(8,128)(2,1)} %get-tuple-element.30.sent_in), channel_id=1, source_target_pairs={{0,8},{8,0},{16,24},{24,16},{32,40},{40,32},{48,56},{56,48},{64,72... | collective-permute-start | bytes 1277960 | tf_op jit(solution)/shard_map/ppermute | solution.py:419
  11.7 1.3 collective-permute-start.1
  12.4 0.7 collective-permute-start.2
  13.0 0.6 copy-start.3
  13.1 0.6 copy-start.4
  13.6 0.8 copy-start.2
  19.7 27.5 %all-to-all-start = ((bf16[8,80,256]{2,1,0:T(8,128)(2,1)}), bf16[8,80,256]{2,1,0:T(8,128)(2,1)S(1)}, u32[]{:S(2)}, u32[]{:S(2)}) async-start(bf16[8,80,256]{2,1,0:T(8,128)(2,1)} %get-tuple-element.34), calls=%async_computation | async-start | bytes 655360 | tf_op jit(solution)/shard_map/all_to_all | solution.py:452
  34.7 54.8 %all-gather.5.cloned.1.call-start = ((), (), s32[]{:S(2)}) async-start(), calls=%async_computation.6 | async-start | bytes 6291456 | tf_op jit(solution)/shard_map/all_gather | solution.py:483
  62.2 77.5 %reduce-scatter.2.cloned.1.call-start = ((), (), s32[]{:S(2)}) async-start(), calls=%async_computation.7 | async-start | bytes 819200 | tf_op jit(solution)/shard_map/reduce_scatter | solution.py:537
  64.6 8.7 %collective-permute-start.3 = (bf16[80,512]{1,0:T(8,128)(2,1)}, bf16[80,512]{1,0:T(8,128)(2,1)S(1)}, u32[]{:S(2)}, u32[]{:S(2)}) collective-permute-start(bf16[80,512]{1,0:T(8,128)(2,1)} %get-tuple-element.44), channel_id=1, source_target_pairs={{0,9},{1,8},{2,11},{3,10},{4,13},{5,12},{6,15},{7,14},{8,1},{9,0},... | collective-permute-start | bytes 245768 | tf_op jit(solution)/shard_map/ppermute | solution.py:504
  69.0 6.5 %collective-permute-start.4 = (bf16[80,512]{1,0:T(8,128)(2,1)}, bf16[80,512]{1,0:T(8,128)(2,1)S(1)}, u32[]{:S(2)}, u32[]{:S(2)}) collective-permute-start(bf16[80,512]{1,0:T(8,128)(2,1)} %get-tuple-element.45), channel_id=1, source_target_pairs={{0,1},{1,0},{2,3},{3,2},{4,5},{5,4},{6,7},{7,6},{8,9},{9,8},{10,11... | collective-permute-start | bytes 245768 | tf_op jit(solution)/shard_map/ppermute | solution.py:505
  71.4 4.2 %collective-permute-start.5 = (bf16[80,512]{1,0:T(8,128)(2,1)}, bf16[80,512]{1,0:T(8,128)(2,1)S(1)}, u32[]{:S(2)}, u32[]{:S(2)}) collective-permute-start(bf16[80,512]{1,0:T(8,128)(2,1)} %get-tuple-element.46), channel_id=1, source_target_pairs={{0,8},{8,0},{16,24},{24,16},{32,40},{40,32},{48,56},{56,48},{64,72... | collective-permute-start | bytes 245768 | tf_op jit(solution)/shard_map/ppermute | solution.py:506
  75.5 0.9 copy-start.1
  76.6 9.5 %collective-permute-start.7 = (bf16[64,2048]{1,0:T(8,128)(2,1)S(1)}, bf16[64,2048]{1,0:T(8,128)(2,1)S(1)}, u32[]{:S(2)}, u32[]{:S(2)}) collective-permute-start(bf16[64,2048]{1,0:T(8,128)(2,1)S(1)} %shard_map.141.refs_0_), channel_id=1, source_target_pairs={{0,112},{8,120},{16,0},{24,8},{32,16},{40,24},{48,32},{56,40},{64,... | collective-permute-start | bytes 786440 | tf_op jit(solution)/shard_map/ppermute | solution.py:532
  78.5 10.9 %collective-permute-start.6 = (bf16[64,2048]{1,0:T(8,128)(2,1)S(1)}, bf16[64,2048]{1,0:T(8,128)(2,1)S(1)}, u32[]{:S(2)}, u32[]{:S(2)}) collective-permute-start(bf16[64,2048]{1,0:T(8,128)(2,1)S(1)} %shard_map.141.refs_0_), channel_id=1, source_target_pairs={{0,16},{8,24},{16,32},{24,40},{32,48},{40,56},{48,64},{56,72},{64,... | collective-permute-start | bytes 786440 | tf_op jit(solution)/shard_map/ppermute | solution.py:530
  86.1 8.5 %collective-permute-start.9 = (bf16[64,2048]{1,0:T(8,128)(2,1)S(1)}, bf16[64,2048]{1,0:T(8,128)(2,1)S(1)}, u32[]{:S(2)}, u32[]{:S(2)}) collective-permute-start(bf16[64,2048]{1,0:T(8,128)(2,1)S(1)} %collective-permute-done.7.refs_2_), channel_id=1, source_target_pairs={{0,112},{8,120},{16,0},{24,8},{32,16},{40,24},{48,32},{56,40},{64,... | collective-permute-start | bytes 786440 | tf_op jit(solution)/shard_map/ppermute | solution.py:532
  89.5 9.8 %collective-permute-start.8 = (bf16[64,2048]{1,0:T(8,128)(2,1)S(1)}, bf16[64,2048]{1,0:T(8,128)(2,1)S(1)}, u32[]{:S(2)}, u32[]{:S(2)}) collective-permute-start(bf16[64,2048]{1,0:T(8,128)(2,1)S(1)} %collective-permute-done.6.refs_1_), channel_id=1, source_target_pairs={{0,16},{8,24},{16,32},{24,40},{32,48},{40,56},{48,64},{56,72},{64,... | collective-permute-start | bytes 786440 | tf_op jit(solution)/shard_map/ppermute | solution.py:530
  101.6 9.5 %collective-permute-start.10 = (bf16[64,2048]{1,0:T(8,128)(2,1)S(1)}, bf16[64,2048]{1,0:T(8,128)(2,1)S(1)}, u32[]{:S(2)}, u32[]{:S(2)}) collective-permute-start(bf16[64,2048]{1,0:T(8,128)(2,1)S(1)} %collective-permute-done.8.refs_3_), channel_id=1, source_target_pairs={{0,16},{8,24},{16,32},{24,40},{32,48},{40,56},{48,64},{56,72},{64,... | collective-permute-start | bytes 786440 | tf_op jit(solution)/shard_map/ppermute | solution.py:530
  103.5 11.8 %collective-permute-start.11 = (bf16[64,2048]{1,0:T(8,128)(2,1)S(1)}, bf16[64,2048]{1,0:T(8,128)(2,1)S(1)}, u32[]{:S(2)}, u32[]{:S(2)}) collective-permute-start(bf16[64,2048]{1,0:T(8,128)(2,1)S(1)} %collective-permute-done.9.refs_4_), channel_id=1, source_target_pairs={{0,112},{8,120},{16,0},{24,8},{32,16},{40,24},{48,32},{56,40},{64,... | collective-permute-start | bytes 786440 | tf_op jit(solution)/shard_map/ppermute | solution.py:532
  111.1 9.5 %collective-permute-start.12 = (bf16[64,2048]{1,0:T(8,128)(2,1)S(1)}, bf16[64,2048]{1,0:T(8,128)(2,1)S(1)}, u32[]{:S(2)}, u32[]{:S(2)}) collective-permute-start(bf16[64,2048]{1,0:T(8,128)(2,1)S(1)} %collective-permute-done.10.refs_0_), channel_id=1, source_target_pairs={{0,16},{8,24},{16,32},{24,40},{32,48},{40,56},{48,64},{56,72},{64,... | collective-permute-start | bytes 786440 | tf_op jit(solution)/shard_map/ppermute | solution.py:530
  139.7 0.9 copy-start
Sparse Core Ops, SparseCore 0:
  9.4 45.4 all-gather.2
  62.3 19.1 all-gather.4
  101.7 30.4 reduce-scatter.1

commit v5 on v4

--- a/solution.py
+++ b/solution.py
@@ -23,7 +23,7 @@
 PARITY = [[0, 2, 4, 6], [1, 3, 5, 7]]
 CORES = [[2 * i, 2 * i + 1] for i in range(CHIPS)]
 BOTH = [[0, 1], [2, 3], [4, 5], [6, 7]]
-NEAR = (0, 1, 7, 2, 6)
+NEAR = (0, 1, 7, 6, 2)
 FAR = (3, 5, 4)
 TO_CORE_0 = [(2 * i + 1, 2 * i + 2) for i in range(CHIPS - 1)]
 TO_CORE_1 = [(2 * i + 1, 2 * i + 3) for i in range(CHIPS - 1)]
@@ -325,8 +325,8 @@
     fetch([(source.at[i], out.at[i]) for i in range(4)], sems)
 
 
-def product_kernel(*refs):
-    *blocks, weights, out, rows, result, sems = refs
+def product_kernel(first, held, *refs):
+    *blocks, weights, out, rows, result, sems = refs[held:]
     count = len(blocks)
     for r, block in enumerate(blocks):
         rows[r * 64 : (r + 1) * 64, :] = block[...]
@@ -338,7 +338,9 @@
         for r in range(count):
             result[side, :, r] = value[r * 64 : (r + 1) * 64].reshape(4, 16, HALF)
         copy = pltpu.make_async_copy(
-            result.at[side], out.at[:, :, :, side * HALF : (side + 1) * HALF], sems.at[side]
+            result.at[side],
+            out.at[:, first : first + count, :, side * HALF : (side + 1) * HALF],
+            sems.at[side],
         )
         copy.start()
         moving.append(copy)
@@ -346,21 +348,23 @@
         copy.wait()
 
 
-def product(blocks, weights):
+def product(blocks, weights, units, first=0, held=None):
     count = len(blocks)
+    kept = [] if held is None else [held]
     return call(
-        product_kernel,
-        shaped((4, count, 16, 1024), BF16),
+        functools.partial(product_kernel, first, len(kept)),
+        shaped((4, units, 16, 1024), BF16),
         scratch=[
             pltpu.VMEM((count * 64, 2048), BF16),
             pltpu.VMEM((2, 4, count, 16, HALF), BF16),
             pltpu.SemaphoreType.DMA((2,)),
         ],
-        in_specs=[VMEM] * (count + 1),
+        in_specs=[HBM] * len(kept) + [VMEM] * (count + 1),
         out_specs=HBM,
         flops=count * 270_000_000,
         moved=6 << 20,
-    )(*blocks, weights)
+        input_output_aliases={0: 0} if kept else {},
+    )(*kept, *blocks, weights)
 
 
 def summed_over(terms, unit):
@@ -531,9 +535,11 @@
         if step < 3:
             down.append(lax.ppermute(down[-1], "context", DOWN))
     blocks = {**{r: up[r] for r in range(5)}, **{CHIPS - r: down[r] for r in range(1, 4)}}
-    near = product([blocks[r] for r in NEAR], staged(weights))
+    near_weights = staged(weights)
+    near = product([blocks[r] for r in NEAR[:-1]], near_weights, len(NEAR))
+    near = product([blocks[NEAR[-1]]], near_weights, len(NEAR), len(NEAR) - 1, near)
     blocks[3], weights = lax.optimization_barrier((blocks[3], weights))
-    far = product([blocks[r] for r in FAR], staged(weights))
+    far = product([blocks[r] for r in FAR], staged(weights), len(FAR))
     near = lax.psum_scatter(
         near.reshape(4 * 16 * len(NEAR), 1024), "tensor",
         scatter_dimension=0, tiled=True, axis_index_groups=PARITY,

time: 166 us -> 166 us (level)
  waiting for transfers between devices: 28.2 us -> 26 us
    ppermute x4, waiting for transfers between devices: 12.3 us -> 10.2 us  [body(): up.append(lax.ppermute(up[-1], 'context', UP))]
    pallas_call x2 -> x3, Pallas kernels: 3.53 us -> 4.98 us  [product(): call(functools.partial(product_kernel, first, len(kept)), shaped((4, unit...]
  transfers between devices with their start and end apart: 17 -> 17, of which waited for: 8 -> 8; matrix products, arithmetic and copies ran while one was open for 1% -> 1% of each run, Pallas kernels for 12% -> 13%
where the time goes in v5:
time: 166 us; the launch traced here: 165 us
  blocking collectives  50.1 us (30%)
  starting transfers between devices  47.6 us (29%)
  waiting for transfers between devices  26 us (16%)
  Pallas kernels  23.4 us (14%)
  between operations  13.4 us (8%)
  local copies, waits for them, and re-layouts  4.17 us (3%)
    all_to_all x1, blocking collectives, body(): lax.all_to_all(far.reshape(4, 16 * len(FAR), 1024), 'tensor', 0, 0, tiled...  18 us
    all_to_all x1, blocking collectives, body(): lax.all_to_all(ready, 'context', 0, 0, tiled=True, axis_index_groups=SAME...  17.2 us
    all_to_all x1, starting transfers between devices, body(): lax.all_to_all(added, 'context', 0, 0, tiled=True, axis_index_groups=SAME...  15 us
    all_to_all x1, blocking collectives, body(): lax.all_to_all(states, 'context', 0, 0, tiled=True, axis_index_groups=SAM...  14.9 us
    ppermute x3, starting transfers between devices, body(): down.append(lax.ppermute(down[-1], 'context', DOWN))  10.5 us
    ppermute x4, starting transfers between devices, body(): up.append(lax.ppermute(up[-1], 'context', UP))  10.2 us
    ppermute x4, waiting for transfers between devices, body(): up.append(lax.ppermute(up[-1], 'context', UP))  10.2 us
    all_to_all x1, waiting for transfers between devices, body(): lax.all_to_all(added, 'context', 0, 0, tiled=True, axis_index_groups=SAME...  8.28 us
  transfers between devices with their start and end apart: 17, of which 8 were waited for; matrix products, arithmetic and copies ran while one was open for 1% of the time, Pallas kernels for 13%

profile of v5, /device:TPU:16, one launch (start us, length us, event | category | flops | bytes accessed | tf_op | source)
XLA Modules:
  0.0 164.7 jit_solution(479491088397344335)
XLA Ops:
  6.5 0.7 all-gather.3.cloned.1.call-update
  7.3 2.5 %shard_map.136 = (bf16[128,1664]{1,0:T(8,128)(2,1)}, bf16[16,1024]{1,0:T(8,128)(2,1)}, bf16[16,1024]{1,0:T(8,128)(2,1)}, bf16[128,512]{1,0:T(8,128)(2,1)}, f32[32,1024]{1,0:T(8,128)}) custom-call(bf16[128,1024]{1,0:T(8,128)(2,1)} %xs.1, bf16[128,1024]{1,0:T(8,128)(2,1)} %zs.3, bf16[128,2,256]{2,1,0:T(2,128)(2,1)} %bcs.1, bf16[16,128]{1,0:T(8,128)(2,1)} %bitcast.23, ...), custom_call_target="tpu_custom_call" | custom-call | bytes 1048576 | tf_op jit(solution)/shard_map/pallas_call | solution.py:394
  9.8 1.9 %collective-permute-start = (bf16[128,1664]{1,0:T(8,128)(2,1)}, bf16[128,1664]{1,0:T(8,128)(2,1)S(1)}, u32[]{:S(2)}, u32[]{:S(2)}) collective-permute-start(bf16[128,1664]{1,0:T(8,128)(2,1)} %get-tuple-element.30.sent_in), channel_id=1, source_target_pairs={{0,8},{8,0},{16,24},{24,16},{32,40},{40,32},{48,56},{56,48},{64,72... | collective-permute-start | bytes 1277960 | tf_op jit(solution)/shard_map/ppermute | solution.py:423
  11.7 0.7 collective-permute-start.1
  12.4 0.7 collective-permute-start.2
  13.1 0.6 collective-permute-done.got_in.got
  13.6 0.0 copy-done.3
  13.7 0.7 copy-done.2
  14.4 5.2 %shard_map.137 = (bf16[8,80,256]{2,1,0:T(8,128)(2,1)}, bf16[256,512]{1,0:T(8,128)(2,1)}, bf16[256,512]{1,0:T(8,128)(2,1)}, f32[256,128]{1,0:T(8,128)}, f32[256,128]{1,0:T(8,128)}) custom-call(bf16[128,512]{1,0:T(8,128)(2,1)} %get-tuple-element.29.xs_in, bf16[128,1664]{1,0:T(8,128)(2,1)} %get-tuple-element.30.sent_in, bf16[128,1664]{1,0:T(8,128)(2,1)} %copy-done.2, ...), custom_call_target="tpu_custom_call" | custom-call | flops 200000000 | bytes 2097152 | tf_op jit(solution)/shard_map/pallas_call | solution.py:426
  19.7 15.0 %all-to-all-start = ((bf16[8,80,256]{2,1,0:T(8,128)(2,1)}), bf16[8,80,256]{2,1,0:T(8,128)(2,1)S(1)}, u32[]{:S(2)}, u32[]{:S(2)}) async-start(bf16[8,80,256]{2,1,0:T(8,128)(2,1)} %get-tuple-element.34), calls=%async_computation | async-start | bytes 655360 | tf_op jit(solution)/shard_map/all_to_all | solution.py:456
  34.7 0.0 all-gather.5.cloned.1.call-start
  34.7 0.8 dynamic-slice_bitcast_fusion.first
  35.6 3.3 %shard_map.138 = (f32[256,512]{1,0:T(8,128)}, f32[256,512]{1,0:T(8,128)}) custom-call(bf16[256,512]{1,0:T(8,128)(2,1)} %get-tuple-element.35.x_in, bf16[256,512]{1,0:T(8,128)(2,1)} %get-tuple-element.36.bc_in, f32[256,128]{1,0:T(8,128)} %get-tuple-element.37.cum_in, f32[256,128]{1,0:T(8,128)} %get-tuple-element.38.delta_in, f32[1,16]{1,0:T(1,128)} %bitcast.27, ...), custom_call_target="tpu_custom_call" | custom-call | flops 400000000 | bytes 2097152 | tf_op jit(solution)/shard_map/pallas_call | solution.py:457
  38.9 8.3 %all-to-all-done.got = bf16[8,80,256]{2,1,0:T(8,128)(2,1)S(1)} async-done(((bf16[8,80,256]{2,1,0:T(8,128)(2,1)}), bf16[8,80,256]{2,1,0:T(8,128)(2,1)S(1)}, u32[]{:S(2)}, u32[]{:S(2)}) %all-to-all-start) | async-done | bytes 327712 | tf_op jit(solution)/shard_map/all_to_all | solution.py:456
  47.2 0.1 shard_map.139
  47.3 14.9 %all_to_all.20 = bf16[8,64,256]{2,1,0:T(8,128)(2,1)} all-to-all(bf16[8,64,256]{2,1,0:T(8,128)(2,1)S(1)} %shard_map.139), channel_id=1, replica_groups={{0,16,32,48,64,80,96,112},{8,24,40,56,72,88,104,120},{1,17,33,49,65,81,..., dimensions={0} | all-to-all | bytes 524288 | tf_op jit(solution)/shard_map/all_to_all | solution.py:485
  62.2 0.0 all-gather.5.cloned.1.call-update
  62.2 0.0 reduce-scatter.2.cloned.1.call-start
  62.2 2.4 %shard_map.140 = (bf16[80,512]{1,0:T(8,128)(2,1)}, bf16[80,512]{1,0:T(8,128)(2,1)}, bf16[80,512]{1,0:T(8,128)(2,1)}, bf16[80,512]{1,0:T(8,128)(2,1)}) custom-call(bf16[512,256]{1,0:T(8,128)(2,1)} %bitcast.22, bf16[256,512]{1,0:T(8,128)(2,1)} %get-tuple-element.36.bc_in, f32[256,512]{1,0:T(8,128)} %get-tuple-element.42.inside_in, ...), custom_call_target="tpu_custom_call" | custom-call | flops 100000000 | bytes 2097152 | tf_op jit(solution)/shard_map/pallas_call | solution.py:490
  64.6 4.4 %collective-permute-start.3 = (bf16[80,512]{1,0:T(8,128)(2,1)}, bf16[80,512]{1,0:T(8,128)(2,1)S(1)}, u32[]{:S(2)}, u32[]{:S(2)}) collective-permute-start(bf16[80,512]{1,0:T(8,128)(2,1)} %get-tuple-element.44), channel_id=1, source_target_pairs={{0,9},{1,8},{2,11},{3,10},{4,13},{5,12},{6,15},{7,14},{8,1},{9,0},... | collective-permute-start | bytes 245768 | tf_op jit(solution)/shard_map/ppermute | solution.py:508
  69.0 2.4 %collective-permute-start.4 = (bf16[80,512]{1,0:T(8,128)(2,1)}, bf16[80,512]{1,0:T(8,128)(2,1)S(1)}, u32[]{:S(2)}, u32[]{:S(2)}) collective-permute-start(bf16[80,512]{1,0:T(8,128)(2,1)} %get-tuple-element.45), channel_id=1, source_target_pairs={{0,1},{1,0},{2,3},{3,2},{4,5},{5,4},{6,7},{7,6},{8,9},{9,8},{10,11... | collective-permute-start | bytes 245768 | tf_op jit(solution)/shard_map/ppermute | solution.py:509
  71.4 1.9 %collective-permute-start.5 = (bf16[80,512]{1,0:T(8,128)(2,1)}, bf16[80,512]{1,0:T(8,128)(2,1)S(1)}, u32[]{:S(2)}, u32[]{:S(2)}) collective-permute-start(bf16[80,512]{1,0:T(8,128)(2,1)} %get-tuple-element.46), channel_id=1, source_target_pairs={{0,8},{8,0},{16,24},{24,16},{32,40},{40,32},{48,56},{56,48},{64,72... | collective-permute-start | bytes 245768 | tf_op jit(solution)/shard_map/ppermute | solution.py:510
  73.3 2.2 %collective-permute-done.4.next_got = bf16[80,512]{1,0:T(8,128)(2,1)S(1)} collective-permute-done((bf16[80,512]{1,0:T(8,128)(2,1)}, bf16[80,512]{1,0:T(8,128)(2,1)S(1)}, u32[]{:S(2)}, u32[]{:S(2)}) %collective-permute-start.4) | collective-permute-done | bytes 81952 | tf_op jit(solution)/shard_map/ppermute | solution.py:509
  75.5 0.9 copy-done.1
  76.4 0.1 shard_map.141.refs_0_
  76.6 1.9 %collective-permute-start.7 = (bf16[64,2048]{1,0:T(8,128)(2,1)S(1)}, bf16[64,2048]{1,0:T(8,128)(2,1)S(1)}, u32[]{:S(2)}, u32[]{:S(2)}) collective-permute-start(bf16[64,2048]{1,0:T(8,128)(2,1)S(1)} %shard_map.141.refs_0_), channel_id=1, source_target_pairs={{0,112},{8,120},{16,0},{24,8},{32,16},{40,24},{48,32},{56,40},{64,... | collective-permute-start | bytes 786440 | tf_op jit(solution)/shard_map/ppermute | solution.py:536
  78.5 3.9 %collective-permute-start.6 = (bf16[64,2048]{1,0:T(8,128)(2,1)S(1)}, bf16[64,2048]{1,0:T(8,128)(2,1)S(1)}, u32[]{:S(2)}, u32[]{:S(2)}) collective-permute-start(bf16[64,2048]{1,0:T(8,128)(2,1)S(1)} %shard_map.141.refs_0_), channel_id=1, source_target_pairs={{0,16},{8,24},{16,32},{24,40},{32,48},{40,56},{48,64},{56,72},{64,... | collective-permute-start | bytes 786440 | tf_op jit(solution)/shard_map/ppermute | solution.py:534
  82.5 3.6 %collective-permute-done.7.refs_2_ = bf16[64,2048]{1,0:T(8,128)(2,1)S(1)} collective-permute-done((bf16[64,2048]{1,0:T(8,128)(2,1)S(1)}, bf16[64,2048]{1,0:T(8,128)(2,1)S(1)}, u32[]{:S(2)}, u32[]{:S(2)}) %collective-permute-start.7) | collective-permute-done | bytes 262176 | tf_op jit(solution)/shard_map/ppermute | solution.py:536
  86.1 3.4 %collective-permute-start.8 = (bf16[64,2048]{1,0:T(8,128)(2,1)S(1)}, bf16[64,2048]{1,0:T(8,128)(2,1)S(1)}, u32[]{:S(2)}, u32[]{:S(2)}) collective-permute-start(bf16[64,2048]{1,0:T(8,128)(2,1)S(1)} %collective-permute-done.7.refs_2_), channel_id=1, source_target_pairs={{0,112},{8,120},{16,0},{24,8},{32,16},{40,24},{48,32},{56,40},{64,... | collective-permute-start | bytes 786440 | tf_op jit(solution)/shard_map/ppermute | solution.py:536
  89.5 0.0 all-gather.5.cloned.1.call-done
  89.5 2.4 %collective-permute-start.9 = (bf16[64,2048]{1,0:T(8,128)(2,1)S(1)}, bf16[64,2048]{1,0:T(8,128)(2,1)S(1)}, u32[]{:S(2)}, u32[]{:S(2)}) collective-permute-start(bf16[64,2048]{1,0:T(8,128)(2,1)S(1)} %collective-permute-done.6.refs_1_), channel_id=1, source_target_pairs={{0,16},{8,24},{16,32},{24,40},{32,48},{40,56},{48,64},{56,72},{64,... | collective-permute-start | bytes 786440 | tf_op jit(solution)/shard_map/ppermute | solution.py:534
  91.9 2.2 %shard_map.142.refs_4_.refs_2_ = bf16[4,1024,512]{2,1,0:T(8,128)(2,1)S(1)} custom-call(bf16[4,1024,512]{2,1,0:T(8,128)(2,1)} %bitcast.19), custom_call_target="tpu_custom_call" | custom-call | bytes 8388608 | tf_op jit(solution)/shard_map/pallas_call | solution.py:520
  94.2 0.4 collective-permute-done.8.refs_3_
  94.6 2.1 %shard_map.143.refs_0_ = bf16[4,5,16,1024]{3,2,1,0:T(8,128)(2,1)} custom-call(bf16[64,2048]{1,0:T(8,128)(2,1)S(1)} %shard_map.141.refs_0_, bf16[64,2048]{1,0:T(8,128)(2,1)S(1)} %collective-permute-done.6.refs_1_, bf16[64,2048]{1,0:T(8,128)(2,1)S(1)} %collective-permute-done.7.refs_2_, bf16[64,2048]{1,0:T(8,128)(2,1)S(1)} %collective-permute-done.8.refs_3_, ...), custom_call_target="tpu_custom_call" | custom-call | flops 1080000000 | bytes 6291456 | tf_op jit(solution)/shard_map/pallas_call | solution.py:354
  96.7 2.5 %collective-permute-done.9.refs_1_ = bf16[64,2048]{1,0:T(8,128)(2,1)S(1)} collective-permute-done((bf16[64,2048]{1,0:T(8,128)(2,1)S(1)}, bf16[64,2048]{1,0:T(8,128)(2,1)S(1)}, u32[]{:S(2)}, u32[]{:S(2)}) %collective-permute-start.9) | collective-permute-done | bytes 262176 | tf_op jit(solution)/shard_map/ppermute | solution.py:534
  99.3 1.6 shard_map.144
  100.9 1.9 %collective-permute-start.10 = (bf16[64,2048]{1,0:T(8,128)(2,1)S(1)}, bf16[64,2048]{1,0:T(8,128)(2,1)S(1)}, u32[]{:S(2)}, u32[]{:S(2)}) collective-permute-start(bf16[64,2048]{1,0:T(8,128)(2,1)S(1)} %collective-permute-done.9.refs_1_), channel_id=1, source_target_pairs={{0,16},{8,24},{16,32},{24,40},{32,48},{40,56},{48,64},{56,72},{64,... | collective-permute-start | bytes 786440 | tf_op jit(solution)/shard_map/ppermute | solution.py:534
  102.8 5.1 %collective-permute-start.11 = (bf16[64,2048]{1,0:T(8,128)(2,1)S(1)}, bf16[64,2048]{1,0:T(8,128)(2,1)S(1)}, u32[]{:S(2)}, u32[]{:S(2)}) collective-permute-start(bf16[64,2048]{1,0:T(8,128)(2,1)S(1)} %collective-permute-done.8.refs_3_), channel_id=1, source_target_pairs={{0,112},{8,120},{16,0},{24,8},{32,16},{40,24},{48,32},{56,40},{64,... | collective-permute-start | bytes 786440 | tf_op jit(solution)/shard_map/ppermute | solution.py:536
  108.0 2.4 %collective-permute-done.10.refs_0_ = bf16[64,2048]{1,0:T(8,128)(2,1)S(1)} collective-permute-done((bf16[64,2048]{1,0:T(8,128)(2,1)S(1)}, bf16[64,2048]{1,0:T(8,128)(2,1)S(1)}, u32[]{:S(2)}, u32[]{:S(2)}) %collective-permute-start.10) | collective-permute-done | bytes 262176 | tf_op jit(solution)/shard_map/ppermute | solution.py:534
  110.4 1.9 %collective-permute-start.12 = (bf16[64,2048]{1,0:T(8,128)(2,1)S(1)}, bf16[64,2048]{1,0:T(8,128)(2,1)S(1)}, u32[]{:S(2)}, u32[]{:S(2)}) collective-permute-start(bf16[64,2048]{1,0:T(8,128)(2,1)S(1)} %collective-permute-done.10.refs_0_), channel_id=1, source_target_pairs={{0,16},{8,24},{16,32},{24,40},{32,48},{40,56},{48,64},{56,72},{64,... | collective-permute-start | bytes 786440 | tf_op jit(solution)/shard_map/ppermute | solution.py:534
  112.3 2.3 %shard_map.145.refs_3_ = bf16[4,1024,512]{2,1,0:T(8,128)(2,1)S(1)} custom-call(bf16[4,1024,512]{2,1,0:T(8,128)(2,1)} %bitcast.20), custom_call_target="tpu_custom_call" | custom-call | bytes 8388608 | tf_op jit(solution)/shard_map/pallas_call | solution.py:520
  114.6 5.2 %collective-permute-done.12.refs_2_ = bf16[64,2048]{1,0:T(8,128)(2,1)S(1)} collective-permute-done((bf16[64,2048]{1,0:T(8,128)(2,1)S(1)}, bf16[64,2048]{1,0:T(8,128)(2,1)S(1)}, u32[]{:S(2)}, u32[]{:S(2)}) %collective-permute-start.12) | collective-permute-done | bytes 262176 | tf_op jit(solution)/shard_map/ppermute | solution.py:534
  119.8 1.2 shard_map.146
  121.1 18.0 %all_to_all.21 = bf16[4,48,1024]{2,1,0:T(8,128)(2,1)S(1)} all-to-all(bf16[4,48,1024]{2,1,0:T(8,128)(2,1)S(1)} %bitcast.17), channel_id=1, replica_groups={{0,2,4,6},{1,3,5,7},{8,10,12,14},{9,11,13,15},{16,18,20,22},{17,19,21,2..., dimensions={0} | all-to-all | bytes 786432 | tf_op jit(solution)/shard_map/all_to_all | solution.py:547
  139.1 0.9 copy-done
  140.0 0.3 shard_map.147
  140.2 17.2 %all_to_all.22 = bf16[8,16,1024]{2,1,0:T(8,128)(2,1)S(1)} all-to-all(bf16[8,16,1024]{2,1,0:T(8,128)(2,1)S(1)} %shard_map.147), channel_id=1, replica_groups={{0,16,32,48,64,80,96,112},{8,24,40,56,72,88,104,120},{1,17,33,49,65,81,..., dimensions={0} | all-to-all | bytes 524288 | tf_op jit(solution)/shard_map/all_to_all | solution.py:557
  157.4 0.7 copy.17
  (16 shorter events, 0.1 us)
Async XLA Ops:
  6.5 55.6 %all-gather.3.cloned.1.call-start = ((), (), s32[]{:S(2)}) async-start(), calls=%async_computation.5 | async-start | bytes 3145728 | tf_op jit(solution)/shard_map/all_gather | solution.py:393
  9.8 3.9 %collective-permute-start = (bf16[128,1664]{1,0:T(8,128)(2,1)}, bf16[128,1664]{1,0:T(8,128)(2,1)S(1)}, u32[]{:S(2)}, u32[]{:S(2)}) collective-permute-start(bf16[128,1664]{1,0:T(8,128)(2,1)} %get-tuple-element.30.sent_in), channel_id=1, source_target_pairs={{0,8},{8,0},{16,24},{24,16},{32,40},{40,32},{48,56},{56,48},{64,72... | collective-permute-start | bytes 1277960 | tf_op jit(solution)/shard_map/ppermute | solution.py:423
  11.7 1.3 collective-permute-start.1
  12.4 0.7 collective-permute-start.2
  13.0 0.6 copy-start.3
  13.1 0.6 copy-start.4
  13.6 0.8 copy-start.2
  19.7 27.5 %all-to-all-start = ((bf16[8,80,256]{2,1,0:T(8,128)(2,1)}), bf16[8,80,256]{2,1,0:T(8,128)(2,1)S(1)}, u32[]{:S(2)}, u32[]{:S(2)}) async-start(bf16[8,80,256]{2,1,0:T(8,128)(2,1)} %get-tuple-element.34), calls=%async_computation | async-start | bytes 655360 | tf_op jit(solution)/shard_map/all_to_all | solution.py:456
  34.7 54.8 %all-gather.5.cloned.1.call-start = ((), (), s32[]{:S(2)}) async-start(), calls=%async_computation.6 | async-start | bytes 6291456 | tf_op jit(solution)/shard_map/all_gather | solution.py:487
  62.2 76.9 %reduce-scatter.2.cloned.1.call-start = ((), (), s32[]{:S(2)}) async-start(), calls=%async_computation.7 | async-start | bytes 819200 | tf_op jit(solution)/shard_map/reduce_scatter | solution.py:543
  64.6 8.7 %collective-permute-start.3 = (bf16[80,512]{1,0:T(8,128)(2,1)}, bf16[80,512]{1,0:T(8,128)(2,1)S(1)}, u32[]{:S(2)}, u32[]{:S(2)}) collective-permute-start(bf16[80,512]{1,0:T(8,128)(2,1)} %get-tuple-element.44), channel_id=1, source_target_pairs={{0,9},{1,8},{2,11},{3,10},{4,13},{5,12},{6,15},{7,14},{8,1},{9,0},... | collective-permute-start | bytes 245768 | tf_op jit(solution)/shard_map/ppermute | solution.py:508
  69.0 6.5 %collective-permute-start.4 = (bf16[80,512]{1,0:T(8,128)(2,1)}, bf16[80,512]{1,0:T(8,128)(2,1)S(1)}, u32[]{:S(2)}, u32[]{:S(2)}) collective-permute-start(bf16[80,512]{1,0:T(8,128)(2,1)} %get-tuple-element.45), channel_id=1, source_target_pairs={{0,1},{1,0},{2,3},{3,2},{4,5},{5,4},{6,7},{7,6},{8,9},{9,8},{10,11... | collective-permute-start | bytes 245768 | tf_op jit(solution)/shard_map/ppermute | solution.py:509
  71.4 4.2 %collective-permute-start.5 = (bf16[80,512]{1,0:T(8,128)(2,1)}, bf16[80,512]{1,0:T(8,128)(2,1)S(1)}, u32[]{:S(2)}, u32[]{:S(2)}) collective-permute-start(bf16[80,512]{1,0:T(8,128)(2,1)} %get-tuple-element.46), channel_id=1, source_target_pairs={{0,8},{8,0},{16,24},{24,16},{32,40},{40,32},{48,56},{56,48},{64,72... | collective-permute-start | bytes 245768 | tf_op jit(solution)/shard_map/ppermute | solution.py:510
  75.5 0.9 copy-start.1
  76.6 9.5 %collective-permute-start.7 = (bf16[64,2048]{1,0:T(8,128)(2,1)S(1)}, bf16[64,2048]{1,0:T(8,128)(2,1)S(1)}, u32[]{:S(2)}, u32[]{:S(2)}) collective-permute-start(bf16[64,2048]{1,0:T(8,128)(2,1)S(1)} %shard_map.141.refs_0_), channel_id=1, source_target_pairs={{0,112},{8,120},{16,0},{24,8},{32,16},{40,24},{48,32},{56,40},{64,... | collective-permute-start | bytes 786440 | tf_op jit(solution)/shard_map/ppermute | solution.py:536
  78.5 10.9 %collective-permute-start.6 = (bf16[64,2048]{1,0:T(8,128)(2,1)S(1)}, bf16[64,2048]{1,0:T(8,128)(2,1)S(1)}, u32[]{:S(2)}, u32[]{:S(2)}) collective-permute-start(bf16[64,2048]{1,0:T(8,128)(2,1)S(1)} %shard_map.141.refs_0_), channel_id=1, source_target_pairs={{0,16},{8,24},{16,32},{24,40},{32,48},{40,56},{48,64},{56,72},{64,... | collective-permute-start | bytes 786440 | tf_op jit(solution)/shard_map/ppermute | solution.py:534
  86.1 8.5 %collective-permute-start.8 = (bf16[64,2048]{1,0:T(8,128)(2,1)S(1)}, bf16[64,2048]{1,0:T(8,128)(2,1)S(1)}, u32[]{:S(2)}, u32[]{:S(2)}) collective-permute-start(bf16[64,2048]{1,0:T(8,128)(2,1)S(1)} %collective-permute-done.7.refs_2_), channel_id=1, source_target_pairs={{0,112},{8,120},{16,0},{24,8},{32,16},{40,24},{48,32},{56,40},{64,... | collective-permute-start | bytes 786440 | tf_op jit(solution)/shard_map/ppermute | solution.py:536
  89.5 9.8 %collective-permute-start.9 = (bf16[64,2048]{1,0:T(8,128)(2,1)S(1)}, bf16[64,2048]{1,0:T(8,128)(2,1)S(1)}, u32[]{:S(2)}, u32[]{:S(2)}) collective-permute-start(bf16[64,2048]{1,0:T(8,128)(2,1)S(1)} %collective-permute-done.6.refs_1_), channel_id=1, source_target_pairs={{0,16},{8,24},{16,32},{24,40},{32,48},{40,56},{48,64},{56,72},{64,... | collective-permute-start | bytes 786440 | tf_op jit(solution)/shard_map/ppermute | solution.py:534
  100.9 9.5 %collective-permute-start.10 = (bf16[64,2048]{1,0:T(8,128)(2,1)S(1)}, bf16[64,2048]{1,0:T(8,128)(2,1)S(1)}, u32[]{:S(2)}, u32[]{:S(2)}) collective-permute-start(bf16[64,2048]{1,0:T(8,128)(2,1)S(1)} %collective-permute-done.9.refs_1_), channel_id=1, source_target_pairs={{0,16},{8,24},{16,32},{24,40},{32,48},{40,56},{48,64},{56,72},{64,... | collective-permute-start | bytes 786440 | tf_op jit(solution)/shard_map/ppermute | solution.py:534
  102.8 11.8 %collective-permute-start.11 = (bf16[64,2048]{1,0:T(8,128)(2,1)S(1)}, bf16[64,2048]{1,0:T(8,128)(2,1)S(1)}, u32[]{:S(2)}, u32[]{:S(2)}) collective-permute-start(bf16[64,2048]{1,0:T(8,128)(2,1)S(1)} %collective-permute-done.8.refs_3_), channel_id=1, source_target_pairs={{0,112},{8,120},{16,0},{24,8},{32,16},{40,24},{48,32},{56,40},{64,... | collective-permute-start | bytes 786440 | tf_op jit(solution)/shard_map/ppermute | solution.py:536
  110.4 9.5 %collective-permute-start.12 = (bf16[64,2048]{1,0:T(8,128)(2,1)S(1)}, bf16[64,2048]{1,0:T(8,128)(2,1)S(1)}, u32[]{:S(2)}, u32[]{:S(2)}) collective-permute-start(bf16[64,2048]{1,0:T(8,128)(2,1)S(1)} %collective-permute-done.10.refs_0_), channel_id=1, source_target_pairs={{0,16},{8,24},{16,32},{24,40},{32,48},{40,56},{48,64},{56,72},{64,... | collective-permute-start | bytes 786440 | tf_op jit(solution)/shard_map/ppermute | solution.py:534
  139.1 0.9 copy-start
Sparse Core Ops, SparseCore 0:
  9.4 45.4 all-gather.2
  62.3 19.1 all-gather.4
  101.0 30.4 reduce-scatter.1

commit v6 on v5

--- a/solution.py
+++ b/solution.py
@@ -16,6 +16,7 @@
 CHIPS = 8
 PAIR = [(i, i ^ 1) for i in range(16)]
 SAME_CORE = [[2 * i + k for i in range(CHIPS)] for k in range(2)]
+BACKWARD = [group[::-1] for group in SAME_CORE]
 UP = [(i, (i + 2) % 16) for i in range(16)]
 DOWN = [(i, (i - 2) % 16) for i in range(16)]
 CROSS = [(8 * i + t, 8 * (i ^ 1) + (t ^ 1)) for i in range(16) for t in range(8)]
@@ -262,7 +263,7 @@
 def prefix_kernel(got, first, out):
     state = first[...]
     for chip in range(CHIPS):
-        out[chip] = state.astype(BF16)
+        out[CHIPS - 1 - chip] = state.astype(BF16)
         if chip < CHIPS - 1:
             terms = got[chip, P_SIZE : P_SIZE + 16, :].astype(F32)
             decay = jnp.exp(terms[0:1] + terms[1:2] + terms[2:3])
@@ -277,10 +278,13 @@
     fetch(
         [
             (bc_in.at[:, N : 2 * N], c),
-            (state_in, state),
             (inside_in, inside),
             (scale_in, scale),
             (gain_in, gain),
+        ]
+        + [
+            (state_in.at[(7 - h) * P_SIZE : (8 - h) * P_SIZE], state.at[h * P_SIZE : (h + 1) * P_SIZE])
+            for h in range(HEADS)
         ],
         sems,
     )
@@ -379,10 +383,10 @@
     moving = copies([(near, summed)], sems)
     moving[0].start()
     for r, before in enumerate(FAR):
-        out[lax.rem(chip + (CHIPS - before), CHIPS)] = summed_over(far, r)
+        out[CHIPS - 1 - lax.rem(chip + (CHIPS - before), CHIPS)] = summed_over(far, r)
     moving[0].wait()
     for r, before in enumerate(NEAR):
-        out[lax.rem(chip + (CHIPS - before), CHIPS)] = summed[r]
+        out[CHIPS - 1 - lax.rem(chip + (CHIPS - before), CHIPS)] = summed[r]
 
 
 def body(
@@ -482,7 +486,7 @@
         in_specs=[VMEM] * 2,
         moved=1 << 20,
     )(increments, first)
-    states = lax.all_to_all(states, "context", 0, 0, tiled=True, axis_index_groups=SAME_CORE)
+    states = lax.all_to_all(states, "context", 0, 0, tiled=True, axis_index_groups=BACKWARD)
     states, weights = lax.optimization_barrier((states, weights))
     weights = lax.all_gather(weights, "context", axis=0, tiled=True, axis_index_groups=CORES)
     weights = weights.reshape(4, 1024, HALF)
@@ -497,7 +501,7 @@
             pltpu.VMEM((CHIP, HALF), F32),
             pltpu.VMEM((1, 1024), F32),
             pltpu.VMEM((2, 4, 2, 16, HALF), BF16),
-            pltpu.SemaphoreType.DMA((5,)),
+            pltpu.SemaphoreType.DMA((4 + HEADS,)),
         ],
         in_specs=[HBM] * 5,
         out_specs=[VMEM] * 4,
@@ -555,8 +559,8 @@
         moved=2 << 20,
     )(near.reshape(len(NEAR), 16, 1024), far.reshape(4, len(FAR), 16, 1024))
     return lax.all_to_all(
-        ready, "context", 0, 0, tiled=True, axis_index_groups=SAME_CORE
-    ).transpose(1, 0, 2).reshape(16, 8192)
+        ready, "context", 0, 0, tiled=True, axis_index_groups=BACKWARD
+    )[::-1].transpose(1, 0, 2).reshape(16, 8192)
 
 
 def solution(mesh):

time: 166 us -> 162 us (0.976)
  the two profiles are of different devices: /device:TPU:16 before, /device:TPU:2 now
where the time goes in v6:
time: 162 us
  starting transfers between devices  52.1 us (32%)
  blocking collectives  42.2 us (26%)
  waiting for transfers between devices  26.5 us (16%)
  Pallas kernels  23.3 us (14%)
  between operations  13.4 us (8%)
  local copies, waits for them, and re-layouts  4.16 us (3%)
    ppermute x3, starting transfers between devices, body(): down.append(lax.ppermute(down[-1], 'context', DOWN))  18 us
    all_to_all x1, blocking collectives, body(): lax.all_to_all(far.reshape(4, 16 * len(FAR), 1024), 'tensor', 0, 0, tiled...  17.8 us
    all_to_all x1, starting transfers between devices, body(): lax.all_to_all(added, 'context', 0, 0, tiled=True, axis_index_groups=SAME...  15 us
    all_to_all x1, blocking collectives, body(): lax.all_to_all(ready, 'context', 0, 0, tiled=True, axis_index_groups=BACK...  12.3 us
    all_to_all x1, blocking collectives, body(): lax.all_to_all(states, 'context', 0, 0, tiled=True, axis_index_groups=BAC...  12.1 us
    ppermute x4, waiting for transfers between devices, body(): up.append(lax.ppermute(up[-1], 'context', UP))  10.9 us
    all_to_all x1, waiting for transfers between devices, body(): lax.all_to_all(added, 'context', 0, 0, tiled=True, axis_index_groups=SAME...  8.28 us
    ppermute x4, starting transfers between devices, body(): up.append(lax.ppermute(up[-1], 'context', UP))  7.67 us
  transfers between devices with their start and end apart: 17, of which 8 were waited for; matrix products, arithmetic and copies ran while one was open for 1% of the time, Pallas kernels for 13%

profile of v6, /device:TPU:2, one launch (start us, length us, event | category | flops | bytes accessed | tf_op | source)
XLA Modules:
  0.0 161.6 jit_solution(12812938792674118629)
XLA Ops:
  6.5 0.7 all-gather.3.cloned.1.call-update
  7.3 2.5 %shard_map.136 = (bf16[128,1664]{1,0:T(8,128)(2,1)}, bf16[16,1024]{1,0:T(8,128)(2,1)}, bf16[16,1024]{1,0:T(8,128)(2,1)}, bf16[128,512]{1,0:T(8,128)(2,1)}, f32[32,1024]{1,0:T(8,128)}) custom-call(bf16[128,1024]{1,0:T(8,128)(2,1)} %xs.1, bf16[128,1024]{1,0:T(8,128)(2,1)} %zs.3, bf16[128,2,256]{2,1,0:T(2,128)(2,1)} %bcs.1, bf16[16,128]{1,0:T(8,128)(2,1)} %bitcast.23, ...), custom_call_target="tpu_custom_call" | custom-call | bytes 1048576 | tf_op jit(solution)/shard_map/pallas_call | solution.py:398
  9.8 1.9 %collective-permute-start = (bf16[128,1664]{1,0:T(8,128)(2,1)}, bf16[128,1664]{1,0:T(8,128)(2,1)S(1)}, u32[]{:S(2)}, u32[]{:S(2)}) collective-permute-start(bf16[128,1664]{1,0:T(8,128)(2,1)} %get-tuple-element.30.sent_in), channel_id=1, source_target_pairs={{0,8},{8,0},{16,24},{24,16},{32,40},{40,32},{48,56},{56,48},{64,72... | collective-permute-start | bytes 1277960 | tf_op jit(solution)/shard_map/ppermute | solution.py:427
  11.7 0.7 collective-permute-start.1
  12.4 0.7 collective-permute-start.2
  13.1 0.6 collective-permute-done.got_in.got
  13.6 0.0 copy-done.3
  13.7 0.7 copy-done.2
  14.4 5.2 %shard_map.137 = (bf16[8,80,256]{2,1,0:T(8,128)(2,1)}, bf16[256,512]{1,0:T(8,128)(2,1)}, bf16[256,512]{1,0:T(8,128)(2,1)}, f32[256,128]{1,0:T(8,128)}, f32[256,128]{1,0:T(8,128)}) custom-call(bf16[128,512]{1,0:T(8,128)(2,1)} %get-tuple-element.29.xs_in, bf16[128,1664]{1,0:T(8,128)(2,1)} %get-tuple-element.30.sent_in, bf16[128,1664]{1,0:T(8,128)(2,1)} %copy-done.2, ...), custom_call_target="tpu_custom_call" | custom-call | flops 200000000 | bytes 2097152 | tf_op jit(solution)/shard_map/pallas_call | solution.py:430
  19.6 15.0 %all-to-all-start = ((bf16[8,80,256]{2,1,0:T(8,128)(2,1)}), bf16[8,80,256]{2,1,0:T(8,128)(2,1)S(1)}, u32[]{:S(2)}, u32[]{:S(2)}) async-start(bf16[8,80,256]{2,1,0:T(8,128)(2,1)} %get-tuple-element.34), calls=%async_computation | async-start | bytes 655360 | tf_op jit(solution)/shard_map/all_to_all | solution.py:460
  34.7 0.0 all-gather.5.cloned.1.call-start
  34.7 0.8 dynamic-slice_bitcast_fusion.first
  35.6 3.3 %shard_map.138 = (f32[256,512]{1,0:T(8,128)}, f32[256,512]{1,0:T(8,128)}) custom-call(bf16[256,512]{1,0:T(8,128)(2,1)} %get-tuple-element.35.x_in, bf16[256,512]{1,0:T(8,128)(2,1)} %get-tuple-element.36.bc_in, f32[256,128]{1,0:T(8,128)} %get-tuple-element.37.cum_in, f32[256,128]{1,0:T(8,128)} %get-tuple-element.38.delta_in, f32[1,16]{1,0:T(1,128)} %bitcast.27, ...), custom_call_target="tpu_custom_call" | custom-call | flops 400000000 | bytes 2097152 | tf_op jit(solution)/shard_map/pallas_call | solution.py:461
  38.9 8.3 %all-to-all-done.got = bf16[8,80,256]{2,1,0:T(8,128)(2,1)S(1)} async-done(((bf16[8,80,256]{2,1,0:T(8,128)(2,1)}), bf16[8,80,256]{2,1,0:T(8,128)(2,1)S(1)}, u32[]{:S(2)}, u32[]{:S(2)}) %all-to-all-start) | async-done | bytes 327712 | tf_op jit(solution)/shard_map/all_to_all | solution.py:460
  47.2 0.1 shard_map.139
  47.3 12.1 %all_to_all.20 = bf16[8,64,256]{2,1,0:T(8,128)(2,1)} all-to-all(bf16[8,64,256]{2,1,0:T(8,128)(2,1)S(1)} %shard_map.139), channel_id=1, replica_groups={{112,96,80,64,48,32,16,0},{120,104,88,72,56,40,24,8},{113,97,81,65,49,3..., dimensions={0} | all-to-all | bytes 524288 | tf_op jit(solution)/shard_map/all_to_all | solution.py:489
  59.4 0.0 all-gather.5.cloned.1.call-update
  59.4 0.0 reduce-scatter.2.cloned.1.call-start
  59.5 2.4 %shard_map.140 = (bf16[80,512]{1,0:T(8,128)(2,1)}, bf16[80,512]{1,0:T(8,128)(2,1)}, bf16[80,512]{1,0:T(8,128)(2,1)}, bf16[80,512]{1,0:T(8,128)(2,1)}) custom-call(bf16[512,256]{1,0:T(8,128)(2,1)} %bitcast.22, bf16[256,512]{1,0:T(8,128)(2,1)} %get-tuple-element.36.bc_in, f32[256,512]{1,0:T(8,128)} %get-tuple-element.42.inside_in, ...), custom_call_target="tpu_custom_call" | custom-call | flops 100000000 | bytes 2097152 | tf_op jit(solution)/shard_map/pallas_call | solution.py:494
  61.8 3.7 %collective-permute-start.3 = (bf16[80,512]{1,0:T(8,128)(2,1)}, bf16[80,512]{1,0:T(8,128)(2,1)S(1)}, u32[]{:S(2)}, u32[]{:S(2)}) collective-permute-start(bf16[80,512]{1,0:T(8,128)(2,1)} %get-tuple-element.44), channel_id=1, source_target_pairs={{0,9},{1,8},{2,11},{3,10},{4,13},{5,12},{6,15},{7,14},{8,1},{9,0},... | collective-permute-start | bytes 245768 | tf_op jit(solution)/shard_map/ppermute | solution.py:512
  65.6 2.4 %collective-permute-start.4 = (bf16[80,512]{1,0:T(8,128)(2,1)}, bf16[80,512]{1,0:T(8,128)(2,1)S(1)}, u32[]{:S(2)}, u32[]{:S(2)}) collective-permute-start(bf16[80,512]{1,0:T(8,128)(2,1)} %get-tuple-element.45), channel_id=1, source_target_pairs={{0,1},{1,0},{2,3},{3,2},{4,5},{5,4},{6,7},{7,6},{8,9},{9,8},{10,11... | collective-permute-start | bytes 245768 | tf_op jit(solution)/shard_map/ppermute | solution.py:513
  67.9 1.9 %collective-permute-start.5 = (bf16[80,512]{1,0:T(8,128)(2,1)}, bf16[80,512]{1,0:T(8,128)(2,1)S(1)}, u32[]{:S(2)}, u32[]{:S(2)}) collective-permute-start(bf16[80,512]{1,0:T(8,128)(2,1)} %get-tuple-element.46), channel_id=1, source_target_pairs={{0,8},{8,0},{16,24},{24,16},{32,40},{40,32},{48,56},{56,48},{64,72... | collective-permute-start | bytes 245768 | tf_op jit(solution)/shard_map/ppermute | solution.py:514
  69.9 2.2 %collective-permute-done.4.next_got = bf16[80,512]{1,0:T(8,128)(2,1)S(1)} collective-permute-done((bf16[80,512]{1,0:T(8,128)(2,1)}, bf16[80,512]{1,0:T(8,128)(2,1)S(1)}, u32[]{:S(2)}, u32[]{:S(2)}) %collective-permute-start.4) | collective-permute-done | bytes 81952 | tf_op jit(solution)/shard_map/ppermute | solution.py:513
  72.1 0.9 copy-done.1
  73.0 0.1 shard_map.141.refs_0_
  73.2 7.3 %collective-permute-start.7 = (bf16[64,2048]{1,0:T(8,128)(2,1)S(1)}, bf16[64,2048]{1,0:T(8,128)(2,1)S(1)}, u32[]{:S(2)}, u32[]{:S(2)}) collective-permute-start(bf16[64,2048]{1,0:T(8,128)(2,1)S(1)} %shard_map.141.refs_0_), channel_id=1, source_target_pairs={{0,112},{8,120},{16,0},{24,8},{32,16},{40,24},{48,32},{56,40},{64,... | collective-permute-start | bytes 786440 | tf_op jit(solution)/shard_map/ppermute | solution.py:540
  80.5 1.9 %collective-permute-start.6 = (bf16[64,2048]{1,0:T(8,128)(2,1)S(1)}, bf16[64,2048]{1,0:T(8,128)(2,1)S(1)}, u32[]{:S(2)}, u32[]{:S(2)}) collective-permute-start(bf16[64,2048]{1,0:T(8,128)(2,1)S(1)} %shard_map.141.refs_0_), channel_id=1, source_target_pairs={{0,16},{8,24},{16,32},{24,40},{32,48},{40,56},{48,64},{56,72},{64,... | collective-permute-start | bytes 786440 | tf_op jit(solution)/shard_map/ppermute | solution.py:538
  82.4 3.4 %collective-permute-done.7.refs_2_ = bf16[64,2048]{1,0:T(8,128)(2,1)S(1)} collective-permute-done((bf16[64,2048]{1,0:T(8,128)(2,1)S(1)}, bf16[64,2048]{1,0:T(8,128)(2,1)S(1)}, u32[]{:S(2)}, u32[]{:S(2)}) %collective-permute-start.7) | collective-permute-done | bytes 262176 | tf_op jit(solution)/shard_map/ppermute | solution.py:540
  85.8 5.6 %collective-permute-start.8 = (bf16[64,2048]{1,0:T(8,128)(2,1)S(1)}, bf16[64,2048]{1,0:T(8,128)(2,1)S(1)}, u32[]{:S(2)}, u32[]{:S(2)}) collective-permute-start(bf16[64,2048]{1,0:T(8,128)(2,1)S(1)} %collective-permute-done.7.refs_2_), channel_id=1, source_target_pairs={{0,112},{8,120},{16,0},{24,8},{32,16},{40,24},{48,32},{56,40},{64,... | collective-permute-start | bytes 786440 | tf_op jit(solution)/shard_map/ppermute | solution.py:540
  91.4 0.0 all-gather.5.cloned.1.call-done
  91.5 1.9 %collective-permute-start.9 = (bf16[64,2048]{1,0:T(8,128)(2,1)S(1)}, bf16[64,2048]{1,0:T(8,128)(2,1)S(1)}, u32[]{:S(2)}, u32[]{:S(2)}) collective-permute-start(bf16[64,2048]{1,0:T(8,128)(2,1)S(1)} %collective-permute-done.6.refs_1_), channel_id=1, source_target_pairs={{0,16},{8,24},{16,32},{24,40},{32,48},{40,56},{48,64},{56,72},{64,... | collective-permute-start | bytes 786440 | tf_op jit(solution)/shard_map/ppermute | solution.py:538
  93.4 2.2 %shard_map.142.refs_4_.refs_2_ = bf16[4,1024,512]{2,1,0:T(8,128)(2,1)S(1)} custom-call(bf16[4,1024,512]{2,1,0:T(8,128)(2,1)} %bitcast.20), custom_call_target="tpu_custom_call" | custom-call | bytes 8388608 | tf_op jit(solution)/shard_map/pallas_call | solution.py:524
  95.6 0.3 collective-permute-done.8.refs_3_
  95.9 2.1 %shard_map.143.refs_0_ = bf16[4,5,16,1024]{3,2,1,0:T(8,128)(2,1)} custom-call(bf16[64,2048]{1,0:T(8,128)(2,1)S(1)} %shard_map.141.refs_0_, bf16[64,2048]{1,0:T(8,128)(2,1)S(1)} %collective-permute-done.6.refs_1_, bf16[64,2048]{1,0:T(8,128)(2,1)S(1)} %collective-permute-done.7.refs_2_, bf16[64,2048]{1,0:T(8,128)(2,1)S(1)} %collective-permute-done.8.refs_3_, ...), custom_call_target="tpu_custom_call" | custom-call | flops 1080000000 | bytes 6291456 | tf_op jit(solution)/shard_map/pallas_call | solution.py:358
  98.0 3.2 %collective-permute-done.9.refs_1_ = bf16[64,2048]{1,0:T(8,128)(2,1)S(1)} collective-permute-done((bf16[64,2048]{1,0:T(8,128)(2,1)S(1)}, bf16[64,2048]{1,0:T(8,128)(2,1)S(1)}, u32[]{:S(2)}, u32[]{:S(2)}) %collective-permute-start.9) | collective-permute-done | bytes 262176 | tf_op jit(solution)/shard_map/ppermute | solution.py:538
  101.2 1.6 shard_map.144
  102.9 1.9 %collective-permute-start.10 = (bf16[64,2048]{1,0:T(8,128)(2,1)S(1)}, bf16[64,2048]{1,0:T(8,128)(2,1)S(1)}, u32[]{:S(2)}, u32[]{:S(2)}) collective-permute-start(bf16[64,2048]{1,0:T(8,128)(2,1)S(1)} %collective-permute-done.9.refs_1_), channel_id=1, source_target_pairs={{0,16},{8,24},{16,32},{24,40},{32,48},{40,56},{48,64},{56,72},{64,... | collective-permute-start | bytes 786440 | tf_op jit(solution)/shard_map/ppermute | solution.py:538
  104.8 5.1 %collective-permute-start.11 = (bf16[64,2048]{1,0:T(8,128)(2,1)S(1)}, bf16[64,2048]{1,0:T(8,128)(2,1)S(1)}, u32[]{:S(2)}, u32[]{:S(2)}) collective-permute-start(bf16[64,2048]{1,0:T(8,128)(2,1)S(1)} %collective-permute-done.8.refs_3_), channel_id=1, source_target_pairs={{0,112},{8,120},{16,0},{24,8},{32,16},{40,24},{48,32},{56,40},{64,... | collective-permute-start | bytes 786440 | tf_op jit(solution)/shard_map/ppermute | solution.py:540
  109.9 2.4 %collective-permute-done.10.refs_0_ = bf16[64,2048]{1,0:T(8,128)(2,1)S(1)} collective-permute-done((bf16[64,2048]{1,0:T(8,128)(2,1)S(1)}, bf16[64,2048]{1,0:T(8,128)(2,1)S(1)}, u32[]{:S(2)}, u32[]{:S(2)}) %collective-permute-start.10) | collective-permute-done | bytes 262176 | tf_op jit(solution)/shard_map/ppermute | solution.py:538
  112.3 1.9 %collective-permute-start.12 = (bf16[64,2048]{1,0:T(8,128)(2,1)S(1)}, bf16[64,2048]{1,0:T(8,128)(2,1)S(1)}, u32[]{:S(2)}, u32[]{:S(2)}) collective-permute-start(bf16[64,2048]{1,0:T(8,128)(2,1)S(1)} %collective-permute-done.10.refs_0_), channel_id=1, source_target_pairs={{0,16},{8,24},{16,32},{24,40},{32,48},{40,56},{48,64},{56,72},{64,... | collective-permute-start | bytes 786440 | tf_op jit(solution)/shard_map/ppermute | solution.py:538
  114.3 2.2 %shard_map.145.refs_3_ = bf16[4,1024,512]{2,1,0:T(8,128)(2,1)S(1)} custom-call(bf16[4,1024,512]{2,1,0:T(8,128)(2,1)} %bitcast.21), custom_call_target="tpu_custom_call" | custom-call | bytes 8388608 | tf_op jit(solution)/shard_map/pallas_call | solution.py:524
  116.5 5.3 %collective-permute-done.12.refs_2_ = bf16[64,2048]{1,0:T(8,128)(2,1)S(1)} collective-permute-done((bf16[64,2048]{1,0:T(8,128)(2,1)S(1)}, bf16[64,2048]{1,0:T(8,128)(2,1)S(1)}, u32[]{:S(2)}, u32[]{:S(2)}) %collective-permute-start.12) | collective-permute-done | bytes 262176 | tf_op jit(solution)/shard_map/ppermute | solution.py:538
  121.8 1.3 shard_map.146
  123.1 17.8 %all_to_all.21 = bf16[4,48,1024]{2,1,0:T(8,128)(2,1)S(1)} all-to-all(bf16[4,48,1024]{2,1,0:T(8,128)(2,1)S(1)} %bitcast.18), channel_id=1, replica_groups={{0,2,4,6},{1,3,5,7},{8,10,12,14},{9,11,13,15},{16,18,20,22},{17,19,21,2..., dimensions={0} | all-to-all | bytes 786432 | tf_op jit(solution)/shard_map/all_to_all | solution.py:551
  140.8 0.9 copy-done
  141.7 0.3 shard_map.147
  142.0 12.3 %all_to_all.22 = bf16[8,16,1024]{2,1,0:T(8,128)(2,1)S(1)} all-to-all(bf16[8,16,1024]{2,1,0:T(8,128)(2,1)S(1)} %shard_map.147), channel_id=1, replica_groups={{112,96,80,64,48,32,16,0},{120,104,88,72,56,40,24,8},{113,97,81,65,49,3..., dimensions={0} | all-to-all | bytes 524288 | tf_op jit(solution)/shard_map/all_to_all | solution.py:561
  154.3 0.7 copy.17
  (17 shorter events, 0.1 us)
Async XLA Ops:
  6.5 52.8 %all-gather.3.cloned.1.call-start = ((), (), s32[]{:S(2)}) async-start(), calls=%async_computation.5 | async-start | bytes 3145728 | tf_op jit(solution)/shard_map/all_gather | solution.py:397
  9.8 3.9 %collective-permute-start = (bf16[128,1664]{1,0:T(8,128)(2,1)}, bf16[128,1664]{1,0:T(8,128)(2,1)S(1)}, u32[]{:S(2)}, u32[]{:S(2)}) collective-permute-start(bf16[128,1664]{1,0:T(8,128)(2,1)} %get-tuple-element.30.sent_in), channel_id=1, source_target_pairs={{0,8},{8,0},{16,24},{24,16},{32,40},{40,32},{48,56},{56,48},{64,72... | collective-permute-start | bytes 1277960 | tf_op jit(solution)/shard_map/ppermute | solution.py:427
  11.7 1.3 collective-permute-start.1
  12.4 0.7 collective-permute-start.2
  13.0 0.6 copy-start.3
  13.1 0.6 copy-start.4
  13.6 0.8 copy-start.2
  19.6 27.5 %all-to-all-start = ((bf16[8,80,256]{2,1,0:T(8,128)(2,1)}), bf16[8,80,256]{2,1,0:T(8,128)(2,1)S(1)}, u32[]{:S(2)}, u32[]{:S(2)}) async-start(bf16[8,80,256]{2,1,0:T(8,128)(2,1)} %get-tuple-element.34), calls=%async_computation | async-start | bytes 655360 | tf_op jit(solution)/shard_map/all_to_all | solution.py:460
  34.7 56.8 %all-gather.5.cloned.1.call-start = ((), (), s32[]{:S(2)}) async-start(), calls=%async_computation.6 | async-start | bytes 6291456 | tf_op jit(solution)/shard_map/all_gather | solution.py:491
  59.4 81.4 %reduce-scatter.2.cloned.1.call-start = ((), (), s32[]{:S(2)}) async-start(), calls=%async_computation.7 | async-start | bytes 819200 | tf_op jit(solution)/shard_map/reduce_scatter | solution.py:547
  61.8 8.0 %collective-permute-start.3 = (bf16[80,512]{1,0:T(8,128)(2,1)}, bf16[80,512]{1,0:T(8,128)(2,1)S(1)}, u32[]{:S(2)}, u32[]{:S(2)}) collective-permute-start(bf16[80,512]{1,0:T(8,128)(2,1)} %get-tuple-element.44), channel_id=1, source_target_pairs={{0,9},{1,8},{2,11},{3,10},{4,13},{5,12},{6,15},{7,14},{8,1},{9,0},... | collective-permute-start | bytes 245768 | tf_op jit(solution)/shard_map/ppermute | solution.py:512
  65.6 6.5 %collective-permute-start.4 = (bf16[80,512]{1,0:T(8,128)(2,1)}, bf16[80,512]{1,0:T(8,128)(2,1)S(1)}, u32[]{:S(2)}, u32[]{:S(2)}) collective-permute-start(bf16[80,512]{1,0:T(8,128)(2,1)} %get-tuple-element.45), channel_id=1, source_target_pairs={{0,1},{1,0},{2,3},{3,2},{4,5},{5,4},{6,7},{7,6},{8,9},{9,8},{10,11... | collective-permute-start | bytes 245768 | tf_op jit(solution)/shard_map/ppermute | solution.py:513
  67.9 4.2 %collective-permute-start.5 = (bf16[80,512]{1,0:T(8,128)(2,1)}, bf16[80,512]{1,0:T(8,128)(2,1)S(1)}, u32[]{:S(2)}, u32[]{:S(2)}) collective-permute-start(bf16[80,512]{1,0:T(8,128)(2,1)} %get-tuple-element.46), channel_id=1, source_target_pairs={{0,8},{8,0},{16,24},{24,16},{32,40},{40,32},{48,56},{56,48},{64,72... | collective-permute-start | bytes 245768 | tf_op jit(solution)/shard_map/ppermute | solution.py:514
  72.1 0.9 copy-start.1
  73.2 12.7 %collective-permute-start.7 = (bf16[64,2048]{1,0:T(8,128)(2,1)S(1)}, bf16[64,2048]{1,0:T(8,128)(2,1)S(1)}, u32[]{:S(2)}, u32[]{:S(2)}) collective-permute-start(bf16[64,2048]{1,0:T(8,128)(2,1)S(1)} %shard_map.141.refs_0_), channel_id=1, source_target_pairs={{0,112},{8,120},{16,0},{24,8},{32,16},{40,24},{48,32},{56,40},{64,... | collective-permute-start | bytes 786440 | tf_op jit(solution)/shard_map/ppermute | solution.py:540
  80.5 10.9 %collective-permute-start.6 = (bf16[64,2048]{1,0:T(8,128)(2,1)S(1)}, bf16[64,2048]{1,0:T(8,128)(2,1)S(1)}, u32[]{:S(2)}, u32[]{:S(2)}) collective-permute-start(bf16[64,2048]{1,0:T(8,128)(2,1)S(1)} %shard_map.141.refs_0_), channel_id=1, source_target_pairs={{0,16},{8,24},{16,32},{24,40},{32,48},{40,56},{48,64},{56,72},{64,... | collective-permute-start | bytes 786440 | tf_op jit(solution)/shard_map/ppermute | solution.py:538
  85.8 10.0 %collective-permute-start.8 = (bf16[64,2048]{1,0:T(8,128)(2,1)S(1)}, bf16[64,2048]{1,0:T(8,128)(2,1)S(1)}, u32[]{:S(2)}, u32[]{:S(2)}) collective-permute-start(bf16[64,2048]{1,0:T(8,128)(2,1)S(1)} %collective-permute-done.7.refs_2_), channel_id=1, source_target_pairs={{0,112},{8,120},{16,0},{24,8},{32,16},{40,24},{48,32},{56,40},{64,... | collective-permute-start | bytes 786440 | tf_op jit(solution)/shard_map/ppermute | solution.py:540
  91.5 9.8 %collective-permute-start.9 = (bf16[64,2048]{1,0:T(8,128)(2,1)S(1)}, bf16[64,2048]{1,0:T(8,128)(2,1)S(1)}, u32[]{:S(2)}, u32[]{:S(2)}) collective-permute-start(bf16[64,2048]{1,0:T(8,128)(2,1)S(1)} %collective-permute-done.6.refs_1_), channel_id=1, source_target_pairs={{0,16},{8,24},{16,32},{24,40},{32,48},{40,56},{48,64},{56,72},{64,... | collective-permute-start | bytes 786440 | tf_op jit(solution)/shard_map/ppermute | solution.py:538
  102.9 9.5 %collective-permute-start.10 = (bf16[64,2048]{1,0:T(8,128)(2,1)S(1)}, bf16[64,2048]{1,0:T(8,128)(2,1)S(1)}, u32[]{:S(2)}, u32[]{:S(2)}) collective-permute-start(bf16[64,2048]{1,0:T(8,128)(2,1)S(1)} %collective-permute-done.9.refs_1_), channel_id=1, source_target_pairs={{0,16},{8,24},{16,32},{24,40},{32,48},{40,56},{48,64},{56,72},{64,... | collective-permute-start | bytes 786440 | tf_op jit(solution)/shard_map/ppermute | solution.py:538
  104.8 11.7 %collective-permute-start.11 = (bf16[64,2048]{1,0:T(8,128)(2,1)S(1)}, bf16[64,2048]{1,0:T(8,128)(2,1)S(1)}, u32[]{:S(2)}, u32[]{:S(2)}) collective-permute-start(bf16[64,2048]{1,0:T(8,128)(2,1)S(1)} %collective-permute-done.8.refs_3_), channel_id=1, source_target_pairs={{0,112},{8,120},{16,0},{24,8},{32,16},{40,24},{48,32},{56,40},{64,... | collective-permute-start | bytes 786440 | tf_op jit(solution)/shard_map/ppermute | solution.py:540
  112.3 9.5 %collective-permute-start.12 = (bf16[64,2048]{1,0:T(8,128)(2,1)S(1)}, bf16[64,2048]{1,0:T(8,128)(2,1)S(1)}, u32[]{:S(2)}, u32[]{:S(2)}) collective-permute-start(bf16[64,2048]{1,0:T(8,128)(2,1)S(1)} %collective-permute-done.10.refs_0_), channel_id=1, source_target_pairs={{0,16},{8,24},{16,32},{24,40},{32,48},{40,56},{48,64},{56,72},{64,... | collective-permute-start | bytes 786440 | tf_op jit(solution)/shard_map/ppermute | solution.py:538
  140.8 0.9 copy-start
Sparse Core Ops, SparseCore 0:
  9.4 45.6 all-gather.2
  59.5 22.9 all-gather.4
  103.0 26.7 reduce-scatter.1

commit v7 on v6

--- a/solution.py
+++ b/solution.py
@@ -543,7 +543,9 @@
     near = product([blocks[r] for r in NEAR[:-1]], near_weights, len(NEAR))
     near = product([blocks[NEAR[-1]]], near_weights, len(NEAR), len(NEAR) - 1, near)
     blocks[3], weights = lax.optimization_barrier((blocks[3], weights))
-    far = product([blocks[r] for r in FAR], staged(weights), len(FAR))
+    far_weights = staged(weights)
+    far = product([blocks[r] for r in FAR[:-1]], far_weights, len(FAR))
+    far = product([blocks[FAR[-1]]], far_weights, len(FAR), len(FAR) - 1, far)
     near = lax.psum_scatter(
         near.reshape(4 * 16 * len(NEAR), 1024), "tensor",
         scatter_dimension=0, tiled=True, axis_index_groups=PARITY,

time: 162 us -> 162 us (level)
  the two profiles are of different devices: /device:TPU:2 before, /device:TPU:16 now
where the time goes in v7:
time: 162 us; the launch traced here: 161 us
  starting transfers between devices  52.1 us (32%)
  blocking collectives  42.3 us (26%)
  waiting for transfers between devices  25.5 us (16%)
  Pallas kernels  24 us (15%)
  between operations  13.4 us (8%)
  local copies, waits for them, and re-layouts  4.16 us (3%)
    ppermute x3, starting transfers between devices, body(): down.append(lax.ppermute(down[-1], 'context', DOWN))  18 us
    all_to_all x1, blocking collectives, body(): lax.all_to_all(far.reshape(4, 16 * len(FAR), 1024), 'tensor', 0, 0, tiled...  16.1 us
    all_to_all x1, starting transfers between devices, body(): lax.all_to_all(added, 'context', 0, 0, tiled=True, axis_index_groups=SAME...  15 us
    all_to_all x1, blocking collectives, body(): lax.all_to_all(ready, 'context', 0, 0, tiled=True, axis_index_groups=BACK...  14 us
    all_to_all x1, blocking collectives, body(): lax.all_to_all(states, 'context', 0, 0, tiled=True, axis_index_groups=BAC...  12.1 us
    ppermute x4, waiting for transfers between devices, body(): up.append(lax.ppermute(up[-1], 'context', UP))  9.99 us
    all_to_all x1, waiting for transfers between devices, body(): lax.all_to_all(added, 'context', 0, 0, tiled=True, axis_index_groups=SAME...  8.28 us
    ppermute x4, starting transfers between devices, body(): up.append(lax.ppermute(up[-1], 'context', UP))  7.67 us
  transfers between devices with their start and end apart: 17, of which 8 were waited for; matrix products, arithmetic and copies ran while one was open for 1% of the time, Pallas kernels for 14%

profile of v7, /device:TPU:16, one launch (start us, length us, event | category | flops | bytes accessed | tf_op | source)
XLA Modules:
  0.0 161.4 jit_solution(1670745548668428378)
XLA Ops:
  6.5 0.7 all-gather.3.cloned.1.call-update
  7.3 2.5 %shard_map.136 = (bf16[128,1664]{1,0:T(8,128)(2,1)}, bf16[16,1024]{1,0:T(8,128)(2,1)}, bf16[16,1024]{1,0:T(8,128)(2,1)}, bf16[128,512]{1,0:T(8,128)(2,1)}, f32[32,1024]{1,0:T(8,128)}) custom-call(bf16[128,1024]{1,0:T(8,128)(2,1)} %xs.1, bf16[128,1024]{1,0:T(8,128)(2,1)} %zs.3, bf16[128,2,256]{2,1,0:T(2,128)(2,1)} %bcs.1, bf16[16,128]{1,0:T(8,128)(2,1)} %bitcast.23, ...), custom_call_target="tpu_custom_call" | custom-call | bytes 1048576 | tf_op jit(solution)/shard_map/pallas_call | solution.py:398
  9.8 1.9 %collective-permute-start = (bf16[128,1664]{1,0:T(8,128)(2,1)}, bf16[128,1664]{1,0:T(8,128)(2,1)S(1)}, u32[]{:S(2)}, u32[]{:S(2)}) collective-permute-start(bf16[128,1664]{1,0:T(8,128)(2,1)} %get-tuple-element.30.sent_in), channel_id=1, source_target_pairs={{0,8},{8,0},{16,24},{24,16},{32,40},{40,32},{48,56},{56,48},{64,72... | collective-permute-start | bytes 1277960 | tf_op jit(solution)/shard_map/ppermute | solution.py:427
  11.7 0.7 collective-permute-start.1
  12.4 0.7 collective-permute-start.2
  13.1 0.6 collective-permute-done.got_in.got
  13.6 0.0 copy-done.3
  13.7 0.7 copy-done.2
  14.4 5.2 %shard_map.137 = (bf16[8,80,256]{2,1,0:T(8,128)(2,1)}, bf16[256,512]{1,0:T(8,128)(2,1)}, bf16[256,512]{1,0:T(8,128)(2,1)}, f32[256,128]{1,0:T(8,128)}, f32[256,128]{1,0:T(8,128)}) custom-call(bf16[128,512]{1,0:T(8,128)(2,1)} %get-tuple-element.29.xs_in, bf16[128,1664]{1,0:T(8,128)(2,1)} %get-tuple-element.30.sent_in, bf16[128,1664]{1,0:T(8,128)(2,1)} %copy-done.2, ...), custom_call_target="tpu_custom_call" | custom-call | flops 200000000 | bytes 2097152 | tf_op jit(solution)/shard_map/pallas_call | solution.py:430
  19.7 15.0 %all-to-all-start = ((bf16[8,80,256]{2,1,0:T(8,128)(2,1)}), bf16[8,80,256]{2,1,0:T(8,128)(2,1)S(1)}, u32[]{:S(2)}, u32[]{:S(2)}) async-start(bf16[8,80,256]{2,1,0:T(8,128)(2,1)} %get-tuple-element.34), calls=%async_computation | async-start | bytes 655360 | tf_op jit(solution)/shard_map/all_to_all | solution.py:460
  34.7 0.0 all-gather.5.cloned.1.call-start
  34.7 0.8 dynamic-slice_bitcast_fusion.first
  35.6 3.3 %shard_map.138 = (f32[256,512]{1,0:T(8,128)}, f32[256,512]{1,0:T(8,128)}) custom-call(bf16[256,512]{1,0:T(8,128)(2,1)} %get-tuple-element.35.x_in, bf16[256,512]{1,0:T(8,128)(2,1)} %get-tuple-element.36.bc_in, f32[256,128]{1,0:T(8,128)} %get-tuple-element.37.cum_in, f32[256,128]{1,0:T(8,128)} %get-tuple-element.38.delta_in, f32[1,16]{1,0:T(1,128)} %bitcast.27, ...), custom_call_target="tpu_custom_call" | custom-call | flops 400000000 | bytes 2097152 | tf_op jit(solution)/shard_map/pallas_call | solution.py:461
  38.9 8.3 %all-to-all-done.got = bf16[8,80,256]{2,1,0:T(8,128)(2,1)S(1)} async-done(((bf16[8,80,256]{2,1,0:T(8,128)(2,1)}), bf16[8,80,256]{2,1,0:T(8,128)(2,1)S(1)}, u32[]{:S(2)}, u32[]{:S(2)}) %all-to-all-start) | async-done | bytes 327712 | tf_op jit(solution)/shard_map/all_to_all | solution.py:460
  47.2 0.1 shard_map.139
  47.3 12.1 %all_to_all.20 = bf16[8,64,256]{2,1,0:T(8,128)(2,1)} all-to-all(bf16[8,64,256]{2,1,0:T(8,128)(2,1)S(1)} %shard_map.139), channel_id=1, replica_groups={{112,96,80,64,48,32,16,0},{120,104,88,72,56,40,24,8},{113,97,81,65,49,3..., dimensions={0} | all-to-all | bytes 524288 | tf_op jit(solution)/shard_map/all_to_all | solution.py:489
  59.4 0.0 reduce-scatter.2.cloned.1.call-start
  59.4 2.4 %shard_map.140 = (bf16[80,512]{1,0:T(8,128)(2,1)}, bf16[80,512]{1,0:T(8,128)(2,1)}, bf16[80,512]{1,0:T(8,128)(2,1)}, bf16[80,512]{1,0:T(8,128)(2,1)}) custom-call(bf16[512,256]{1,0:T(8,128)(2,1)} %bitcast.22, bf16[256,512]{1,0:T(8,128)(2,1)} %get-tuple-element.36.bc_in, f32[256,512]{1,0:T(8,128)} %get-tuple-element.42.inside_in, ...), custom_call_target="tpu_custom_call" | custom-call | flops 100000000 | bytes 2097152 | tf_op jit(solution)/shard_map/pallas_call | solution.py:494
  61.8 3.7 %collective-permute-start.3 = (bf16[80,512]{1,0:T(8,128)(2,1)}, bf16[80,512]{1,0:T(8,128)(2,1)S(1)}, u32[]{:S(2)}, u32[]{:S(2)}) collective-permute-start(bf16[80,512]{1,0:T(8,128)(2,1)} %get-tuple-element.44), channel_id=1, source_target_pairs={{0,9},{1,8},{2,11},{3,10},{4,13},{5,12},{6,15},{7,14},{8,1},{9,0},... | collective-permute-start | bytes 245768 | tf_op jit(solution)/shard_map/ppermute | solution.py:512
  65.6 2.4 %collective-permute-start.4 = (bf16[80,512]{1,0:T(8,128)(2,1)}, bf16[80,512]{1,0:T(8,128)(2,1)S(1)}, u32[]{:S(2)}, u32[]{:S(2)}) collective-permute-start(bf16[80,512]{1,0:T(8,128)(2,1)} %get-tuple-element.45), channel_id=1, source_target_pairs={{0,1},{1,0},{2,3},{3,2},{4,5},{5,4},{6,7},{7,6},{8,9},{9,8},{10,11... | collective-permute-start | bytes 245768 | tf_op jit(solution)/shard_map/ppermute | solution.py:513
  67.9 1.9 %collective-permute-start.5 = (bf16[80,512]{1,0:T(8,128)(2,1)}, bf16[80,512]{1,0:T(8,128)(2,1)S(1)}, u32[]{:S(2)}, u32[]{:S(2)}) collective-permute-start(bf16[80,512]{1,0:T(8,128)(2,1)} %get-tuple-element.46), channel_id=1, source_target_pairs={{0,8},{8,0},{16,24},{24,16},{32,40},{40,32},{48,56},{56,48},{64,72... | collective-permute-start | bytes 245768 | tf_op jit(solution)/shard_map/ppermute | solution.py:514
  69.9 2.2 %collective-permute-done.4.next_got = bf16[80,512]{1,0:T(8,128)(2,1)S(1)} collective-permute-done((bf16[80,512]{1,0:T(8,128)(2,1)}, bf16[80,512]{1,0:T(8,128)(2,1)S(1)}, u32[]{:S(2)}, u32[]{:S(2)}) %collective-permute-start.4) | collective-permute-done | bytes 81952 | tf_op jit(solution)/shard_map/ppermute | solution.py:513
  72.1 0.9 copy-done.1
  73.0 0.1 shard_map.141.refs_0_
  73.2 7.3 %collective-permute-start.7 = (bf16[64,2048]{1,0:T(8,128)(2,1)S(1)}, bf16[64,2048]{1,0:T(8,128)(2,1)S(1)}, u32[]{:S(2)}, u32[]{:S(2)}) collective-permute-start(bf16[64,2048]{1,0:T(8,128)(2,1)S(1)} %shard_map.141.refs_0_), channel_id=1, source_target_pairs={{0,112},{8,120},{16,0},{24,8},{32,16},{40,24},{48,32},{56,40},{64,... | collective-permute-start | bytes 786440 | tf_op jit(solution)/shard_map/ppermute | solution.py:540
  80.5 1.9 %collective-permute-start.6 = (bf16[64,2048]{1,0:T(8,128)(2,1)S(1)}, bf16[64,2048]{1,0:T(8,128)(2,1)S(1)}, u32[]{:S(2)}, u32[]{:S(2)}) collective-permute-start(bf16[64,2048]{1,0:T(8,128)(2,1)S(1)} %shard_map.141.refs_0_), channel_id=1, source_target_pairs={{0,16},{8,24},{16,32},{24,40},{32,48},{40,56},{48,64},{56,72},{64,... | collective-permute-start | bytes 786440 | tf_op jit(solution)/shard_map/ppermute | solution.py:538
  82.4 3.4 %collective-permute-done.7.refs_2_ = bf16[64,2048]{1,0:T(8,128)(2,1)S(1)} collective-permute-done((bf16[64,2048]{1,0:T(8,128)(2,1)S(1)}, bf16[64,2048]{1,0:T(8,128)(2,1)S(1)}, u32[]{:S(2)}, u32[]{:S(2)}) %collective-permute-start.7) | collective-permute-done | bytes 262176 | tf_op jit(solution)/shard_map/ppermute | solution.py:540
  85.8 5.6 %collective-permute-start.8 = (bf16[64,2048]{1,0:T(8,128)(2,1)S(1)}, bf16[64,2048]{1,0:T(8,128)(2,1)S(1)}, u32[]{:S(2)}, u32[]{:S(2)}) collective-permute-start(bf16[64,2048]{1,0:T(8,128)(2,1)S(1)} %collective-permute-done.7.refs_2_), channel_id=1, source_target_pairs={{0,112},{8,120},{16,0},{24,8},{32,16},{40,24},{48,32},{56,40},{64,... | collective-permute-start | bytes 786440 | tf_op jit(solution)/shard_map/ppermute | solution.py:540
  91.4 0.0 all-gather.5.cloned.1.call-done
  91.5 1.9 %collective-permute-start.9 = (bf16[64,2048]{1,0:T(8,128)(2,1)S(1)}, bf16[64,2048]{1,0:T(8,128)(2,1)S(1)}, u32[]{:S(2)}, u32[]{:S(2)}) collective-permute-start(bf16[64,2048]{1,0:T(8,128)(2,1)S(1)} %collective-permute-done.6.refs_1_), channel_id=1, source_target_pairs={{0,16},{8,24},{16,32},{24,40},{32,48},{40,56},{48,64},{56,72},{64,... | collective-permute-start | bytes 786440 | tf_op jit(solution)/shard_map/ppermute | solution.py:538
  93.4 2.2 %shard_map.142.refs_4_.refs_2_ = bf16[4,1024,512]{2,1,0:T(8,128)(2,1)S(1)} custom-call(bf16[4,1024,512]{2,1,0:T(8,128)(2,1)} %bitcast.20), custom_call_target="tpu_custom_call" | custom-call | bytes 8388608 | tf_op jit(solution)/shard_map/pallas_call | solution.py:524
  95.6 0.3 collective-permute-done.8.refs_3_
  95.9 2.1 %shard_map.143.refs_0_ = bf16[4,5,16,1024]{3,2,1,0:T(8,128)(2,1)} custom-call(bf16[64,2048]{1,0:T(8,128)(2,1)S(1)} %shard_map.141.refs_0_, bf16[64,2048]{1,0:T(8,128)(2,1)S(1)} %collective-permute-done.6.refs_1_, bf16[64,2048]{1,0:T(8,128)(2,1)S(1)} %collective-permute-done.7.refs_2_, bf16[64,2048]{1,0:T(8,128)(2,1)S(1)} %collective-permute-done.8.refs_3_, ...), custom_call_target="tpu_custom_call" | custom-call | flops 1080000000 | bytes 6291456 | tf_op jit(solution)/shard_map/pallas_call | solution.py:358
  98.0 3.2 %collective-permute-done.9.refs_1_ = bf16[64,2048]{1,0:T(8,128)(2,1)S(1)} collective-permute-done((bf16[64,2048]{1,0:T(8,128)(2,1)S(1)}, bf16[64,2048]{1,0:T(8,128)(2,1)S(1)}, u32[]{:S(2)}, u32[]{:S(2)}) %collective-permute-start.9) | collective-permute-done | bytes 262176 | tf_op jit(solution)/shard_map/ppermute | solution.py:538
  101.2 1.6 shard_map.144
  102.9 1.9 %collective-permute-start.10 = (bf16[64,2048]{1,0:T(8,128)(2,1)S(1)}, bf16[64,2048]{1,0:T(8,128)(2,1)S(1)}, u32[]{:S(2)}, u32[]{:S(2)}) collective-permute-start(bf16[64,2048]{1,0:T(8,128)(2,1)S(1)} %collective-permute-done.9.refs_1_), channel_id=1, source_target_pairs={{0,16},{8,24},{16,32},{24,40},{32,48},{40,56},{48,64},{56,72},{64,... | collective-permute-start | bytes 786440 | tf_op jit(solution)/shard_map/ppermute | solution.py:538
  104.8 5.1 %collective-permute-start.11 = (bf16[64,2048]{1,0:T(8,128)(2,1)S(1)}, bf16[64,2048]{1,0:T(8,128)(2,1)S(1)}, u32[]{:S(2)}, u32[]{:S(2)}) collective-permute-start(bf16[64,2048]{1,0:T(8,128)(2,1)S(1)} %collective-permute-done.8.refs_3_), channel_id=1, source_target_pairs={{0,112},{8,120},{16,0},{24,8},{32,16},{40,24},{48,32},{56,40},{64,... | collective-permute-start | bytes 786440 | tf_op jit(solution)/shard_map/ppermute | solution.py:540
  109.9 2.4 %collective-permute-done.10.refs_0_ = bf16[64,2048]{1,0:T(8,128)(2,1)S(1)} collective-permute-done((bf16[64,2048]{1,0:T(8,128)(2,1)S(1)}, bf16[64,2048]{1,0:T(8,128)(2,1)S(1)}, u32[]{:S(2)}, u32[]{:S(2)}) %collective-permute-start.10) | collective-permute-done | bytes 262176 | tf_op jit(solution)/shard_map/ppermute | solution.py:538
  112.3 1.9 %collective-permute-start.12 = (bf16[64,2048]{1,0:T(8,128)(2,1)S(1)}, bf16[64,2048]{1,0:T(8,128)(2,1)S(1)}, u32[]{:S(2)}, u32[]{:S(2)}) collective-permute-start(bf16[64,2048]{1,0:T(8,128)(2,1)S(1)} %collective-permute-done.10.refs_0_), channel_id=1, source_target_pairs={{0,16},{8,24},{16,32},{24,40},{32,48},{40,56},{48,64},{56,72},{64,... | collective-permute-start | bytes 786440 | tf_op jit(solution)/shard_map/ppermute | solution.py:538
  114.3 2.2 %shard_map.145.refs_2_ = bf16[4,1024,512]{2,1,0:T(8,128)(2,1)S(1)} custom-call(bf16[4,1024,512]{2,1,0:T(8,128)(2,1)} %bitcast.21), custom_call_target="tpu_custom_call" | custom-call | bytes 8388608 | tf_op jit(solution)/shard_map/pallas_call | solution.py:524
  116.5 0.9 shard_map.146.refs_0_
  117.4 4.4 %collective-permute-done.12.refs_1_ = bf16[64,2048]{1,0:T(8,128)(2,1)S(1)} collective-permute-done((bf16[64,2048]{1,0:T(8,128)(2,1)S(1)}, bf16[64,2048]{1,0:T(8,128)(2,1)S(1)}, u32[]{:S(2)}, u32[]{:S(2)}) %collective-permute-start.12) | collective-permute-done | bytes 262176 | tf_op jit(solution)/shard_map/ppermute | solution.py:538
  121.8 1.0 shard_map.147
  122.8 16.1 %all_to_all.21 = bf16[4,48,1024]{2,1,0:T(8,128)(2,1)S(1)} all-to-all(bf16[4,48,1024]{2,1,0:T(8,128)(2,1)S(1)} %bitcast.17), channel_id=1, replica_groups={{0,2,4,6},{1,3,5,7},{8,10,12,14},{9,11,13,15},{16,18,20,22},{17,19,21,2..., dimensions={0} | all-to-all | bytes 786432 | tf_op jit(solution)/shard_map/all_to_all | solution.py:553
  138.9 0.9 copy-done
  139.9 0.3 shard_map.148
  140.1 14.0 %all_to_all.22 = bf16[8,16,1024]{2,1,0:T(8,128)(2,1)S(1)} all-to-all(bf16[8,16,1024]{2,1,0:T(8,128)(2,1)S(1)} %shard_map.148), channel_id=1, replica_groups={{112,96,80,64,48,32,16,0},{120,104,88,72,56,40,24,8},{113,97,81,65,49,3..., dimensions={0} | all-to-all | bytes 524288 | tf_op jit(solution)/shard_map/all_to_all | solution.py:563
  154.2 0.7 copy.18
  (18 shorter events, 0.1 us)
Async XLA Ops:
  6.5 52.8 %all-gather.3.cloned.1.call-start = ((), (), s32[]{:S(2)}) async-start(), calls=%async_computation.5 | async-start | bytes 3145728 | tf_op jit(solution)/shard_map/all_gather | solution.py:397
  9.8 3.9 %collective-permute-start = (bf16[128,1664]{1,0:T(8,128)(2,1)}, bf16[128,1664]{1,0:T(8,128)(2,1)S(1)}, u32[]{:S(2)}, u32[]{:S(2)}) collective-permute-start(bf16[128,1664]{1,0:T(8,128)(2,1)} %get-tuple-element.30.sent_in), channel_id=1, source_target_pairs={{0,8},{8,0},{16,24},{24,16},{32,40},{40,32},{48,56},{56,48},{64,72... | collective-permute-start | bytes 1277960 | tf_op jit(solution)/shard_map/ppermute | solution.py:427
  11.7 1.3 collective-permute-start.1
  12.4 0.7 collective-permute-start.2
  13.0 0.6 copy-start.3
  13.1 0.6 copy-start.4
  13.6 0.8 copy-start.2
  19.7 27.5 %all-to-all-start = ((bf16[8,80,256]{2,1,0:T(8,128)(2,1)}), bf16[8,80,256]{2,1,0:T(8,128)(2,1)S(1)}, u32[]{:S(2)}, u32[]{:S(2)}) async-start(bf16[8,80,256]{2,1,0:T(8,128)(2,1)} %get-tuple-element.34), calls=%async_computation | async-start | bytes 655360 | tf_op jit(solution)/shard_map/all_to_all | solution.py:460
  34.7 56.8 %all-gather.5.cloned.1.call-start = ((), (), s32[]{:S(2)}) async-start(), calls=%async_computation.6 | async-start | bytes 6291456 | tf_op jit(solution)/shard_map/all_gather | solution.py:491
  59.4 79.5 %reduce-scatter.2.cloned.1.call-start = ((), (), s32[]{:S(2)}) async-start(), calls=%async_computation.7 | async-start | bytes 819200 | tf_op jit(solution)/shard_map/reduce_scatter | solution.py:549
  61.8 8.0 %collective-permute-start.3 = (bf16[80,512]{1,0:T(8,128)(2,1)}, bf16[80,512]{1,0:T(8,128)(2,1)S(1)}, u32[]{:S(2)}, u32[]{:S(2)}) collective-permute-start(bf16[80,512]{1,0:T(8,128)(2,1)} %get-tuple-element.44), channel_id=1, source_target_pairs={{0,9},{1,8},{2,11},{3,10},{4,13},{5,12},{6,15},{7,14},{8,1},{9,0},... | collective-permute-start | bytes 245768 | tf_op jit(solution)/shard_map/ppermute | solution.py:512
  65.6 6.5 %collective-permute-start.4 = (bf16[80,512]{1,0:T(8,128)(2,1)}, bf16[80,512]{1,0:T(8,128)(2,1)S(1)}, u32[]{:S(2)}, u32[]{:S(2)}) collective-permute-start(bf16[80,512]{1,0:T(8,128)(2,1)} %get-tuple-element.45), channel_id=1, source_target_pairs={{0,1},{1,0},{2,3},{3,2},{4,5},{5,4},{6,7},{7,6},{8,9},{9,8},{10,11... | collective-permute-start | bytes 245768 | tf_op jit(solution)/shard_map/ppermute | solution.py:513
  67.9 4.2 %collective-permute-start.5 = (bf16[80,512]{1,0:T(8,128)(2,1)}, bf16[80,512]{1,0:T(8,128)(2,1)S(1)}, u32[]{:S(2)}, u32[]{:S(2)}) collective-permute-start(bf16[80,512]{1,0:T(8,128)(2,1)} %get-tuple-element.46), channel_id=1, source_target_pairs={{0,8},{8,0},{16,24},{24,16},{32,40},{40,32},{48,56},{56,48},{64,72... | collective-permute-start | bytes 245768 | tf_op jit(solution)/shard_map/ppermute | solution.py:514
  72.1 0.9 copy-start.1
  73.2 12.7 %collective-permute-start.7 = (bf16[64,2048]{1,0:T(8,128)(2,1)S(1)}, bf16[64,2048]{1,0:T(8,128)(2,1)S(1)}, u32[]{:S(2)}, u32[]{:S(2)}) collective-permute-start(bf16[64,2048]{1,0:T(8,128)(2,1)S(1)} %shard_map.141.refs_0_), channel_id=1, source_target_pairs={{0,112},{8,120},{16,0},{24,8},{32,16},{40,24},{48,32},{56,40},{64,... | collective-permute-start | bytes 786440 | tf_op jit(solution)/shard_map/ppermute | solution.py:540
  80.5 10.9 %collective-permute-start.6 = (bf16[64,2048]{1,0:T(8,128)(2,1)S(1)}, bf16[64,2048]{1,0:T(8,128)(2,1)S(1)}, u32[]{:S(2)}, u32[]{:S(2)}) collective-permute-start(bf16[64,2048]{1,0:T(8,128)(2,1)S(1)} %shard_map.141.refs_0_), channel_id=1, source_target_pairs={{0,16},{8,24},{16,32},{24,40},{32,48},{40,56},{48,64},{56,72},{64,... | collective-permute-start | bytes 786440 | tf_op jit(solution)/shard_map/ppermute | solution.py:538
  85.8 10.0 %collective-permute-start.8 = (bf16[64,2048]{1,0:T(8,128)(2,1)S(1)}, bf16[64,2048]{1,0:T(8,128)(2,1)S(1)}, u32[]{:S(2)}, u32[]{:S(2)}) collective-permute-start(bf16[64,2048]{1,0:T(8,128)(2,1)S(1)} %collective-permute-done.7.refs_2_), channel_id=1, source_target_pairs={{0,112},{8,120},{16,0},{24,8},{32,16},{40,24},{48,32},{56,40},{64,... | collective-permute-start | bytes 786440 | tf_op jit(solution)/shard_map/ppermute | solution.py:540
  91.5 9.8 %collective-permute-start.9 = (bf16[64,2048]{1,0:T(8,128)(2,1)S(1)}, bf16[64,2048]{1,0:T(8,128)(2,1)S(1)}, u32[]{:S(2)}, u32[]{:S(2)}) collective-permute-start(bf16[64,2048]{1,0:T(8,128)(2,1)S(1)} %collective-permute-done.6.refs_1_), channel_id=1, source_target_pairs={{0,16},{8,24},{16,32},{24,40},{32,48},{40,56},{48,64},{56,72},{64,... | collective-permute-start | bytes 786440 | tf_op jit(solution)/shard_map/ppermute | solution.py:538
  102.9 9.5 %collective-permute-start.10 = (bf16[64,2048]{1,0:T(8,128)(2,1)S(1)}, bf16[64,2048]{1,0:T(8,128)(2,1)S(1)}, u32[]{:S(2)}, u32[]{:S(2)}) collective-permute-start(bf16[64,2048]{1,0:T(8,128)(2,1)S(1)} %collective-permute-done.9.refs_1_), channel_id=1, source_target_pairs={{0,16},{8,24},{16,32},{24,40},{32,48},{40,56},{48,64},{56,72},{64,... | collective-permute-start | bytes 786440 | tf_op jit(solution)/shard_map/ppermute | solution.py:538
  104.8 11.7 %collective-permute-start.11 = (bf16[64,2048]{1,0:T(8,128)(2,1)S(1)}, bf16[64,2048]{1,0:T(8,128)(2,1)S(1)}, u32[]{:S(2)}, u32[]{:S(2)}) collective-permute-start(bf16[64,2048]{1,0:T(8,128)(2,1)S(1)} %collective-permute-done.8.refs_3_), channel_id=1, source_target_pairs={{0,112},{8,120},{16,0},{24,8},{32,16},{40,24},{48,32},{56,40},{64,... | collective-permute-start | bytes 786440 | tf_op jit(solution)/shard_map/ppermute | solution.py:540
  112.3 9.5 %collective-permute-start.12 = (bf16[64,2048]{1,0:T(8,128)(2,1)S(1)}, bf16[64,2048]{1,0:T(8,128)(2,1)S(1)}, u32[]{:S(2)}, u32[]{:S(2)}) collective-permute-start(bf16[64,2048]{1,0:T(8,128)(2,1)S(1)} %collective-permute-done.10.refs_0_), channel_id=1, source_target_pairs={{0,16},{8,24},{16,32},{24,40},{32,48},{40,56},{48,64},{56,72},{64,... | collective-permute-start | bytes 786440 | tf_op jit(solution)/shard_map/ppermute | solution.py:538
  138.9 0.9 copy-start
Sparse Core Ops, SparseCore 0:
  9.4 45.4 all-gather.2
  59.5 22.8 all-gather.4
  103.0 26.7 reduce-scatter.1
